TPU v7x, 256 devices: a whole 4x4x8 slice. The times are simulated.
256 devices in a mesh: row: 64 (over z, y, x_lo), col: 4 (over x_hi, core).
Axes of the slice: x: 4 (x_hi: 2, x_lo: 2; x = x_hi * 2 + x_lo), y: 4, z: 8, core: 2. Of those that a mesh axis runs over, the one named last changes fastest.
Arguments:
- moments: float32 [1536, 2, 16, 1536], P('row', None, None, 'col'), may hold values from 0.1 to 2.5
Outputs:
- first_y: float32 [1536, 2, 16, 1536], P('row', None, None, 'col')
- second_y: float32 [1536, 2, 16, 1536], P('row', None, None, 'col')
- first_z: float32 [1536, 2, 16, 1536], P('row', None, None, 'col')
- second_z: float32 [1536, 2, 16, 1536], P('row', None, None, 'col')
All inputs are finite; a program needn't handle non-finite values.
Results may differ from a plain program's by a relative error of at most 0.00013.
Values sent between devices are 32-bit elements; how exact they have to be, the bound alone decides.
No kernel may reach another device: no remote copies, remote signals or barrier semaphores. Data moves between devices by JAX's collectives and lax.ppermute only.
A program may use at most 128 MiB of HBM per device.

v0:
```python
import math

import jax
import jax.numpy as jnp
from jax import lax
from jax.sharding import PartitionSpec as P


def exact_sum(form, left, right):
    return jnp.einsum(
        form, left, right, precision=lax.Precision.HIGHEST, preferred_element_type=jnp.float32
    )


def trig_tables(first_count, second_count, period):
    first_idx = jnp.arange(first_count, dtype=jnp.int32)
    second_idx = jnp.arange(second_count, dtype=jnp.int32)
    product = jnp.remainder(first_idx[:, None] * second_idx[None, :], period)
    angle = product.astype(jnp.float32) * (2.0 * math.pi / period)
    return (jnp.cos(angle), jnp.sin(angle))


def factor_pair(length):
    small = 1
    for cand in range(1, length + 1):
        if cand * cand > length:
            break
        if length % cand == 0:
            small = cand
    return (small, length // small)


def line_pair(lines):
    length = lines.shape[0]
    width = lines.shape[1]
    pfac, qfac = factor_pair(length)
    cos_q, sin_q = trig_tables(qfac, qfac, qfac)
    cos_p, sin_p = trig_tables(pfac, pfac, pfac)
    cos_t, sin_t = trig_tables(qfac, pfac, length)
    cos_t = cos_t[:, :, None]
    sin_t = sin_t[:, :, None]
    cube = lines.reshape(qfac, pfac, width)
    section_re = exact_sum("ab,bck->ack", cos_q, cube)
    section_im = -exact_sum("ab,bck->ack", sin_q, cube)
    twist_re = section_re * cos_t + section_im * sin_t
    twist_im = section_im * cos_t - section_re * sin_t
    spec_re = exact_sum("ab,cbk->ack", cos_p, twist_re) + exact_sum("ab,cbk->ack", sin_p, twist_im)
    spec_im = exact_sum("ab,cbk->ack", cos_p, twist_im) - exact_sum("ab,cbk->ack", sin_p, twist_re)
    mode_k = (
        qfac * jnp.arange(pfac, dtype=jnp.int32)[:, None]
        + jnp.arange(qfac, dtype=jnp.int32)[None, :]
    )
    signed_k = jnp.where(mode_k > length // 2, mode_k - length, mode_k)
    wave = signed_k.astype(jnp.float32) * (2.0 * math.pi / length)
    wave_first = jnp.where(mode_k == length // 2, 0.0, wave)[:, :, None]
    wave_square = (wave * wave)[:, :, None]

    def inverse(value_re, value_im):
        back_re = exact_sum("ab,bck->ack", cos_p, value_re) - exact_sum(
            "ab,bck->ack", sin_p, value_im
        )
        back_im = exact_sum("ab,bck->ack", cos_p, value_im) + exact_sum(
            "ab,bck->ack", sin_p, value_re
        )
        cos_back = jnp.transpose(cos_t, (1, 0, 2))
        sin_back = jnp.transpose(sin_t, (1, 0, 2))
        turn_re = back_re * cos_back - back_im * sin_back
        turn_im = back_im * cos_back + back_re * sin_back
        result = exact_sum("ab,cbk->ack", cos_q, turn_re) - exact_sum("ab,cbk->ack", sin_q, turn_im)
        return (result * (1.0 / length)).reshape(length, width)

    first_out = inverse(-wave_first * spec_im, wave_first * spec_re)
    second_out = inverse(-wave_square * spec_re, -wave_square * spec_im)
    return (first_out, second_out)


def shards(moments):
    grid_shape = moments.shape
    y_count = grid_shape[0]
    z_count = grid_shape[3]
    lines_y = moments.reshape(y_count, -1)
    pencil = lax.all_to_all(lines_y, "row", split_axis=1, concat_axis=0, tiled=True)
    first_pen, second_pen = line_pair(pencil)
    first_y, second_y = (
        lax.all_to_all(first_pen, "row", split_axis=0, concat_axis=1, tiled=True),
        lax.all_to_all(second_pen, "row", split_axis=0, concat_axis=1, tiled=True),
    )
    lines_z = moments.reshape(-1, z_count)
    pencil_z = lax.all_to_all(lines_z, "col", split_axis=0, concat_axis=1, tiled=True)
    first_line, second_line = line_pair(pencil_z.T)
    first_z, second_z = (
        lax.all_to_all(first_line.T, "col", split_axis=1, concat_axis=0, tiled=True),
        lax.all_to_all(second_line.T, "col", split_axis=1, concat_axis=0, tiled=True),
    )
    return (
        first_y.reshape(grid_shape),
        second_y.reshape(grid_shape),
        first_z.reshape(grid_shape),
        second_z.reshape(grid_shape),
    )


def solution(mesh):
    placed = (P("row", None, None, "col"),)
    return jax.shard_map(
        shards,
        mesh=mesh,
        in_specs=placed,
        out_specs=(
            P("row", None, None, "col"),
            P("row", None, None, "col"),
            P("row", None, None, "col"),
            P("row", None, None, "col"),
        ),
        check_vma=False,
    )
```

profile of v0, /device:TPU:4, one launch (start us, length us, event | category | flops | bytes accessed | tf_op | source)
XLA Modules:
  0.0 278.7 jit_solution(949315619033058820)
XLA Ops:
  0.6 5.8 %all-to-all-start.3 = ((f32[4,192,384]{2,1,0:T(8,128)}), f32[4,192,384]{2,1,0:T(8,128)S(1)}, u32[]{:S(2)}, u32[]{:S(2)}) async-start(f32[4,192,384]{2,1,0:T(8,128)} %bitcast.129), calls=%async_computation.3 | async-start | bytes 2359296 | tf_op jit(solution)/shard_map/all_to_all | solution.py:89
  6.4 1.6 all_to_all.74
  8.0 2.0 copy.82
  10.1 10.5 %all-to-all-done.3 = f32[4,192,384]{2,1,0:T(8,128)S(1)} async-done(((f32[4,192,384]{2,1,0:T(8,128)}), f32[4,192,384]{2,1,0:T(8,128)S(1)}, u32[]{:S(2)}, u32[]{:S(2)}) %all-to-all-start.3) | async-done | bytes 1179680 | tf_op jit(solution)/shard_map/all_to_all | solution.py:89
  20.6 12.1 %all-to-all-start = ((f32[24,64,192]{2,0,1:T(8,128)}), f32[24,64,192]{2,0,1:T(8,128)S(1)}, u32[]{:S(2)}, u32[]{:S(2)}) async-start(f32[24,64,192]{2,0,1:T(8,128)} %copy.82), calls=%async_computation | async-start | bytes 3145728 | tf_op jit(solution)/shard_map/all_to_all | solution.py:82
  32.9 1.2 copy.119
  34.1 1.7 copy.98
  35.8 3.6 %fusion.30 = f32[48,32,192]{2,0,1:T(8,128)} fusion(f32[48,32,192]{2,1,0:T(8,128)S(1)} %bitcast.122), kind=kOutput, calls=%fused_computation.52 | convolution fusion | flops 169890048 | bytes 2359296 | tf_op jit(solution)/shard_map/ab,bck->ack/dot_general | solution.py:10
  39.4 33.4 %all-to-all-done = f32[24,64,192]{2,0,1:T(8,128)S(1)} async-done(((f32[24,64,192]{2,0,1:T(8,128)}), f32[24,64,192]{2,0,1:T(8,128)S(1)}, u32[]{:S(2)}, u32[]{:S(2)}) %all-to-all-start) | async-done | bytes 1179680 | tf_op jit(solution)/shard_map/all_to_all | solution.py:82
  72.8 2.4 convolution_negate_fusion.1
  75.2 2.4 fusion.39
  77.6 3.0 %multiply_add_fusion.2 = (f32[48,32,192]{2,0,1:T(8,128)S(1)}, f32[48,32,192]{2,0,1:T(8,128)S(1)}, f32[48,32,192]{2,0,1:T(8,128)S(1)}, f32[48,32,192]{2,0,1:T(8,128)S(1)}) fusion(f32[48,32,192]{2,0,1:T(8,128)S(1)} %copy-done.2, f32[48,32]{0,1:T(8,128)S(1)} %get-tuple-element.27, f32[48,32]{0,1:T(8,128)S(1)} %get-tuple-element.28, ...), kind=kOutput, calls=%fused_computation.22 | convolution fusion | flops 173723904 | bytes 9449472 | tf_op jit(solution)/shard_map/ab,bck->ack/dot_general | solution.py:10
  80.6 2.5 fusion.37
  83.2 2.3 fusion.33
  85.5 2.3 convolution_add_fusion.5
  87.8 2.3 fusion.24
  90.1 2.3 fusion.28
  92.5 2.8 %convolution_add_fusion.2 = f32[32,48,192]{2,0,1:T(8,128)S(1)} fusion(f32[32,48,192]{2,0,1:T(8,128)S(1)} %fusion.24, f32[48,32,192]{2,0,1:T(8,128)S(1)} %get-tuple-element.13), kind=kOutput, calls=%fused_computation.36 | convolution fusion | flops 113555456 | bytes 3538944 | tf_op jit(solution)/shard_map/ab,cbk->ack/dot_general | solution.py:10
  95.3 1.5 fusion.58
  96.8 1.5 fusion.46
  98.2 1.5 fusion.60
  99.7 1.5 fusion.48
  101.2 2.4 convolution_subtract_fusion.5
  103.6 1.5 fusion.54
  105.1 2.5 convolution_subtract_fusion.2
  107.6 1.5 fusion.64
  109.1 1.5 fusion.52
  110.6 1.5 fusion.42
  112.1 1.5 convolution_add_fusion.3
  113.6 1.5 convolution_subtract_fusion.3
  115.1 1.5 convolution_subtract_fusion
  116.7 1.5 convolution_add_fusion.4
  118.2 1.7 convolution_subtract_fusion.4
  120.0 1.5 convolution_add_fusion.1
  121.6 1.5 convolution_subtract_fusion.1
  123.1 4.7 %multiply_subtract_fusion = (f32[32,48,192]{2,0,1:T(8,128)S(1)}, f32[32,48,192]{2,0,1:T(8,128)S(1)}, f32[32,48,192]{2,0,1:T(8,128)}, f32[32,48,192]{2,0,1:T(8,12...) fusion(f32[32,48,192]{2,0,1:T(8,128)S(1)} %convolution_subtract, ...), kind=kOutput, calls=%fused_computation.18 | convolution fusion | flops 120928256 | bytes 20072448 | tf_op jit(solution)/shard_map/ab,bck->ack/dot_general | solution.py:10
  127.8 2.4 fusion
  130.2 2.4 subtract_multiply_fusion
  132.6 2.1 copy.112
  134.7 2.9 %copy.114 = f32[192,4,384]{2,0,1:T(8,128)} copy(f32[192,4,384]{0,2,1:T(8,128)} %bitcast.126) | data formatting | bytes 2359296 | tf_op jit(solution)/shard_map/all_to_all | solution.py:93
  137.6 7.0 %all-to-all-start.5 = ((f32[192,4,384]{2,0,1:T(8,128)}), f32[192,4,384]{2,0,1:T(8,128)}, u32[]{:S(2)}, u32[]{:S(2)}) async-start(f32[192,4,384]{2,0,1:T(8,128)} %copy.114), calls=%async_computation.5 | async-start | bytes 2359296 | tf_op jit(solution)/shard_map/all_to_all | solution.py:93
  144.6 3.9 %fusion.4 = f32[48,32,192]{2,0,1:T(8,128)S(1)} fusion(f32[32,48,192]{2,0,1:T(8,128)} %get-tuple-element.18), kind=kOutput, calls=%fused_computation.4 | convolution fusion | flops 169890048 | bytes 2359296 | tf_op jit(solution)/shard_map/ab,cbk->ack/dot_general | solution.py:10
  148.4 2.4 subtract_multiply_fusion.1
  150.8 2.1 copy.107
  152.9 2.9 %copy.109 = f32[192,4,384]{2,0,1:T(8,128)} copy(f32[192,4,384]{0,2,1:T(8,128)} %bitcast.127) | data formatting | bytes 2359296 | tf_op jit(solution)/shard_map/all_to_all | solution.py:92
  155.8 3.0 %all-to-all-done.5 = f32[192,4,384]{2,0,1:T(8,128)} async-done(((f32[192,4,384]{2,0,1:T(8,128)}), f32[192,4,384]{2,0,1:T(8,128)}, u32[]{:S(2)}, u32[]{:S(2)}) %all-to-all-start.5) | async-done | bytes 1179680 | tf_op jit(solution)/shard_map/all_to_all | solution.py:93
  158.8 7.4 %all-to-all-start.4 = ((f32[192,4,384]{2,0,1:T(8,128)}), f32[192,4,384]{2,0,1:T(8,128)}, u32[]{:S(2)}, u32[]{:S(2)}) async-start(f32[192,4,384]{2,0,1:T(8,128)} %copy.109), calls=%async_computation.4 | async-start | bytes 2359296 | tf_op jit(solution)/shard_map/all_to_all | solution.py:92
  166.2 3.9 %fusion.8 = f32[48,32,192]{2,0,1:T(8,128)S(1)} fusion(f32[32,48,192]{2,0,1:T(8,128)} %get-tuple-element.16), kind=kOutput, calls=%fused_computation.8 | convolution fusion | flops 169890048 | bytes 2359296 | tf_op jit(solution)/shard_map/ab,cbk->ack/dot_general | solution.py:10
  170.1 2.4 subtract_multiply_fusion.2
  172.5 2.1 copy.95
  174.6 5.9 %all-to-all-done.4 = f32[192,4,384]{2,0,1:T(8,128)} async-done(((f32[192,4,384]{2,0,1:T(8,128)}), f32[192,4,384]{2,0,1:T(8,128)}, u32[]{:S(2)}, u32[]{:S(2)}) %all-to-all-start.4) | async-done | bytes 1179680 | tf_op jit(solution)/shard_map/all_to_all | solution.py:92
  180.5 6.3 %all-to-all-start.2 = ((f32[64,24,192]{2,1,0:T(8,128)}), f32[64,24,192]{2,1,0:T(8,128)}, u32[]{:S(2)}, u32[]{:S(2)}) async-start(f32[64,24,192]{2,1,0:T(8,128)} %bitcast.124), calls=%async_computation.2 | async-start | bytes 3145728 | tf_op jit(solution)/shard_map/all_to_all | solution.py:86
  186.9 2.4 fusion.12
  189.3 2.4 subtract_multiply_fusion.3
  191.7 2.0 copy.91
  193.7 33.3 %all-to-all-done.2 = f32[64,24,192]{2,1,0:T(8,128)} async-done(((f32[64,24,192]{2,1,0:T(8,128)}), f32[64,24,192]{2,1,0:T(8,128)}, u32[]{:S(2)}, u32[]{:S(2)}) %all-to-all-start.2) | async-done | bytes 1179680 | tf_op jit(solution)/shard_map/all_to_all | solution.py:86
  227.1 5.7 %all-to-all-start.1 = ((f32[64,24,192]{2,1,0:T(8,128)}), f32[64,24,192]{2,1,0:T(8,128)S(1)}, u32[]{:S(2)}, u32[]{:S(2)}) async-start(f32[64,24,192]{2,1,0:T(8,128)} %bitcast.11), calls=%async_computation.1 | async-start | bytes 3145728 | tf_op jit(solution)/shard_map/all_to_all | solution.py:85
  232.8 1.9 copy.96
  234.7 1.4 reshape.195
  236.1 35.8 %all-to-all-done.1 = f32[64,24,192]{2,1,0:T(8,128)S(1)} async-done(((f32[64,24,192]{2,1,0:T(8,128)}), f32[64,24,192]{2,1,0:T(8,128)S(1)}, u32[]{:S(2)}, u32[]{:S(2)}) %all-to-all-start.1) | async-done | bytes 1179680 | tf_op jit(solution)/shard_map/all_to_all | solution.py:85
  271.9 0.5 copy.92
  272.4 1.4 reshape.194
  273.8 2.4 copy.172
  276.1 2.4 copy.173
  (10 shorter events, 0.2 us)
Async XLA Ops:
  0.6 20.0 %all-to-all-start.3 = ((f32[4,192,384]{2,1,0:T(8,128)}), f32[4,192,384]{2,1,0:T(8,128)S(1)}, u32[]{:S(2)}, u32[]{:S(2)}) async-start(f32[4,192,384]{2,1,0:T(8,128)} %bitcast.129), calls=%async_computation.3 | async-start | bytes 2359296 | tf_op jit(solution)/shard_map/all_to_all | solution.py:89
  20.6 52.2 %all-to-all-start = ((f32[24,64,192]{2,0,1:T(8,128)}), f32[24,64,192]{2,0,1:T(8,128)S(1)}, u32[]{:S(2)}, u32[]{:S(2)}) async-start(f32[24,64,192]{2,0,1:T(8,128)} %copy.82), calls=%async_computation | async-start | bytes 3145728 | tf_op jit(solution)/shard_map/all_to_all | solution.py:82
  75.2 2.4 copy-start.2
  137.6 21.2 %all-to-all-start.5 = ((f32[192,4,384]{2,0,1:T(8,128)}), f32[192,4,384]{2,0,1:T(8,128)}, u32[]{:S(2)}, u32[]{:S(2)}) async-start(f32[192,4,384]{2,0,1:T(8,128)} %copy.114), calls=%async_computation.5 | async-start | bytes 2359296 | tf_op jit(solution)/shard_map/all_to_all | solution.py:93
  144.5 3.9 %copy-start.1 = (f32[32,48,192]{2,0,1:T(8,128)S(1)}, f32[32,48,192]{2,0,1:T(8,128)}, u32[]{:S(2)}) copy-start(f32[32,48,192]{2,0,1:T(8,128)} %get-tuple-element.19) | copy-start | bytes 3538948
  158.8 21.7 %all-to-all-start.4 = ((f32[192,4,384]{2,0,1:T(8,128)}), f32[192,4,384]{2,0,1:T(8,128)}, u32[]{:S(2)}, u32[]{:S(2)}) async-start(f32[192,4,384]{2,0,1:T(8,128)} %copy.109), calls=%async_computation.4 | async-start | bytes 2359296 | tf_op jit(solution)/shard_map/all_to_all | solution.py:92
  166.2 3.9 %copy-start = (f32[32,48,192]{2,0,1:T(8,128)S(1)}, f32[32,48,192]{2,0,1:T(8,128)}, u32[]{:S(2)}) copy-start(f32[32,48,192]{2,0,1:T(8,128)} %get-tuple-element.17) | copy-start | bytes 3538948
  180.5 46.5 %all-to-all-start.2 = ((f32[64,24,192]{2,1,0:T(8,128)}), f32[64,24,192]{2,1,0:T(8,128)}, u32[]{:S(2)}, u32[]{:S(2)}) async-start(f32[64,24,192]{2,1,0:T(8,128)} %bitcast.124), calls=%async_computation.2 | async-start | bytes 3145728 | tf_op jit(solution)/shard_map/all_to_all | solution.py:86
  227.1 44.8 %all-to-all-start.1 = ((f32[64,24,192]{2,1,0:T(8,128)}), f32[64,24,192]{2,1,0:T(8,128)S(1)}, u32[]{:S(2)}, u32[]{:S(2)}) async-start(f32[64,24,192]{2,1,0:T(8,128)} %bitcast.11), calls=%async_computation.1 | async-start | bytes 3145728 | tf_op jit(solution)/shard_map/all_to_all | solution.py:85
where the time goes:
time: 283 us; the launch traced here: 279 us
  waiting for transfers between devices  122 us (43%)
  matrix products  80.5 us (28%)
  starting transfers between devices  44.3 us (16%)
  local copies, waits for them, and re-layouts  30.5 us (11%)
    dot_general x36, matrix products, exact_sum(): jnp.einsum(form, left, right, precision=lax.Precision.HIGHEST, preferred_...  80.5 us
    all_to_all x1, waiting for transfers between devices, shards(): lax.all_to_all(first_pen, 'row', split_axis=0, concat_axis=1, tiled=True)  35.8 us
    all_to_all x1, waiting for transfers between devices, shards(): lax.all_to_all(lines_y, 'row', split_axis=1, concat_axis=0, tiled=True)  33.4 us
    all_to_all x1, waiting for transfers between devices, shards(): lax.all_to_all(second_pen, 'row', split_axis=0, concat_axis=1, tiled=True)  33.3 us
    all_to_all x1, starting transfers between devices, shards(): lax.all_to_all(lines_y, 'row', split_axis=1, concat_axis=0, tiled=True)  12.1 us
    all_to_all x1, waiting for transfers between devices, shards(): lax.all_to_all(lines_z, 'col', split_axis=0, concat_axis=1, tiled=True)  10.5 us
    mul x4, local copies, waits for them, and re-layouts, inverse(): return (result * (1.0 / length)).reshape(length, width)  8.26 us
    all_to_all x1, starting transfers between devices, shards(): lax.all_to_all(first_line.T, 'col', split_axis=1, concat_axis=0, tiled=True)  7.42 us
  transfers between devices with their start and end apart: 6, of which 6 were waited for; matrix products, arithmetic and copies ran while one was open for 14% of the time, Pallas kernels for 0%

commit v1 on v0

v1 whole, which is shorter than its diff:
```python
import math

import jax
import jax.numpy as jnp
import ml_dtypes
import numpy as np
from jax import lax
from jax.experimental import pallas as pl
from jax.experimental.pallas import tpu as pltpu
from jax.sharding import Mesh
from jax.sharding import PartitionSpec as P

COUNT = 1536
HALF = COUNT // 2
QUARTER = COUNT // 4
ROWS = 24
LANES = 384
PLANES = 32
F32 = jnp.float32
BF16 = jnp.bfloat16


def kernels():
    k = np.arange(COUNT, dtype=np.float64)
    sign = np.where(np.arange(COUNT) % 2 == 0, 1.0, -1.0)
    angle = math.pi * np.where(k == 0, 1.0, k) / COUNT
    first = np.where(k == 0, 0.0, math.pi / COUNT * sign / np.tan(angle))
    second = np.where(
        k == 0,
        -math.pi**2 / 3 - (2 * math.pi / COUNT) ** 2 / 6,
        -sign * (2 * math.pi**2 / COUNT**2) / np.sin(angle) ** 2,
    )
    return first, second


def halves(table):
    high = table.astype(ml_dtypes.bfloat16)
    low = (table - high.astype(np.float64)).astype(ml_dtypes.bfloat16)
    return np.stack([high, low])


def tables():
    def folded(size, value):
        gap = np.arange(size)[:, None] - np.arange(size)[None, :]
        return halves(np.concatenate([value(d, gap) for d in kernels()]))

    def plus(d, gap):
        return (d[gap % COUNT] + d[(gap + HALF) % COUNT]) / 2

    parts = []
    for sign in (1, -1):
        high, low = folded(
            QUARTER, lambda d, gap: (plus(d, gap) + sign * plus(d, gap + QUARTER)) / 2
        )
        parts.append(np.concatenate([high, low], axis=1))
    parts.extend(folded(HALF, lambda d, gap: (d[gap % COUNT] - d[(gap + HALF) % COUNT]) / 2))
    cell = np.arange(LANES)
    blocks = [
        np.concatenate(
            [d[(cell[None, :] - cell[:, None] - LANES * r) % COUNT] for d in kernels()], axis=1
        )
        for r in range(4)
    ]
    parts.extend(halves(np.concatenate(blocks)))
    return np.concatenate(parts)


def split(value):
    high = value.astype(BF16)
    return high, (value - high.astype(F32)).astype(BF16)


def three(left_high, left_low, right_high, right_low):
    total = jnp.dot(left_high, right_high, preferred_element_type=F32)
    total = total + jnp.dot(left_high, right_low, preferred_element_type=F32)
    return total + jnp.dot(left_low, right_high, preferred_element_type=F32)


def low_lanes(shape):
    return lax.broadcasted_iota(jnp.int32, shape, len(shape) - 1) < 64


def pack_kernel(x_hbm, msg_hbm, x_ref, msg_ref, in_sems, out_sems):
    gets = [
        pltpu.make_async_copy(x_hbm.at[:, 8 * g : 8 * g + 8], x_ref.at[g], in_sems.at[g])
        for g in range(4)
    ]
    puts = [
        pltpu.make_async_copy(msg_ref.at[g], msg_hbm.at[576 * g : 576 * g + 576], out_sems.at[g])
        for g in range(4)
    ]
    near = low_lanes((8, 128))
    for get in gets:
        get.start()
    for g in range(4):
        gets[g].wait()
        for i in range(ROWS):
            for low in range(2):
                at = pl.ds(36 * low + i, 8, stride=72)
                msg_ref[g, at, :] = x_ref[g, i, :, 128 * low : 128 * low + 128]
        for i in range(12):
            top, bottom = x_ref[g, i, :, 256:384], x_ref[g, i + 12, :, 256:384]
            lower = jnp.where(near, top, pltpu.roll(bottom, 64, 1))
            upper = jnp.where(near, pltpu.roll(top, 64, 1), bottom)
            msg_ref[g, pl.ds(24 + i, 8, stride=72), :] = lower
            msg_ref[g, pl.ds(60 + i, 8, stride=72), :] = upper
        puts[g].start()
    for put in puts:
        put.wait()


def pack(block):
    return pl.pallas_call(
        pack_kernel,
        in_specs=[pl.BlockSpec(memory_space=pltpu.HBM)],
        out_specs=pl.BlockSpec(memory_space=pltpu.HBM),
        out_shape=jax.ShapeDtypeStruct((2304, 128), F32),
        scratch_shapes=[
            pltpu.VMEM((4, ROWS, 8, LANES), F32),
            pltpu.VMEM((4, 576, 128), F32),
            pltpu.SemaphoreType.DMA((4,)),
            pltpu.SemaphoreType.DMA((4,)),
        ],
        compiler_params=pltpu.CompilerParams(vmem_limit_bytes=56 * 2**20),
    )(block)


def unpack_kernel(msg_ref, first_ref, second_ref):
    near = low_lanes((8, 128))
    for out_ref, full, part in ((first_ref, 0, 24), (second_ref, 48, 36)):
        for i in range(ROWS):
            for low in range(2):
                at = pl.ds(72 * low + full + i, 8, stride=144)
                out_ref[i, :, 128 * low : 128 * low + 128] = msg_ref[at, :]
        for i in range(12):
            lower = msg_ref[pl.ds(part + i, 8, stride=144), :]
            upper = msg_ref[pl.ds(72 + part + i, 8, stride=144), :]
            out_ref[i, :, 256:384] = jnp.where(near, lower, pltpu.roll(upper, 64, 1))
            out_ref[i + 12, :, 256:384] = jnp.where(near, pltpu.roll(lower, 64, 1), upper)


def unpack(message):
    out = jax.ShapeDtypeStruct((ROWS, PLANES, LANES), F32)
    return pl.pallas_call(
        unpack_kernel,
        grid=(4,),
        in_specs=[pl.BlockSpec((1152, 128), lambda i: (i, 0))],
        out_specs=[pl.BlockSpec((ROWS, 8, LANES), lambda i: (0, i, 0))] * 2,
        out_shape=(out, out),
        compiler_params=pltpu.CompilerParams(vmem_limit_bytes=16 * 2**20),
    )(message)


def cross_kernel(
    table_hbm, msg, out_hbm, small, large, out, line, got_small, got_large, table_sems, out_sems
):
    loads = [
        pltpu.make_async_copy(table_hbm.at[0:768], small.at[0], table_sems.at[0]),
        pltpu.make_async_copy(table_hbm.at[768:1536], small.at[1], table_sems.at[1]),
        pltpu.make_async_copy(table_hbm.at[1536:3072], large.at[0], table_sems.at[2]),
        pltpu.make_async_copy(table_hbm.at[3072:4608], large.at[1], table_sems.at[3]),
    ]
    puts = [pltpu.make_async_copy(out.at[z], out_hbm.at[z], out_sems.at[z]) for z in range(8)]
    for load in loads:
        load.start()

    for c in range(4):
        for y in range(4):
            at = 48 * (4 * c + y)
            top, bottom = msg[0, c, y], msg[1, c, y]
            for k, value in enumerate((top + bottom, top - bottom)):
                line[k, at : at + 24, 0:128] = value[0:24]
                line[k, at + 24 : at + 48, 0:128] = value[36:60]
                even, odd = value[24:36], value[60:72]
                parts = [even, pltpu.roll(even, 64, 1), odd, pltpu.roll(odd, 64, 1)]
                line[k, at : at + 48, 128:256] = jnp.concatenate(parts, axis=0)

    head, tail = line[0, :QUARTER, :], line[0, QUARTER:, :]
    for k, value in enumerate((head + tail, head - tail)):
        high, low = split(value)
        loads[k].wait()
        got_small[k] = three(small[k, :, :QUARTER], small[k, :, QUARTER:], high, low)
    high, low = split(line[1])
    loads[2].wait()
    total = jnp.dot(large[0], high, preferred_element_type=F32)
    total = total + jnp.dot(large[0], low, preferred_element_type=F32)
    loads[3].wait()
    got_large[...] = total + jnp.dot(large[1], high, preferred_element_type=F32)

    near = low_lanes((12, 128))
    for c in range(4):
        for y in range(4):
            for low in range(2):
                at = 48 * (4 * c + y) + ROWS * low
                for d, (full, part) in enumerate(((0, 24), (48, 36))):
                    minus = got_large[HALF * d + at : HALF * d + at + ROWS, :]
                    place = QUARTER * d + at % QUARTER
                    one = got_small[0, place : place + ROWS, :]
                    two = got_small[1, place : place + ROWS, :]
                    plus = one + two if at < QUARTER else one - two
                    for z, value in ((c, plus + minus), (c + 4, plus - minus)):
                        out[z, y, low, full : full + 24] = value[:, 0:128]
                        top, bottom = value[:12, 128:256], value[12:, 128:256]
                        out[z, y, low, part : part + 12] = jnp.where(
                            near, top, pltpu.roll(bottom, 64, 1)
                        )
        puts[c].start()
        puts[c + 4].start()
    for put in puts:
        put.wait()


def cross(table, message):
    return pl.pallas_call(
        cross_kernel,
        out_shape=jax.ShapeDtypeStruct((8, 4, 2, 72, 128), F32),
        in_specs=[pl.BlockSpec(memory_space=pltpu.HBM), pl.BlockSpec(memory_space=pltpu.VMEM)],
        out_specs=pl.BlockSpec(memory_space=pltpu.HBM),
        scratch_shapes=[
            pltpu.VMEM((2, HALF, HALF), BF16),
            pltpu.VMEM((2, COUNT, HALF), BF16),
            pltpu.VMEM((8, 4, 2, 72, 128), F32),
            pltpu.VMEM((2, HALF, 256), F32),
            pltpu.VMEM((2, HALF, 256), F32),
            pltpu.VMEM((COUNT, 256), F32),
            pltpu.SemaphoreType.DMA((4,)),
            pltpu.SemaphoreType.DMA((8,)),
        ],
        compiler_params=pltpu.CompilerParams(vmem_limit_bytes=50 * 2**20),
        cost_estimate=pl.CostEstimate(
            flops=3 * 2 * 3 * HALF * HALF * 256, bytes_accessed=12 * 2**20, transcendentals=0
        ),
    )(table, message.reshape(2, 4, 4, 72, 128))


def along_kernel(
    core_ref,
    table_hbm,
    own,
    near,
    far_a,
    far_b,
    far_near_a,
    far_near_b,
    first_ref,
    second_ref,
    table_ref,
    sem,
):
    core = core_ref[0]

    @pl.when(pl.program_id(0) == 0)
    def _():
        load = pltpu.make_async_copy(table_hbm.at[4608:7680], table_ref, sem)
        load.start()
        load.wait()

    def block_of(h, r):
        return table_ref[pl.ds(pl.multiple_of(COUNT * h + LANES * r, LANES), LANES), :]

    early = pl.program_id(0) == 0
    far = jnp.where(early, far_a[...], far_b[...])
    far_near = jnp.where(early, far_near_a[...], far_near_b[...])
    total = jnp.zeros((256, 2 * LANES), F32)
    pairs = ((own[...], 0), (near[...], 1 + 2 * core), (far, 2), (far_near, 3 - 2 * core))
    for block, r in pairs:
        high, low = split(block)
        total = total + three(high, low, block_of(0, r), block_of(1, r))
    first_ref[...] = total[:, :LANES]
    second_ref[...] = total[:, LANES:]


def along(core, table, *blocks):
    out = jax.ShapeDtypeStruct((ROWS * PLANES, LANES), F32)
    lines = pl.BlockSpec((256, LANES), lambda i, core: (i, 0))
    early = pl.BlockSpec((256, LANES), lambda i, core: (0, 0))
    late = pl.BlockSpec((256, LANES), lambda i, core: (jnp.maximum(i, 1) - 1, 0))
    return pl.pallas_call(
        along_kernel,
        grid_spec=pltpu.PrefetchScalarGridSpec(
            num_scalar_prefetch=1,
            grid=(3,),
            in_specs=[pl.BlockSpec(memory_space=pltpu.HBM)]
            + [lines, lines, early, late, early, late],
            out_specs=[lines] * 2,
            scratch_shapes=[
                pltpu.VMEM((2 * COUNT, 2 * LANES), BF16),
                pltpu.SemaphoreType.DMA,
            ],
        ),
        out_shape=(out, out),
        compiler_params=pltpu.CompilerParams(vmem_limit_bytes=50 * 2**20),
        cost_estimate=pl.CostEstimate(
            flops=2 * 3 * 768 * COUNT * 768, bytes_accessed=16 * 2**20, transcendentals=0
        ),
    )(core, table, *blocks)


def solution(mesh):
    fine = Mesh(mesh.devices.reshape(8, 4, 2, 2, 2), ("z", "y", "xl", "xh", "c"))
    table_t = tables()
    pair = [(0, 1), (1, 0)]

    def swap(message):
        return lax.all_to_all(message, ("z", "y", "xl"), split_axis=0, concat_axis=0, tiled=True)

    def shards(moments):
        grid = moments.shape
        table = jnp.asarray(table_t)
        own = moments.reshape(ROWS * PLANES, LANES)
        far_a = lax.ppermute(own[:256], "xh", pair)
        near = lax.ppermute(own, "c", pair)
        home = swap(pack(moments.reshape(ROWS, PLANES, LANES)).reshape(64, 9, 4, 128))
        home, far_a, near = lax.optimization_barrier((home, far_a, near))
        far_b = lax.ppermute(own[256:], "xh", pair)
        back = swap(cross(table, home).reshape(64, 72, 128))
        far_near_a = lax.ppermute(far_a, "c", pair)
        far_near_b = lax.ppermute(far_b, "c", pair)
        core = lax.axis_index("c").reshape(1)
        first_z, second_z = along(
            core, table, own, near, far_a, far_b, far_near_a, far_near_b
        )
        first_z, second_z, back = lax.optimization_barrier((first_z, second_z, back))
        first, second = unpack(back.reshape(4608, 128))
        return (
            first.reshape(grid),
            second.reshape(grid),
            first_z.reshape(grid),
            second_z.reshape(grid),
        )

    spec = P(("z", "y", "xl"), None, None, ("xh", "c"))
    return jax.shard_map(
        shards, mesh=fine, in_specs=(spec,), out_specs=(spec,) * 4, check_vma=False
    )
```

time: 283 us -> 123 us (0.43); the launches traced: 279 us -> 123 us
  matrix products: 80.5 us -> 0 us
  waiting for transfers between devices: 122 us -> 72.3 us
  local copies, waits for them, and re-layouts: 30.5 us -> 3.79 us
  Pallas kernels: 0 us -> 24.7 us
  starting transfers between devices: 44.3 us -> 21.2 us
    all_to_all x6 -> x2, waiting for transfers between devices: 122 us -> 16.3 us  [swap(): lax.all_to_all(message, ('z', 'y', 'xl'), split_axis=0, concat_axis=0, ti...]
    dot_general x36 -> x0, matrix products: 80.5 us -> none  [exact_sum(): jnp.einsum(form, left, right, precision=lax.Precision.HIGHEST, preferred_...]
    ppermute x0 -> x5, waiting for transfers between devices: none -> 56 us  [the longest x1 34.3 us: shards(): far_b = lax.ppermute(own[256:], 'xh', pair)]
    all_to_all x6 -> x2, starting transfers between devices: 44.3 us -> 18.8 us  [swap(): lax.all_to_all(message, ('z', 'y', 'xl'), split_axis=0, concat_axis=0, ti...]
    pallas_call x0 -> x4, Pallas kernels: none -> 24.7 us  [the longest x1 12.5 us: along(): pl.pallas_call(along_kernel, grid_spec=pltpu.PrefetchScalarGridSpec(num_s...]
    all_to_all x7 -> x0, local copies, waits for them, and re-layouts: 13 us -> none  [the longest x2 3.67 us: shards(): lax.all_to_all(lines_y, 'row', split_axis=1, concat_axis=0, tiled=True)]
    mul x4 -> x0, local copies, waits for them, and re-layouts: 8.26 us -> none  [inverse(): return (result * (1.0 / length)).reshape(length, width)]
  transfers between devices with their start and end apart: 6 -> 7, of which waited for: 6 -> 6; matrix products, arithmetic and copies ran while one was open for 14% -> 0% of each run, Pallas kernels for 0% -> 10%
where the time goes in v1:
time: 123 us
  waiting for transfers between devices  72.3 us (59%)
  Pallas kernels  24.7 us (20%)
  starting transfers between devices  21.2 us (17%)
  local copies, waits for them, and re-layouts  3.79 us (3%)
    ppermute x1, waiting for transfers between devices, shards(): far_b = lax.ppermute(own[256:], 'xh', pair)  34.3 us
    ppermute x1, waiting for transfers between devices, shards(): far_a = lax.ppermute(own[:256], 'xh', pair)  19.1 us
    all_to_all x2, starting transfers between devices, swap(): lax.all_to_all(message, ('z', 'y', 'xl'), split_axis=0, concat_axis=0, ti...  18.8 us
    all_to_all x2, waiting for transfers between devices, swap(): lax.all_to_all(message, ('z', 'y', 'xl'), split_axis=0, concat_axis=0, ti...  16.3 us
    pallas_call x1, Pallas kernels, along(): pl.pallas_call(along_kernel, grid_spec=pltpu.PrefetchScalarGridSpec(num_s...  12.5 us
    pallas_call x1, Pallas kernels, cross(): pl.pallas_call(cross_kernel, out_shape=jax.ShapeDtypeStruct((8, 4, 2, 72,...  8 us
    unnamed x8, local copies, waits for them, and re-layouts  3.71 us
  transfers between devices with their start and end apart: 7, of which 6 were waited for; matrix products, arithmetic and copies ran while one was open for 0% of the time, Pallas kernels for 10%

profile of v1, /device:TPU:4, one launch (start us, length us, event | category | flops | bytes accessed | tf_op | source)
XLA Modules:
  0.0 122.8 jit_solution(7751630604464888165)
XLA Ops:
  0.6 2.1 %shard_map.57 = f32[2304,128]{1,0:T(8,128)} custom-call(f32[24,32,384]{2,1,0:T(8,128)} %bitcast.15), custom_call_target="tpu_custom_call" | custom-call | tf_op jit(solution)/shard_map/pallas_call | solution.py:113
  2.8 0.0 copy-start.1
  2.8 12.9 %all-to-all-start = ((f32[64,9,4,128]{3,2,1,0:T(4,128)}), f32[64,9,4,128]{3,2,1,0:T(4,128)S(1)}, u32[]{:S(2)}, u32[]{:S(2)}) async-start(f32[64,9,4,128]{3,2,1,0:T(4,128)} %bitcast.19), calls=%async_computation | async-start | bytes 2359296 | tf_op jit(solution)/shard_map/all_to_all | solution.py:305
  15.7 0.0 copy-done.1
  15.7 0.1 collective-permute-start.1
  15.8 0.9 collective-permute-start
  16.7 19.1 %collective-permute-done.far_a = f32[256,384]{1,0:T(8,128)} collective-permute-done((f32[256,384]{1,0:T(8,128)S(1)}, f32[256,384]{1,0:T(8,128)}, u32[]{:S(2)}, u32[]{:S(2)}) %collective-permute-start) | collective-permute-done | bytes 393248 | tf_op jit(solution)/shard_map/ppermute | solution.py:311
  35.8 0.0 collective-permute-done.1.near
  35.8 11.5 %all-to-all-done = f32[64,9,4,128]{3,2,1,0:T(4,128)S(1)} async-done(((f32[64,9,4,128]{3,2,1,0:T(4,128)}), f32[64,9,4,128]{3,2,1,0:T(4,128)S(1)}, u32[]{:S(2)}, u32[]{:S(2)}) %all-to-all-start) | async-done | bytes 1179680 | tf_op jit(solution)/shard_map/all_to_all | solution.py:305
  47.3 0.0 copy-start.2
  47.3 1.0 copy-done.2
  48.3 0.0 copy-start.3
  48.3 1.3 %copy-done.3 = f32[64,9,4,128]{3,2,1,0:T(4,128)S(1)} copy-done((f32[64,9,4,128]{3,2,1,0:T(4,128)S(1)}, f32[64,9,4,128]{3,2,1,0:T(4,128)}, u32[]{:S(2)}) %copy-start.3) | copy-done | bytes 1179672
  49.5 8.0 %shard_map.59 = f32[8,4,2,72,128]{4,3,2,1,0:T(8,128)S(1)} custom-call(bf16[7680,768]{1,0:T(8,128)(2,1)} %constant.6.clone.table_hbm, f32[2,4,4,72,128]{4,3,2,1,0:T(8,128)S(1)} %bitcast.18), custom_call_target="tpu_custom_call" | custom-call | flops 2717908992 | bytes 12582912 | tf_op jit(solution)/shard_map/pallas_call | solution.py:214
  57.6 0.0 copy-start
  57.6 1.4 %copy-done = f32[8,4,2,72,128]{4,3,2,1,0:T(8,128)} copy-done((f32[8,4,2,72,128]{4,3,2,1,0:T(8,128)}, f32[8,4,2,72,128]{4,3,2,1,0:T(8,128)S(1)}, u32[]{:S(2)}) %copy-start) | copy-done | bytes 2359320
  59.0 6.0 %all-to-all-start.1 = ((f32[64,72,128]{2,1,0:T(8,128)}), f32[64,72,128]{2,1,0:T(8,128)S(1)}, u32[]{:S(2)}, u32[]{:S(2)}) async-start(f32[64,72,128]{2,1,0:T(8,128)} %bitcast.14), calls=%async_computation.1 | async-start | bytes 4718592 | tf_op jit(solution)/shard_map/all_to_all | solution.py:305
  65.0 0.1 slice.14
  65.0 0.9 collective-permute-start.2
  65.9 34.3 %collective-permute-done.2.far_b = f32[512,384]{1,0:T(8,128)} collective-permute-done((f32[512,384]{1,0:T(8,128)S(1)}, f32[512,384]{1,0:T(8,128)}, u32[]{:S(2)}, u32[]{:S(2)}) %collective-permute-start.2) | collective-permute-done | bytes 786464 | tf_op jit(solution)/shard_map/ppermute | solution.py:315
  100.2 0.0 collective-permute-start.4
  100.2 0.5 collective-permute-start.3
  100.7 2.1 %collective-permute-done.4.far_near_b = f32[512,384]{1,0:T(8,128)} collective-permute-done((f32[512,384]{1,0:T(8,128)}, f32[512,384]{1,0:T(8,128)}, u32[]{:S(2)}, u32[]{:S(2)}) %collective-permute-start.4) | collective-permute-done | bytes 786464 | tf_op jit(solution)/shard_map/ppermute | solution.py:318
  102.8 0.6 collective-permute-done.3.far_near_a
  103.3 12.5 %shard_map.58 = (f32[768,384]{1,0:T(8,128)}, f32[768,384]{1,0:T(8,128)}) custom-call(s32[1]{0:T(128)} %bitcast.core_ref, bf16[7680,768]{1,0:T(8,128)(2,1)} %constant.6.clone.table_hbm, f32[768,384]{1,0:T(8,128)S(1)} %bitcast.17, f32[768,384]{1,0:T(8,128)} %collective-permute-done.1.near, f32[256,384]{1,0:T(8,128)} %collective-permute-done.far_a, ...), custom_call_target="tpu_custom_call" | custom-call | flops 5435817984 | bytes 16777216 | tf_op jit(solution)/shard_map/pallas_call | solution.py:278
  115.9 4.9 %all-to-all-done.1 = f32[64,72,128]{2,1,0:T(8,128)S(1)} async-done(((f32[64,72,128]{2,1,0:T(8,128)}), f32[64,72,128]{2,1,0:T(8,128)S(1)}, u32[]{:S(2)}, u32[]{:S(2)}) %all-to-all-start.1) | async-done | bytes 2359328 | tf_op jit(solution)/shard_map/all_to_all | solution.py:305
  120.7 2.0 %shard_map.60 = (f32[24,32,384]{2,1,0:T(8,128)}, f32[24,32,384]{2,1,0:T(8,128)}) custom-call(f32[4608,128]{1,0:T(8,128)S(1)} %bitcast.13), custom_call_target="tpu_custom_call" | custom-call | tf_op jit(solution)/shard_map/pallas_call | solution.py:144
  (1 shorter events, 0.0 us)
Async XLA Ops:
  2.8 12.9 %copy-start.1 = (f32[24,2,16,384]{3,2,1,0:T(8,128)S(1)}, f32[24,2,16,384]{3,2,1,0:T(8,128)}, u32[]{:S(2)}) copy-start(f32[24,2,16,384]{3,2,1,0:T(8,128)} %param.2) | copy-start | bytes 3538948
  2.8 44.5 %all-to-all-start = ((f32[64,9,4,128]{3,2,1,0:T(4,128)}), f32[64,9,4,128]{3,2,1,0:T(4,128)S(1)}, u32[]{:S(2)}, u32[]{:S(2)}) async-start(f32[64,9,4,128]{3,2,1,0:T(4,128)} %bitcast.19), calls=%async_computation | async-start | bytes 2359296 | tf_op jit(solution)/shard_map/all_to_all | solution.py:305
  15.7 20.1 %collective-permute-start.1 = (f32[768,384]{1,0:T(8,128)S(1)}, f32[768,384]{1,0:T(8,128)}, u32[]{:S(2)}, u32[]{:S(2)}) collective-permute-start(f32[768,384]{1,0:T(8,128)S(1)} %bitcast.16), channel_id=1, source_target_pairs={{0,1},{1,0},{2,3},{3,2},{4,5},{5,4},{6,7},{7,6},{8,9},{9,8},{10,11... | collective-permute-start | bytes 3538952 | tf_op jit(solution)/shard_map/ppermute | solution.py:312
  15.8 20.0 %collective-permute-start = (f32[256,384]{1,0:T(8,128)S(1)}, f32[256,384]{1,0:T(8,128)}, u32[]{:S(2)}, u32[]{:S(2)}) collective-permute-start(f32[256,384]{1,0:T(8,128)S(1)} %bitcast.21), channel_id=1, source_target_pairs={{0,2},{2,0},{1,3},{3,1},{4,6},{6,4},{5,7},{7,5},{8,10},{10,8},{9,1... | collective-permute-start | bytes 1179656 | tf_op jit(solution)/shard_map/ppermute | solution.py:311
  47.3 1.0 copy-start.2
  48.3 1.3 %copy-start.3 = (f32[64,9,4,128]{3,2,1,0:T(4,128)S(1)}, f32[64,9,4,128]{3,2,1,0:T(4,128)}, u32[]{:S(2)}) copy-start(f32[64,9,4,128]{3,2,1,0:T(4,128)} %copy-done.2) | copy-start | bytes 3538948
  57.6 1.4 %copy-start = (f32[8,4,2,72,128]{4,3,2,1,0:T(8,128)}, f32[8,4,2,72,128]{4,3,2,1,0:T(8,128)S(1)}, u32[]{:S(2)}) copy-start(f32[8,4,2,72,128]{4,3,2,1,0:T(8,128)S(1)} %shard_map.59) | copy-start | bytes 7077892
  59.0 61.7 %all-to-all-start.1 = ((f32[64,72,128]{2,1,0:T(8,128)}), f32[64,72,128]{2,1,0:T(8,128)S(1)}, u32[]{:S(2)}, u32[]{:S(2)}) async-start(f32[64,72,128]{2,1,0:T(8,128)} %bitcast.14), calls=%async_computation.1 | async-start | bytes 4718592 | tf_op jit(solution)/shard_map/all_to_all | solution.py:305
  65.0 35.1 %collective-permute-start.2 = (f32[512,384]{1,0:T(8,128)S(1)}, f32[512,384]{1,0:T(8,128)}, u32[]{:S(2)}, u32[]{:S(2)}) collective-permute-start(f32[512,384]{1,0:T(8,128)S(1)} %bitcast.20), channel_id=1, source_target_pairs={{0,2},{2,0},{1,3},{3,1},{4,6},{6,4},{5,7},{7,5},{8,10},{10,8},{9,1... | collective-permute-start | bytes 2359304 | tf_op jit(solution)/shard_map/ppermute | solution.py:315
  100.2 2.6 %collective-permute-start.4 = (f32[512,384]{1,0:T(8,128)}, f32[512,384]{1,0:T(8,128)}, u32[]{:S(2)}, u32[]{:S(2)}) collective-permute-start(f32[512,384]{1,0:T(8,128)} %collective-permute-done.2.far_b), channel_id=1, source_target_pairs={{0,1},{1,0},{2,3},{3,2},{4,5},{5,4},{6,7},{7,6},{8,9},{9,8},{10,11... | collective-permute-start | bytes 2359304 | tf_op jit(solution)/shard_map/ppermute | solution.py:318
  100.2 3.2 %collective-permute-start.3 = (f32[256,384]{1,0:T(8,128)}, f32[256,384]{1,0:T(8,128)}, u32[]{:S(2)}, u32[]{:S(2)}) collective-permute-start(f32[256,384]{1,0:T(8,128)} %collective-permute-done.far_a), channel_id=1, source_target_pairs={{0,1},{1,0},{2,3},{3,2},{4,5},{5,4},{6,7},{7,6},{8,9},{9,8},{10,11... | collective-permute-start | bytes 1179656 | tf_op jit(solution)/shard_map/ppermute | solution.py:317

commit v2 on v1

--- a/solution.py
+++ b/solution.py
@@ -39,21 +39,21 @@
     return np.stack([high, low])
 
 
-def tables():
-    def folded(size, value):
-        gap = np.arange(size)[:, None] - np.arange(size)[None, :]
-        return halves(np.concatenate([value(d, gap) for d in kernels()]))
+def cross_strips():
+    def strip(block, value):
+        gap = 2 * block + np.arange(block)[:, None] - np.arange(5 * block)[None, :]
+        return halves(np.stack([value(d, gap) for d in kernels()]))
 
     def plus(d, gap):
         return (d[gap % COUNT] + d[(gap + HALF) % COUNT]) / 2
 
-    parts = []
-    for sign in (1, -1):
-        high, low = folded(
-            QUARTER, lambda d, gap: (plus(d, gap) + sign * plus(d, gap + QUARTER)) / 2
-        )
-        parts.append(np.concatenate([high, low], axis=1))
-    parts.extend(folded(HALF, lambda d, gap: (d[gap % COUNT] - d[(gap + HALF) % COUNT]) / 2))
+    both = strip(128, lambda d, gap: (plus(d, gap) + plus(d, gap + QUARTER)) / 2)
+    cross = strip(128, lambda d, gap: (plus(d, gap) - plus(d, gap + QUARTER)) / 2)
+    minus = strip(256, lambda d, gap: (d[gap % COUNT] - d[(gap + HALF) % COUNT]) / 2)
+    return np.stack([both, cross]), minus
+
+
+def along_table():
     cell = np.arange(LANES)
     blocks = [
         np.concatenate(
@@ -61,8 +61,7 @@
         )
         for r in range(4)
     ]
-    parts.extend(halves(np.concatenate(blocks)))
-    return np.concatenate(parts)
+    return halves(np.stack(blocks))
 
 
 def split(value):
@@ -152,22 +151,39 @@
 
 
 def cross_kernel(
-    table_hbm, msg, out_hbm, small, large, out, line, got_small, got_large, table_sems, out_sems
+    small_hbm,
+    large_hbm,
+    msg_hbm,
+    out_hbm,
+    small_strip,
+    large_strip,
+    small,
+    large,
+    msg,
+    out,
+    line,
+    got_small,
+    got_large,
+    in_sems,
+    table_sems,
+    out_sems,
 ):
-    loads = [
-        pltpu.make_async_copy(table_hbm.at[0:768], small.at[0], table_sems.at[0]),
-        pltpu.make_async_copy(table_hbm.at[768:1536], small.at[1], table_sems.at[1]),
-        pltpu.make_async_copy(table_hbm.at[1536:3072], large.at[0], table_sems.at[2]),
-        pltpu.make_async_copy(table_hbm.at[3072:4608], large.at[1], table_sems.at[3]),
+    gets = [
+        pltpu.make_async_copy(msg_hbm.at[:, c], msg.at[c], in_sems.at[c]) for c in range(4)
+    ]
+    strips = [
+        pltpu.make_async_copy(small_hbm, small_strip, table_sems.at[0]),
+        pltpu.make_async_copy(large_hbm, large_strip, table_sems.at[1]),
     ]
     puts = [pltpu.make_async_copy(out.at[z], out_hbm.at[z], out_sems.at[z]) for z in range(8)]
-    for load in loads:
-        load.start()
+    for copy in gets + strips:
+        copy.start()
 
     for c in range(4):
+        gets[c].wait()
         for y in range(4):
             at = 48 * (4 * c + y)
-            top, bottom = msg[0, c, y], msg[1, c, y]
+            top, bottom = msg[c, 0, y], msg[c, 1, y]
             for k, value in enumerate((top + bottom, top - bottom)):
                 line[k, at : at + 24, 0:128] = value[0:24]
                 line[k, at + 24 : at + 48, 0:128] = value[36:60]
@@ -175,16 +191,29 @@
                 parts = [even, pltpu.roll(even, 64, 1), odd, pltpu.roll(odd, 64, 1)]
                 line[k, at : at + 48, 128:256] = jnp.concatenate(parts, axis=0)
 
+    for copy in strips:
+        copy.wait()
+    for h in range(2):
+        for d in range(2):
+            for i in range(3):
+                rows = slice(QUARTER * d + 128 * i, QUARTER * d + 128 * i + 128)
+                lanes = slice(128 * (2 - i), 128 * (2 - i) + QUARTER)
+                for k in range(2):
+                    small[k, h, rows, :] = small_strip[k, h, d, :, lanes]
+    for h in range(2):
+        for d in range(2):
+            for i in range(3):
+                rows = slice(HALF * d + 256 * i, HALF * d + 256 * i + 256)
+                lanes = slice(256 * (2 - i), 256 * (2 - i) + HALF)
+                large[h, rows, :] = large_strip[h, d, :, lanes]
+
     head, tail = line[0, :QUARTER, :], line[0, QUARTER:, :]
     for k, value in enumerate((head + tail, head - tail)):
         high, low = split(value)
-        loads[k].wait()
-        got_small[k] = three(small[k, :, :QUARTER], small[k, :, QUARTER:], high, low)
+        got_small[k] = three(small[k, 0], small[k, 1], high, low)
     high, low = split(line[1])
-    loads[2].wait()
     total = jnp.dot(large[0], high, preferred_element_type=F32)
     total = total + jnp.dot(large[0], low, preferred_element_type=F32)
-    loads[3].wait()
     got_large[...] = total + jnp.dot(large[1], high, preferred_element_type=F32)
 
     near = low_lanes((12, 128))
@@ -210,54 +239,41 @@
         put.wait()
 
 
-def cross(table, message):
+def cross(small, large, message):
     return pl.pallas_call(
         cross_kernel,
         out_shape=jax.ShapeDtypeStruct((8, 4, 2, 72, 128), F32),
-        in_specs=[pl.BlockSpec(memory_space=pltpu.HBM), pl.BlockSpec(memory_space=pltpu.VMEM)],
+        in_specs=[
+            pl.BlockSpec(memory_space=pltpu.HBM),
+            pl.BlockSpec(memory_space=pltpu.HBM),
+            pl.BlockSpec(memory_space=pl.ANY),
+        ],
         out_specs=pl.BlockSpec(memory_space=pltpu.HBM),
         scratch_shapes=[
-            pltpu.VMEM((2, HALF, HALF), BF16),
+            pltpu.VMEM(small.shape, BF16),
+            pltpu.VMEM(large.shape, BF16),
+            pltpu.VMEM((2, 2, HALF, QUARTER), BF16),
             pltpu.VMEM((2, COUNT, HALF), BF16),
+            pltpu.VMEM((4, 2, 4, 72, 128), F32),
             pltpu.VMEM((8, 4, 2, 72, 128), F32),
             pltpu.VMEM((2, HALF, 256), F32),
             pltpu.VMEM((2, HALF, 256), F32),
             pltpu.VMEM((COUNT, 256), F32),
             pltpu.SemaphoreType.DMA((4,)),
+            pltpu.SemaphoreType.DMA((2,)),
             pltpu.SemaphoreType.DMA((8,)),
         ],
-        compiler_params=pltpu.CompilerParams(vmem_limit_bytes=50 * 2**20),
+        compiler_params=pltpu.CompilerParams(vmem_limit_bytes=60 * 2**20),
         cost_estimate=pl.CostEstimate(
             flops=3 * 2 * 3 * HALF * HALF * 256, bytes_accessed=12 * 2**20, transcendentals=0
         ),
-    )(table, message.reshape(2, 4, 4, 72, 128))
+    )(small, large, message.reshape(2, 4, 4, 72, 128))
 
 
 def along_kernel(
-    core_ref,
-    table_hbm,
-    own,
-    near,
-    far_a,
-    far_b,
-    far_near_a,
-    far_near_b,
-    first_ref,
-    second_ref,
-    table_ref,
-    sem,
+    core_ref, table_ref, own, near, far_a, far_b, far_near_a, far_near_b, first_ref, second_ref
 ):
     core = core_ref[0]
-
-    @pl.when(pl.program_id(0) == 0)
-    def _():
-        load = pltpu.make_async_copy(table_hbm.at[4608:7680], table_ref, sem)
-        load.start()
-        load.wait()
-
-    def block_of(h, r):
-        return table_ref[pl.ds(pl.multiple_of(COUNT * h + LANES * r, LANES), LANES), :]
-
     early = pl.program_id(0) == 0
     far = jnp.where(early, far_a[...], far_b[...])
     far_near = jnp.where(early, far_near_a[...], far_near_b[...])
@@ -265,7 +281,7 @@
     pairs = ((own[...], 0), (near[...], 1 + 2 * core), (far, 2), (far_near, 3 - 2 * core))
     for block, r in pairs:
         high, low = split(block)
-        total = total + three(high, low, block_of(0, r), block_of(1, r))
+        total = total + three(high, low, table_ref[0, r], table_ref[1, r])
     first_ref[...] = total[:, :LANES]
     second_ref[...] = total[:, LANES:]
 
@@ -280,16 +296,12 @@
         grid_spec=pltpu.PrefetchScalarGridSpec(
             num_scalar_prefetch=1,
             grid=(3,),
-            in_specs=[pl.BlockSpec(memory_space=pltpu.HBM)]
+            in_specs=[pl.BlockSpec((2, 4, LANES, 2 * LANES), lambda i, core: (0, 0, 0, 0))]
             + [lines, lines, early, late, early, late],
             out_specs=[lines] * 2,
-            scratch_shapes=[
-                pltpu.VMEM((2 * COUNT, 2 * LANES), BF16),
-                pltpu.SemaphoreType.DMA,
-            ],
         ),
         out_shape=(out, out),
-        compiler_params=pltpu.CompilerParams(vmem_limit_bytes=50 * 2**20),
+        compiler_params=pltpu.CompilerParams(vmem_limit_bytes=24 * 2**20),
         cost_estimate=pl.CostEstimate(
             flops=2 * 3 * 768 * COUNT * 768, bytes_accessed=16 * 2**20, transcendentals=0
         ),
@@ -298,7 +310,8 @@
 
 def solution(mesh):
     fine = Mesh(mesh.devices.reshape(8, 4, 2, 2, 2), ("z", "y", "xl", "xh", "c"))
-    table_t = tables()
+    small_t, large_t = cross_strips()
+    along_t = along_table()
     pair = [(0, 1), (1, 0)]
 
     def swap(message):
@@ -306,19 +319,18 @@
 
     def shards(moments):
         grid = moments.shape
-        table = jnp.asarray(table_t)
         own = moments.reshape(ROWS * PLANES, LANES)
         far_a = lax.ppermute(own[:256], "xh", pair)
         near = lax.ppermute(own, "c", pair)
         home = swap(pack(moments.reshape(ROWS, PLANES, LANES)).reshape(64, 9, 4, 128))
         home, far_a, near = lax.optimization_barrier((home, far_a, near))
         far_b = lax.ppermute(own[256:], "xh", pair)
-        back = swap(cross(table, home).reshape(64, 72, 128))
+        back = swap(cross(jnp.asarray(small_t), jnp.asarray(large_t), home).reshape(64, 72, 128))
         far_near_a = lax.ppermute(far_a, "c", pair)
         far_near_b = lax.ppermute(far_b, "c", pair)
         core = lax.axis_index("c").reshape(1)
         first_z, second_z = along(
-            core, table, own, near, far_a, far_b, far_near_a, far_near_b
+            core, jnp.asarray(along_t), own, near, far_a, far_b, far_near_a, far_near_b
         )
         first_z, second_z, back = lax.optimization_barrier((first_z, second_z, back))
         first, second = unpack(back.reshape(4608, 128))

time: 123 us -> 120 us (0.976)
  Pallas kernels: 24.7 us -> 21.4 us
  waiting for transfers between devices: 72.3 us -> 70.2 us
  local copies, waits for them, and re-layouts: 3.79 us -> 5.72 us
    pallas_call x1, Pallas kernels: 12.5 us -> 9.99 us  [along(): pl.pallas_call(along_kernel, grid_spec=pltpu.PrefetchScalarGridSpec(num_s...]
    all_to_all x2, waiting for transfers between devices: 16.3 us -> 14.2 us  [swap(): lax.all_to_all(message, ('z', 'y', 'xl'), split_axis=0, concat_axis=0, ti...]
    unnamed x8 -> x10, local copies, waits for them, and re-layouts: 3.71 us -> 5.64 us
  transfers between devices with their start and end apart: 7 -> 7, of which waited for: 6 -> 6; matrix products, arithmetic and copies ran while one was open for 0% -> 0% of each run, Pallas kernels for 10% -> 8%
where the time goes in v2:
time: 120 us; the launch traced here: 119 us
  waiting for transfers between devices  70.2 us (58%)
  Pallas kernels  21.4 us (18%)
  starting transfers between devices  21.2 us (18%)
  local copies, waits for them, and re-layouts  5.72 us (5%)
    ppermute x1, waiting for transfers between devices, shards(): far_b = lax.ppermute(own[256:], 'xh', pair)  34.3 us
    ppermute x1, waiting for transfers between devices, shards(): far_a = lax.ppermute(own[:256], 'xh', pair)  19.1 us
    all_to_all x2, starting transfers between devices, swap(): lax.all_to_all(message, ('z', 'y', 'xl'), split_axis=0, concat_axis=0, ti...  18.9 us
    all_to_all x2, waiting for transfers between devices, swap(): lax.all_to_all(message, ('z', 'y', 'xl'), split_axis=0, concat_axis=0, ti...  14.2 us
    pallas_call x1, Pallas kernels, along(): pl.pallas_call(along_kernel, grid_spec=pltpu.PrefetchScalarGridSpec(num_s...  9.99 us
    pallas_call x1, Pallas kernels, cross(): pl.pallas_call(cross_kernel, out_shape=jax.ShapeDtypeStruct((8, 4, 2, 72,...  7.21 us
    unnamed x10, local copies, waits for them, and re-layouts  5.64 us
  transfers between devices with their start and end apart: 7, of which 6 were waited for; matrix products, arithmetic and copies ran while one was open for 0% of the time, Pallas kernels for 8%

profile of v2, /device:TPU:4, one launch (start us, length us, event | category | flops | bytes accessed | tf_op | source)
XLA Modules:
  0.0 119.3 jit_solution(1413465713455838821)
XLA Ops:
  0.6 2.1 %shard_map.75 = f32[2304,128]{1,0:T(8,128)} custom-call(f32[24,32,384]{2,1,0:T(8,128)} %bitcast.14), custom_call_target="tpu_custom_call" | custom-call | tf_op jit(solution)/shard_map/pallas_call | solution.py:112
  2.8 0.0 copy-start
  2.8 12.9 %all-to-all-start = ((f32[64,9,4,128]{3,2,1,0:T(4,128)}), f32[64,9,4,128]{3,2,1,0:T(4,128)S(1)}, u32[]{:S(2)}, u32[]{:S(2)}) async-start(f32[64,9,4,128]{3,2,1,0:T(4,128)} %bitcast.17), calls=%async_computation | async-start | bytes 2359296 | tf_op jit(solution)/shard_map/all_to_all | solution.py:318
  15.7 0.0 copy-done
  15.7 0.1 collective-permute-start.1
  15.8 0.9 collective-permute-start
  16.7 19.1 %collective-permute-done.far_a = f32[256,384]{1,0:T(8,128)} collective-permute-done((f32[256,384]{1,0:T(8,128)S(1)}, f32[256,384]{1,0:T(8,128)}, u32[]{:S(2)}, u32[]{:S(2)}) %collective-permute-start) | collective-permute-done | bytes 393248 | tf_op jit(solution)/shard_map/ppermute | solution.py:323
  35.8 0.0 collective-permute-done.1.near
  35.8 0.0 copy-start.1
  35.8 1.0 copy-done.1
  36.8 10.5 %all-to-all-done = f32[64,9,4,128]{3,2,1,0:T(4,128)S(1)} async-done(((f32[64,9,4,128]{3,2,1,0:T(4,128)}), f32[64,9,4,128]{3,2,1,0:T(4,128)S(1)}, u32[]{:S(2)}, u32[]{:S(2)}) %all-to-all-start) | async-done | bytes 1179680 | tf_op jit(solution)/shard_map/all_to_all | solution.py:318
  47.3 0.0 copy-start.4
  47.3 1.0 copy-done.4
  48.3 7.2 %shard_map.77 = f32[8,4,2,72,128]{4,3,2,1,0:T(8,128)} custom-call(bf16[2,2,2,128,640]{4,3,2,1,0:T(8,128)(2,1)} %constant.10.clone.small_hbm, bf16[2,2,256,1280]{3,2,1,0:T(8,128)(2,1)} %constant.11.clone.large_hbm, f32[2,4,4,72,128]{4,3,2,1,0:T(8,128)} %bitcast.19), custom_call_target="tpu_custom_call" | custom-call | flops 2717908992 | bytes 12582912 | tf_op jit(solution)/shard_map/pallas_call | solution.py:243
  55.5 6.0 %all-to-all-start.1 = ((f32[64,72,128]{2,1,0:T(8,128)}), f32[64,72,128]{2,1,0:T(8,128)S(1)}, u32[]{:S(2)}, u32[]{:S(2)}) async-start(f32[64,72,128]{2,1,0:T(8,128)} %bitcast.18), calls=%async_computation.1 | async-start | bytes 4718592 | tf_op jit(solution)/shard_map/all_to_all | solution.py:318
  61.5 0.1 slice.14
  61.5 0.9 collective-permute-start.2
  62.4 34.3 %collective-permute-done.2.far_b = f32[512,384]{1,0:T(8,128)} collective-permute-done((f32[512,384]{1,0:T(8,128)S(1)}, f32[512,384]{1,0:T(8,128)}, u32[]{:S(2)}, u32[]{:S(2)}) %collective-permute-start.2) | collective-permute-done | bytes 786464 | tf_op jit(solution)/shard_map/ppermute | solution.py:327
  96.7 0.0 collective-permute-start.4
  96.7 0.5 collective-permute-start.3
  97.2 2.1 %collective-permute-done.4.far_near_b = f32[512,384]{1,0:T(8,128)} collective-permute-done((f32[512,384]{1,0:T(8,128)}, f32[512,384]{1,0:T(8,128)}, u32[]{:S(2)}, u32[]{:S(2)}) %collective-permute-start.4) | collective-permute-done | bytes 786464 | tf_op jit(solution)/shard_map/ppermute | solution.py:330
  99.3 0.6 collective-permute-done.3.far_near_a
  99.9 0.0 copy-start.2
  99.9 1.3 %copy-done.2 = f32[768,384]{1,0:T(8,128)S(1)} copy-done((f32[768,384]{1,0:T(8,128)S(1)}, f32[768,384]{1,0:T(8,128)}, u32[]{:S(2)}) %copy-start.2) | copy-done | bytes 1179672
  101.1 0.0 copy-start.3
  101.1 2.3 %copy-done.3 = bf16[2,4,384,768]{3,2,1,0:T(8,128)(2,1)S(1)} copy-done((bf16[2,4,384,768]{3,2,1,0:T(8,128)(2,1)S(1)}, bf16[2,4,384,768]{3,2,1,0:T(8,128)(2,1)}, u32[]{:S(2)}) %copy-start.3) | copy-done | bytes 4718616
  103.5 10.0 %shard_map.76 = (f32[768,384]{1,0:T(8,128)}, f32[768,384]{1,0:T(8,128)}) custom-call(s32[1]{0:T(128)} %bitcast.core_ref, bf16[2,4,384,768]{3,2,1,0:T(8,128)(2,1)S(1)} %copy-done.3, f32[768,384]{1,0:T(8,128)S(1)} %bitcast.16, f32[768,384]{1,0:T(8,128)S(1)} %copy-done.2, f32[256,384]{1,0:T(8,128)} %collective-permute-done.far_a, ...), custom_call_target="tpu_custom_call" | custom-call | flops 5435817984 | bytes 16777216 | tf_op jit(solution)/shard_map/pallas_call | solution.py:294
  113.5 3.8 %all-to-all-done.1 = f32[64,72,128]{2,1,0:T(8,128)S(1)} async-done(((f32[64,72,128]{2,1,0:T(8,128)}), f32[64,72,128]{2,1,0:T(8,128)S(1)}, u32[]{:S(2)}, u32[]{:S(2)}) %all-to-all-start.1) | async-done | bytes 2359328 | tf_op jit(solution)/shard_map/all_to_all | solution.py:318
  117.2 2.0 %shard_map.78 = (f32[24,32,384]{2,1,0:T(8,128)}, f32[24,32,384]{2,1,0:T(8,128)}) custom-call(f32[4608,128]{1,0:T(8,128)S(1)} %bitcast.13), custom_call_target="tpu_custom_call" | custom-call | tf_op jit(solution)/shard_map/pallas_call | solution.py:143
  (1 shorter events, 0.0 us)
Async XLA Ops:
  2.8 12.9 %copy-start = (f32[24,2,16,384]{3,2,1,0:T(8,128)S(1)}, f32[24,2,16,384]{3,2,1,0:T(8,128)}, u32[]{:S(2)}) copy-start(f32[24,2,16,384]{3,2,1,0:T(8,128)} %param.4) | copy-start | bytes 3538948
  2.8 44.5 %all-to-all-start = ((f32[64,9,4,128]{3,2,1,0:T(4,128)}), f32[64,9,4,128]{3,2,1,0:T(4,128)S(1)}, u32[]{:S(2)}, u32[]{:S(2)}) async-start(f32[64,9,4,128]{3,2,1,0:T(4,128)} %bitcast.17), calls=%async_computation | async-start | bytes 2359296 | tf_op jit(solution)/shard_map/all_to_all | solution.py:318
  15.7 20.1 %collective-permute-start.1 = (f32[768,384]{1,0:T(8,128)S(1)}, f32[768,384]{1,0:T(8,128)S(1)}, u32[]{:S(2)}, u32[]{:S(2)}) collective-permute-start(f32[768,384]{1,0:T(8,128)S(1)} %bitcast.15), channel_id=1, source_target_pairs={{0,1},{1,0},{2,3},{3,2},{4,5},{5,4},{6,7},{7,6},{8,9},{9,8},{10,11... | collective-permute-start | bytes 3538952 | tf_op jit(solution)/shard_map/ppermute | solution.py:324
  15.8 20.0 %collective-permute-start = (f32[256,384]{1,0:T(8,128)S(1)}, f32[256,384]{1,0:T(8,128)}, u32[]{:S(2)}, u32[]{:S(2)}) collective-permute-start(f32[256,384]{1,0:T(8,128)S(1)} %bitcast.21), channel_id=1, source_target_pairs={{0,2},{2,0},{1,3},{3,1},{4,6},{6,4},{5,7},{7,5},{8,10},{10,8},{9,1... | collective-permute-start | bytes 1179656 | tf_op jit(solution)/shard_map/ppermute | solution.py:323
  35.8 1.0 copy-start.1
  47.3 1.0 copy-start.4
  55.5 61.7 %all-to-all-start.1 = ((f32[64,72,128]{2,1,0:T(8,128)}), f32[64,72,128]{2,1,0:T(8,128)S(1)}, u32[]{:S(2)}, u32[]{:S(2)}) async-start(f32[64,72,128]{2,1,0:T(8,128)} %bitcast.18), calls=%async_computation.1 | async-start | bytes 4718592 | tf_op jit(solution)/shard_map/all_to_all | solution.py:318
  61.5 35.1 %collective-permute-start.2 = (f32[512,384]{1,0:T(8,128)S(1)}, f32[512,384]{1,0:T(8,128)}, u32[]{:S(2)}, u32[]{:S(2)}) collective-permute-start(f32[512,384]{1,0:T(8,128)S(1)} %bitcast.20), channel_id=1, source_target_pairs={{0,2},{2,0},{1,3},{3,1},{4,6},{6,4},{5,7},{7,5},{8,10},{10,8},{9,1... | collective-permute-start | bytes 2359304 | tf_op jit(solution)/shard_map/ppermute | solution.py:327
  96.7 2.6 %collective-permute-start.4 = (f32[512,384]{1,0:T(8,128)}, f32[512,384]{1,0:T(8,128)}, u32[]{:S(2)}, u32[]{:S(2)}) collective-permute-start(f32[512,384]{1,0:T(8,128)} %collective-permute-done.2.far_b), channel_id=1, source_target_pairs={{0,1},{1,0},{2,3},{3,2},{4,5},{5,4},{6,7},{7,6},{8,9},{9,8},{10,11... | collective-permute-start | bytes 2359304 | tf_op jit(solution)/shard_map/ppermute | solution.py:330
  96.7 3.2 %collective-permute-start.3 = (f32[256,384]{1,0:T(8,128)}, f32[256,384]{1,0:T(8,128)}, u32[]{:S(2)}, u32[]{:S(2)}) collective-permute-start(f32[256,384]{1,0:T(8,128)} %collective-permute-done.far_a), channel_id=1, source_target_pairs={{0,1},{1,0},{2,3},{3,2},{4,5},{5,4},{6,7},{7,6},{8,9},{9,8},{10,11... | collective-permute-start | bytes 1179656 | tf_op jit(solution)/shard_map/ppermute | solution.py:329
  99.9 1.3 %copy-start.2 = (f32[768,384]{1,0:T(8,128)S(1)}, f32[768,384]{1,0:T(8,128)}, u32[]{:S(2)}) copy-start(f32[768,384]{1,0:T(8,128)} %copy-done.1) | copy-start | bytes 3538948
  101.1 2.3 %copy-start.3 = (bf16[2,4,384,768]{3,2,1,0:T(8,128)(2,1)S(1)}, bf16[2,4,384,768]{3,2,1,0:T(8,128)(2,1)}, u32[]{:S(2)}) copy-start(bf16[2,4,384,768]{3,2,1,0:T(8,128)(2,1)} %constant.12.clone.table_ref) | copy-start | bytes 14155780

commit v3 on v2

--- a/solution.py
+++ b/solution.py
@@ -79,73 +79,80 @@
     return lax.broadcasted_iota(jnp.int32, shape, len(shape) - 1) < 64
 
 
-def pack_kernel(x_hbm, msg_hbm, x_ref, msg_ref, in_sems, out_sems):
+def pack_kernel(x_hbm, msg_ref, x_ref, sems):
     gets = [
-        pltpu.make_async_copy(x_hbm.at[:, 8 * g : 8 * g + 8], x_ref.at[g], in_sems.at[g])
-        for g in range(4)
-    ]
-    puts = [
-        pltpu.make_async_copy(msg_ref.at[g], msg_hbm.at[576 * g : 576 * g + 576], out_sems.at[g])
+        pltpu.make_async_copy(x_hbm.at[:, 8 * g : 8 * g + 8], x_ref.at[g], sems.at[g])
         for g in range(4)
     ]
     near = low_lanes((8, 128))
     for get in gets:
         get.start()
     for g in range(4):
+        base = 576 * g
         gets[g].wait()
         for i in range(ROWS):
             for low in range(2):
-                at = pl.ds(36 * low + i, 8, stride=72)
-                msg_ref[g, at, :] = x_ref[g, i, :, 128 * low : 128 * low + 128]
+                at = pl.ds(base + 36 * low + i, 8, stride=72)
+                msg_ref[at, :] = x_ref[g, i, :, 128 * low : 128 * low + 128]
         for i in range(12):
             top, bottom = x_ref[g, i, :, 256:384], x_ref[g, i + 12, :, 256:384]
             lower = jnp.where(near, top, pltpu.roll(bottom, 64, 1))
             upper = jnp.where(near, pltpu.roll(top, 64, 1), bottom)
-            msg_ref[g, pl.ds(24 + i, 8, stride=72), :] = lower
-            msg_ref[g, pl.ds(60 + i, 8, stride=72), :] = upper
-        puts[g].start()
-    for put in puts:
-        put.wait()
+            msg_ref[pl.ds(base + 24 + i, 8, stride=72), :] = lower
+            msg_ref[pl.ds(base + 60 + i, 8, stride=72), :] = upper
 
 
 def pack(block):
     return pl.pallas_call(
         pack_kernel,
         in_specs=[pl.BlockSpec(memory_space=pltpu.HBM)],
-        out_specs=pl.BlockSpec(memory_space=pltpu.HBM),
+        out_specs=pl.BlockSpec(memory_space=pltpu.VMEM),
         out_shape=jax.ShapeDtypeStruct((2304, 128), F32),
         scratch_shapes=[
             pltpu.VMEM((4, ROWS, 8, LANES), F32),
-            pltpu.VMEM((4, 576, 128), F32),
-            pltpu.SemaphoreType.DMA((4,)),
             pltpu.SemaphoreType.DMA((4,)),
         ],
         compiler_params=pltpu.CompilerParams(vmem_limit_bytes=56 * 2**20),
     )(block)
 
 
-def unpack_kernel(msg_ref, first_ref, second_ref):
+def unpack_kernel(msg_ref, first_hbm, second_hbm, out_ref, sems):
     near = low_lanes((8, 128))
-    for out_ref, full, part in ((first_ref, 0, 24), (second_ref, 48, 36)):
-        for i in range(ROWS):
-            for low in range(2):
-                at = pl.ds(72 * low + full + i, 8, stride=144)
-                out_ref[i, :, 128 * low : 128 * low + 128] = msg_ref[at, :]
-        for i in range(12):
-            lower = msg_ref[pl.ds(part + i, 8, stride=144), :]
-            upper = msg_ref[pl.ds(72 + part + i, 8, stride=144), :]
-            out_ref[i, :, 256:384] = jnp.where(near, lower, pltpu.roll(upper, 64, 1))
-            out_ref[i + 12, :, 256:384] = jnp.where(near, pltpu.roll(lower, 64, 1), upper)
+    puts = []
+    for g in range(4):
+        base = 1152 * g
+        for d, (out_hbm, full, part) in enumerate(((first_hbm, 0, 24), (second_hbm, 48, 36))):
+            for i in range(ROWS):
+                for low in range(2):
+                    at = pl.ds(base + 72 * low + full + i, 8, stride=144)
+                    out_ref[d, g, i, :, 128 * low : 128 * low + 128] = msg_ref[at, :]
+            for i in range(12):
+                lower = msg_ref[pl.ds(base + part + i, 8, stride=144), :]
+                upper = msg_ref[pl.ds(base + 72 + part + i, 8, stride=144), :]
+                out_ref[d, g, i, :, 256:384] = jnp.where(near, lower, pltpu.roll(upper, 64, 1))
+                out_ref[d, g, i + 12, :, 256:384] = jnp.where(
+                    near, pltpu.roll(lower, 64, 1), upper
+                )
+            put = pltpu.make_async_copy(
+                out_ref.at[d, g], out_hbm.at[:, 8 * g : 8 * g + 8], sems.at[2 * g + d]
+            )
+            put.start()
+            puts.append(put)
+    for put in puts:
+        put.wait()
 
 
 def unpack(message):
     out = jax.ShapeDtypeStruct((ROWS, PLANES, LANES), F32)
     return pl.pallas_call(
         unpack_kernel,
-        grid=(4,),
-        in_specs=[pl.BlockSpec((1152, 128), lambda i: (i, 0))],
-        out_specs=[pl.BlockSpec((ROWS, 8, LANES), lambda i: (0, i, 0))] * 2,
+        in_specs=[pl.BlockSpec(memory_space=pltpu.VMEM)],
+        out_specs=[pl.BlockSpec(memory_space=pltpu.HBM)] * 2,
         out_shape=(out, out),
+        scratch_shapes=[
+            pltpu.VMEM((2, 4, ROWS, 8, LANES), F32),
+            pltpu.SemaphoreType.DMA((8,)),
+        ],
         compiler_params=pltpu.CompilerParams(vmem_limit_bytes=16 * 2**20),
     )(message)
 

time: 120 us -> 120 us (level)
  no operation moved by 1% of the time
where the time goes in v3:
time: 120 us; the launch traced here: 119 us
  waiting for transfers between devices  70.2 us (58%)
  Pallas kernels  21.3 us (18%)
  starting transfers between devices  21.2 us (18%)
  local copies, waits for them, and re-layouts  5.72 us (5%)
    ppermute x1, waiting for transfers between devices, shards(): far_b = lax.ppermute(own[256:], 'xh', pair)  34.3 us
    ppermute x1, waiting for transfers between devices, shards(): far_a = lax.ppermute(own[:256], 'xh', pair)  19.1 us
    all_to_all x2, starting transfers between devices, swap(): lax.all_to_all(message, ('z', 'y', 'xl'), split_axis=0, concat_axis=0, ti...  18.9 us
    all_to_all x2, waiting for transfers between devices, swap(): lax.all_to_all(message, ('z', 'y', 'xl'), split_axis=0, concat_axis=0, ti...  14.2 us
    pallas_call x1, Pallas kernels, along(): pl.pallas_call(along_kernel, grid_spec=pltpu.PrefetchScalarGridSpec(num_s...  9.99 us
    pallas_call x1, Pallas kernels, cross(): pl.pallas_call(cross_kernel, out_shape=jax.ShapeDtypeStruct((8, 4, 2, 72,...  7.21 us
    unnamed x10, local copies, waits for them, and re-layouts  5.64 us
    pallas_call x1, Pallas kernels, pack(): pl.pallas_call(pack_kernel, in_specs=[pl.BlockSpec(memory_space=pltpu.HBM...  2.47 us
  transfers between devices with their start and end apart: 7, of which 6 were waited for; matrix products, arithmetic and copies ran while one was open for 0% of the time, Pallas kernels for 8%

profile of v3, /device:TPU:4, one launch (start us, length us, event | category | flops | bytes accessed | tf_op | source)
XLA Modules:
  0.0 119.2 jit_solution(10957889929260215908)
XLA Ops:
  0.6 2.5 %shard_map.75 = f32[2304,128]{1,0:T(8,128)} custom-call(f32[24,32,384]{2,1,0:T(8,128)} %bitcast.14), custom_call_target="tpu_custom_call" | custom-call | tf_op jit(solution)/shard_map/pallas_call | solution.py:106
  3.1 0.0 copy-start
  3.1 12.9 %all-to-all-start = ((f32[64,9,4,128]{3,2,1,0:T(4,128)}), f32[64,9,4,128]{3,2,1,0:T(4,128)S(1)}, u32[]{:S(2)}, u32[]{:S(2)}) async-start(f32[64,9,4,128]{3,2,1,0:T(4,128)} %bitcast.17), calls=%async_computation | async-start | bytes 2359296 | tf_op jit(solution)/shard_map/all_to_all | solution.py:325
  16.0 0.0 copy-done
  16.0 0.1 collective-permute-start.1
  16.2 0.9 collective-permute-start
  17.0 19.1 %collective-permute-done.far_a = f32[256,384]{1,0:T(8,128)} collective-permute-done((f32[256,384]{1,0:T(8,128)S(1)}, f32[256,384]{1,0:T(8,128)}, u32[]{:S(2)}, u32[]{:S(2)}) %collective-permute-start) | collective-permute-done | bytes 393248 | tf_op jit(solution)/shard_map/ppermute | solution.py:330
  36.1 0.0 collective-permute-done.1.near
  36.1 0.0 copy-start.1
  36.1 1.0 copy-done.1
  37.1 10.5 %all-to-all-done = f32[64,9,4,128]{3,2,1,0:T(4,128)S(1)} async-done(((f32[64,9,4,128]{3,2,1,0:T(4,128)}), f32[64,9,4,128]{3,2,1,0:T(4,128)S(1)}, u32[]{:S(2)}, u32[]{:S(2)}) %all-to-all-start) | async-done | bytes 1179680 | tf_op jit(solution)/shard_map/all_to_all | solution.py:325
  47.6 0.0 copy-start.4
  47.6 1.0 copy-done.4
  48.6 7.2 %shard_map.77 = f32[8,4,2,72,128]{4,3,2,1,0:T(8,128)} custom-call(bf16[2,2,2,128,640]{4,3,2,1,0:T(8,128)(2,1)} %constant.10.clone.small_hbm, bf16[2,2,256,1280]{3,2,1,0:T(8,128)(2,1)} %constant.11.clone.large_hbm, f32[2,4,4,72,128]{4,3,2,1,0:T(8,128)} %bitcast.19), custom_call_target="tpu_custom_call" | custom-call | flops 2717908992 | bytes 12582912 | tf_op jit(solution)/shard_map/pallas_call | solution.py:250
  55.8 6.0 %all-to-all-start.1 = ((f32[64,72,128]{2,1,0:T(8,128)}), f32[64,72,128]{2,1,0:T(8,128)S(1)}, u32[]{:S(2)}, u32[]{:S(2)}) async-start(f32[64,72,128]{2,1,0:T(8,128)} %bitcast.18), calls=%async_computation.1 | async-start | bytes 4718592 | tf_op jit(solution)/shard_map/all_to_all | solution.py:325
  61.8 0.1 slice.14
  61.9 0.9 collective-permute-start.2
  62.8 34.3 %collective-permute-done.2.far_b = f32[512,384]{1,0:T(8,128)} collective-permute-done((f32[512,384]{1,0:T(8,128)S(1)}, f32[512,384]{1,0:T(8,128)}, u32[]{:S(2)}, u32[]{:S(2)}) %collective-permute-start.2) | collective-permute-done | bytes 786464 | tf_op jit(solution)/shard_map/ppermute | solution.py:334
  97.0 0.0 collective-permute-start.4
  97.0 0.5 collective-permute-start.3
  97.5 2.1 %collective-permute-done.4.far_near_b = f32[512,384]{1,0:T(8,128)} collective-permute-done((f32[512,384]{1,0:T(8,128)}, f32[512,384]{1,0:T(8,128)}, u32[]{:S(2)}, u32[]{:S(2)}) %collective-permute-start.4) | collective-permute-done | bytes 786464 | tf_op jit(solution)/shard_map/ppermute | solution.py:337
  99.6 0.6 collective-permute-done.3.far_near_a
  100.2 0.0 copy-start.2
  100.2 1.3 %copy-done.2 = f32[768,384]{1,0:T(8,128)S(1)} copy-done((f32[768,384]{1,0:T(8,128)S(1)}, f32[768,384]{1,0:T(8,128)}, u32[]{:S(2)}) %copy-start.2) | copy-done | bytes 1179672
  101.5 0.0 copy-start.3
  101.5 2.3 %copy-done.3 = bf16[2,4,384,768]{3,2,1,0:T(8,128)(2,1)S(1)} copy-done((bf16[2,4,384,768]{3,2,1,0:T(8,128)(2,1)S(1)}, bf16[2,4,384,768]{3,2,1,0:T(8,128)(2,1)}, u32[]{:S(2)}) %copy-start.3) | copy-done | bytes 4718616
  103.8 10.0 %shard_map.76 = (f32[768,384]{1,0:T(8,128)}, f32[768,384]{1,0:T(8,128)}) custom-call(s32[1]{0:T(128)} %bitcast.core_ref, bf16[2,4,384,768]{3,2,1,0:T(8,128)(2,1)S(1)} %copy-done.3, f32[768,384]{1,0:T(8,128)S(1)} %bitcast.16, f32[768,384]{1,0:T(8,128)S(1)} %copy-done.2, f32[256,384]{1,0:T(8,128)} %collective-permute-done.far_a, ...), custom_call_target="tpu_custom_call" | custom-call | flops 5435817984 | bytes 16777216 | tf_op jit(solution)/shard_map/pallas_call | solution.py:301
  113.8 3.8 %all-to-all-done.1 = f32[64,72,128]{2,1,0:T(8,128)S(1)} async-done(((f32[64,72,128]{2,1,0:T(8,128)}), f32[64,72,128]{2,1,0:T(8,128)S(1)}, u32[]{:S(2)}, u32[]{:S(2)}) %all-to-all-start.1) | async-done | bytes 2359328 | tf_op jit(solution)/shard_map/all_to_all | solution.py:325
  117.6 1.6 %shard_map.78 = (f32[24,32,384]{2,1,0:T(8,128)}, f32[24,32,384]{2,1,0:T(8,128)}) custom-call(f32[4608,128]{1,0:T(8,128)S(1)} %bitcast.13), custom_call_target="tpu_custom_call" | custom-call | tf_op jit(solution)/shard_map/pallas_call | solution.py:147
  (1 shorter events, 0.0 us)
Async XLA Ops:
  3.1 12.9 %copy-start = (f32[24,2,16,384]{3,2,1,0:T(8,128)S(1)}, f32[24,2,16,384]{3,2,1,0:T(8,128)}, u32[]{:S(2)}) copy-start(f32[24,2,16,384]{3,2,1,0:T(8,128)} %param.4) | copy-start | bytes 3538948
  3.1 44.5 %all-to-all-start = ((f32[64,9,4,128]{3,2,1,0:T(4,128)}), f32[64,9,4,128]{3,2,1,0:T(4,128)S(1)}, u32[]{:S(2)}, u32[]{:S(2)}) async-start(f32[64,9,4,128]{3,2,1,0:T(4,128)} %bitcast.17), calls=%async_computation | async-start | bytes 2359296 | tf_op jit(solution)/shard_map/all_to_all | solution.py:325
  16.0 20.1 %collective-permute-start.1 = (f32[768,384]{1,0:T(8,128)S(1)}, f32[768,384]{1,0:T(8,128)S(1)}, u32[]{:S(2)}, u32[]{:S(2)}) collective-permute-start(f32[768,384]{1,0:T(8,128)S(1)} %bitcast.15), channel_id=1, source_target_pairs={{0,1},{1,0},{2,3},{3,2},{4,5},{5,4},{6,7},{7,6},{8,9},{9,8},{10,11... | collective-permute-start | bytes 3538952 | tf_op jit(solution)/shard_map/ppermute | solution.py:331
  16.2 20.0 %collective-permute-start = (f32[256,384]{1,0:T(8,128)S(1)}, f32[256,384]{1,0:T(8,128)}, u32[]{:S(2)}, u32[]{:S(2)}) collective-permute-start(f32[256,384]{1,0:T(8,128)S(1)} %bitcast.21), channel_id=1, source_target_pairs={{0,2},{2,0},{1,3},{3,1},{4,6},{6,4},{5,7},{7,5},{8,10},{10,8},{9,1... | collective-permute-start | bytes 1179656 | tf_op jit(solution)/shard_map/ppermute | solution.py:330
  36.1 1.0 copy-start.1
  47.6 1.0 copy-start.4
  55.8 61.7 %all-to-all-start.1 = ((f32[64,72,128]{2,1,0:T(8,128)}), f32[64,72,128]{2,1,0:T(8,128)S(1)}, u32[]{:S(2)}, u32[]{:S(2)}) async-start(f32[64,72,128]{2,1,0:T(8,128)} %bitcast.18), calls=%async_computation.1 | async-start | bytes 4718592 | tf_op jit(solution)/shard_map/all_to_all | solution.py:325
  61.9 35.1 %collective-permute-start.2 = (f32[512,384]{1,0:T(8,128)S(1)}, f32[512,384]{1,0:T(8,128)}, u32[]{:S(2)}, u32[]{:S(2)}) collective-permute-start(f32[512,384]{1,0:T(8,128)S(1)} %bitcast.20), channel_id=1, source_target_pairs={{0,2},{2,0},{1,3},{3,1},{4,6},{6,4},{5,7},{7,5},{8,10},{10,8},{9,1... | collective-permute-start | bytes 2359304 | tf_op jit(solution)/shard_map/ppermute | solution.py:334
  97.0 2.6 %collective-permute-start.4 = (f32[512,384]{1,0:T(8,128)}, f32[512,384]{1,0:T(8,128)}, u32[]{:S(2)}, u32[]{:S(2)}) collective-permute-start(f32[512,384]{1,0:T(8,128)} %collective-permute-done.2.far_b), channel_id=1, source_target_pairs={{0,1},{1,0},{2,3},{3,2},{4,5},{5,4},{6,7},{7,6},{8,9},{9,8},{10,11... | collective-permute-start | bytes 2359304 | tf_op jit(solution)/shard_map/ppermute | solution.py:337
  97.0 3.2 %collective-permute-start.3 = (f32[256,384]{1,0:T(8,128)}, f32[256,384]{1,0:T(8,128)}, u32[]{:S(2)}, u32[]{:S(2)}) collective-permute-start(f32[256,384]{1,0:T(8,128)} %collective-permute-done.far_a), channel_id=1, source_target_pairs={{0,1},{1,0},{2,3},{3,2},{4,5},{5,4},{6,7},{7,6},{8,9},{9,8},{10,11... | collective-permute-start | bytes 1179656 | tf_op jit(solution)/shard_map/ppermute | solution.py:336
  100.2 1.3 %copy-start.2 = (f32[768,384]{1,0:T(8,128)S(1)}, f32[768,384]{1,0:T(8,128)}, u32[]{:S(2)}) copy-start(f32[768,384]{1,0:T(8,128)} %copy-done.1) | copy-start | bytes 3538948
  101.5 2.3 %copy-start.3 = (bf16[2,4,384,768]{3,2,1,0:T(8,128)(2,1)S(1)}, bf16[2,4,384,768]{3,2,1,0:T(8,128)(2,1)}, u32[]{:S(2)}) copy-start(bf16[2,4,384,768]{3,2,1,0:T(8,128)(2,1)} %constant.12.clone.table_ref) | copy-start | bytes 14155780

commit v4 on v3

--- a/solution.py
+++ b/solution.py
@@ -79,37 +79,45 @@
     return lax.broadcasted_iota(jnp.int32, shape, len(shape) - 1) < 64
 
 
-def pack_kernel(x_hbm, msg_ref, x_ref, sems):
+def pack_kernel(x_hbm, msg_hbm, x_ref, msg_ref, in_sems, out_sems):
     gets = [
-        pltpu.make_async_copy(x_hbm.at[:, 8 * g : 8 * g + 8], x_ref.at[g], sems.at[g])
+        pltpu.make_async_copy(x_hbm.at[:, 8 * g : 8 * g + 8], x_ref.at[g], in_sems.at[g])
+        for g in range(4)
+    ]
+    puts = [
+        pltpu.make_async_copy(msg_ref.at[g], msg_hbm.at[576 * g : 576 * g + 576], out_sems.at[g])
         for g in range(4)
     ]
     near = low_lanes((8, 128))
     for get in gets:
         get.start()
     for g in range(4):
-        base = 576 * g
         gets[g].wait()
         for i in range(ROWS):
             for low in range(2):
-                at = pl.ds(base + 36 * low + i, 8, stride=72)
-                msg_ref[at, :] = x_ref[g, i, :, 128 * low : 128 * low + 128]
+                at = pl.ds(36 * low + i, 8, stride=72)
+                msg_ref[g, at, :] = x_ref[g, i, :, 128 * low : 128 * low + 128]
         for i in range(12):
             top, bottom = x_ref[g, i, :, 256:384], x_ref[g, i + 12, :, 256:384]
             lower = jnp.where(near, top, pltpu.roll(bottom, 64, 1))
             upper = jnp.where(near, pltpu.roll(top, 64, 1), bottom)
-            msg_ref[pl.ds(base + 24 + i, 8, stride=72), :] = lower
-            msg_ref[pl.ds(base + 60 + i, 8, stride=72), :] = upper
+            msg_ref[g, pl.ds(24 + i, 8, stride=72), :] = lower
+            msg_ref[g, pl.ds(60 + i, 8, stride=72), :] = upper
+        puts[g].start()
+    for put in puts:
+        put.wait()
 
 
 def pack(block):
     return pl.pallas_call(
         pack_kernel,
         in_specs=[pl.BlockSpec(memory_space=pltpu.HBM)],
-        out_specs=pl.BlockSpec(memory_space=pltpu.VMEM),
+        out_specs=pl.BlockSpec(memory_space=pltpu.HBM),
         out_shape=jax.ShapeDtypeStruct((2304, 128), F32),
         scratch_shapes=[
             pltpu.VMEM((4, ROWS, 8, LANES), F32),
+            pltpu.VMEM((4, 576, 128), F32),
+            pltpu.SemaphoreType.DMA((4,)),
             pltpu.SemaphoreType.DMA((4,)),
         ],
         compiler_params=pltpu.CompilerParams(vmem_limit_bytes=56 * 2**20),
@@ -165,7 +173,6 @@
     small_strip,
     large_strip,
     small,
-    large,
     msg,
     out,
     line,
@@ -207,27 +214,24 @@
                 lanes = slice(128 * (2 - i), 128 * (2 - i) + QUARTER)
                 for k in range(2):
                     small[k, h, rows, :] = small_strip[k, h, d, :, lanes]
-    for h in range(2):
-        for d in range(2):
-            for i in range(3):
-                rows = slice(HALF * d + 256 * i, HALF * d + 256 * i + 256)
-                lanes = slice(256 * (2 - i), 256 * (2 - i) + HALF)
-                large[h, rows, :] = large_strip[h, d, :, lanes]
-
     head, tail = line[0, :QUARTER, :], line[0, QUARTER:, :]
     for k, value in enumerate((head + tail, head - tail)):
         high, low = split(value)
         got_small[k] = three(small[k, 0], small[k, 1], high, low)
+
     high, low = split(line[1])
-    total = jnp.dot(large[0], high, preferred_element_type=F32)
-    total = total + jnp.dot(large[0], low, preferred_element_type=F32)
-    got_large[...] = total + jnp.dot(large[1], high, preferred_element_type=F32)
-
     near = low_lanes((12, 128))
-    for c in range(4):
+
+    def products(i):
+        for d in range(2):
+            lanes = slice(256 * (2 - i), 256 * (2 - i) + HALF)
+            left = large_strip[0, d, :, lanes], large_strip[1, d, :, lanes]
+            got_large[HALF * d + 256 * i : HALF * d + 256 * i + 256, :] = three(*left, high, low)
+
+    def close(c):
         for y in range(4):
-            for low in range(2):
-                at = 48 * (4 * c + y) + ROWS * low
+            for part_of in range(2):
+                at = 48 * (4 * c + y) + ROWS * part_of
                 for d, (full, part) in enumerate(((0, 24), (48, 36))):
                     minus = got_large[HALF * d + at : HALF * d + at + ROWS, :]
                     place = QUARTER * d + at % QUARTER
@@ -235,13 +239,21 @@
                     two = got_small[1, place : place + ROWS, :]
                     plus = one + two if at < QUARTER else one - two
                     for z, value in ((c, plus + minus), (c + 4, plus - minus)):
-                        out[z, y, low, full : full + 24] = value[:, 0:128]
+                        out[z, y, part_of, full : full + 24] = value[:, 0:128]
                         top, bottom = value[:12, 128:256], value[12:, 128:256]
-                        out[z, y, low, part : part + 12] = jnp.where(
+                        out[z, y, part_of, part : part + 12] = jnp.where(
                             near, top, pltpu.roll(bottom, 64, 1)
                         )
         puts[c].start()
         puts[c + 4].start()
+
+    products(0)
+    products(1)
+    close(0)
+    products(2)
+    close(1)
+    close(2)
+    close(3)
     for put in puts:
         put.wait()
 
@@ -260,7 +272,6 @@
             pltpu.VMEM(small.shape, BF16),
             pltpu.VMEM(large.shape, BF16),
             pltpu.VMEM((2, 2, HALF, QUARTER), BF16),
-            pltpu.VMEM((2, COUNT, HALF), BF16),
             pltpu.VMEM((4, 2, 4, 72, 128), F32),
             pltpu.VMEM((8, 4, 2, 72, 128), F32),
             pltpu.VMEM((2, HALF, 256), F32),

time: 120 us -> 119 us (level)
  no operation moved by 1% of the time
where the time goes in v4:
time: 119 us
  waiting for transfers between devices  70.2 us (59%)
  starting transfers between devices  21.2 us (18%)
  Pallas kernels  20.7 us (17%)
  local copies, waits for them, and re-layouts  5.72 us (5%)
    ppermute x1, waiting for transfers between devices, shards(): far_b = lax.ppermute(own[256:], 'xh', pair)  34.3 us
    ppermute x1, waiting for transfers between devices, shards(): far_a = lax.ppermute(own[:256], 'xh', pair)  19.1 us
    all_to_all x2, starting transfers between devices, swap(): lax.all_to_all(message, ('z', 'y', 'xl'), split_axis=0, concat_axis=0, ti...  18.9 us
    all_to_all x2, waiting for transfers between devices, swap(): lax.all_to_all(message, ('z', 'y', 'xl'), split_axis=0, concat_axis=0, ti...  14.2 us
    pallas_call x1, Pallas kernels, along(): pl.pallas_call(along_kernel, grid_spec=pltpu.PrefetchScalarGridSpec(num_s...  9.99 us
    pallas_call x1, Pallas kernels, cross(): pl.pallas_call(cross_kernel, out_shape=jax.ShapeDtypeStruct((8, 4, 2, 72,...  7 us
    unnamed x10, local copies, waits for them, and re-layouts  5.64 us
  transfers between devices with their start and end apart: 7, of which 6 were waited for; matrix products, arithmetic and copies ran while one was open for 0% of the time, Pallas kernels for 8%

profile of v4, /device:TPU:4, one launch (start us, length us, event | category | flops | bytes accessed | tf_op | source)
XLA Modules:
  0.0 118.7 jit_solution(15614691261993984672)
XLA Ops:
  0.6 2.1 %shard_map.75 = f32[2304,128]{1,0:T(8,128)} custom-call(f32[24,32,384]{2,1,0:T(8,128)} %bitcast.14), custom_call_target="tpu_custom_call" | custom-call | tf_op jit(solution)/shard_map/pallas_call | solution.py:112
  2.8 0.0 copy-start
  2.8 12.9 %all-to-all-start = ((f32[64,9,4,128]{3,2,1,0:T(4,128)}), f32[64,9,4,128]{3,2,1,0:T(4,128)S(1)}, u32[]{:S(2)}, u32[]{:S(2)}) async-start(f32[64,9,4,128]{3,2,1,0:T(4,128)} %bitcast.17), calls=%async_computation | async-start | bytes 2359296 | tf_op jit(solution)/shard_map/all_to_all | solution.py:336
  15.7 0.0 copy-done
  15.7 0.1 collective-permute-start.1
  15.8 0.9 collective-permute-start
  16.7 19.1 %collective-permute-done.far_a = f32[256,384]{1,0:T(8,128)} collective-permute-done((f32[256,384]{1,0:T(8,128)S(1)}, f32[256,384]{1,0:T(8,128)}, u32[]{:S(2)}, u32[]{:S(2)}) %collective-permute-start) | collective-permute-done | bytes 393248 | tf_op jit(solution)/shard_map/ppermute | solution.py:341
  35.8 0.0 collective-permute-done.1.near
  35.8 0.0 copy-start.1
  35.8 1.0 copy-done.1
  36.8 10.5 %all-to-all-done = f32[64,9,4,128]{3,2,1,0:T(4,128)S(1)} async-done(((f32[64,9,4,128]{3,2,1,0:T(4,128)}), f32[64,9,4,128]{3,2,1,0:T(4,128)S(1)}, u32[]{:S(2)}, u32[]{:S(2)}) %all-to-all-start) | async-done | bytes 1179680 | tf_op jit(solution)/shard_map/all_to_all | solution.py:336
  47.3 0.0 copy-start.4
  47.3 1.0 copy-done.4
  48.3 7.0 %shard_map.77 = f32[8,4,2,72,128]{4,3,2,1,0:T(8,128)} custom-call(bf16[2,2,2,128,640]{4,3,2,1,0:T(8,128)(2,1)} %constant.10.clone.small_hbm, bf16[2,2,256,1280]{3,2,1,0:T(8,128)(2,1)} %constant.11.clone.large_hbm, f32[2,4,4,72,128]{4,3,2,1,0:T(8,128)} %bitcast.19), custom_call_target="tpu_custom_call" | custom-call | flops 2717908992 | bytes 12582912 | tf_op jit(solution)/shard_map/pallas_call | solution.py:262
  55.3 6.0 %all-to-all-start.1 = ((f32[64,72,128]{2,1,0:T(8,128)}), f32[64,72,128]{2,1,0:T(8,128)S(1)}, u32[]{:S(2)}, u32[]{:S(2)}) async-start(f32[64,72,128]{2,1,0:T(8,128)} %bitcast.18), calls=%async_computation.1 | async-start | bytes 4718592 | tf_op jit(solution)/shard_map/all_to_all | solution.py:336
  61.3 0.1 slice.14
  61.3 0.9 collective-permute-start.2
  62.2 34.3 %collective-permute-done.2.far_b = f32[512,384]{1,0:T(8,128)} collective-permute-done((f32[512,384]{1,0:T(8,128)S(1)}, f32[512,384]{1,0:T(8,128)}, u32[]{:S(2)}, u32[]{:S(2)}) %collective-permute-start.2) | collective-permute-done | bytes 786464 | tf_op jit(solution)/shard_map/ppermute | solution.py:345
  96.5 0.0 collective-permute-start.4
  96.5 0.5 collective-permute-start.3
  97.0 2.1 %collective-permute-done.4.far_near_b = f32[512,384]{1,0:T(8,128)} collective-permute-done((f32[512,384]{1,0:T(8,128)}, f32[512,384]{1,0:T(8,128)}, u32[]{:S(2)}, u32[]{:S(2)}) %collective-permute-start.4) | collective-permute-done | bytes 786464 | tf_op jit(solution)/shard_map/ppermute | solution.py:348
  99.1 0.6 collective-permute-done.3.far_near_a
  99.7 0.0 copy-start.2
  99.7 1.3 %copy-done.2 = f32[768,384]{1,0:T(8,128)S(1)} copy-done((f32[768,384]{1,0:T(8,128)S(1)}, f32[768,384]{1,0:T(8,128)}, u32[]{:S(2)}) %copy-start.2) | copy-done | bytes 1179672
  100.9 0.0 copy-start.3
  100.9 2.3 %copy-done.3 = bf16[2,4,384,768]{3,2,1,0:T(8,128)(2,1)S(1)} copy-done((bf16[2,4,384,768]{3,2,1,0:T(8,128)(2,1)S(1)}, bf16[2,4,384,768]{3,2,1,0:T(8,128)(2,1)}, u32[]{:S(2)}) %copy-start.3) | copy-done | bytes 4718616
  103.3 10.0 %shard_map.76 = (f32[768,384]{1,0:T(8,128)}, f32[768,384]{1,0:T(8,128)}) custom-call(s32[1]{0:T(128)} %bitcast.core_ref, bf16[2,4,384,768]{3,2,1,0:T(8,128)(2,1)S(1)} %copy-done.3, f32[768,384]{1,0:T(8,128)S(1)} %bitcast.16, f32[768,384]{1,0:T(8,128)S(1)} %copy-done.2, f32[256,384]{1,0:T(8,128)} %collective-permute-done.far_a, ...), custom_call_target="tpu_custom_call" | custom-call | flops 5435817984 | bytes 16777216 | tf_op jit(solution)/shard_map/pallas_call | solution.py:312
  113.3 3.8 %all-to-all-done.1 = f32[64,72,128]{2,1,0:T(8,128)S(1)} async-done(((f32[64,72,128]{2,1,0:T(8,128)}), f32[64,72,128]{2,1,0:T(8,128)S(1)}, u32[]{:S(2)}, u32[]{:S(2)}) %all-to-all-start.1) | async-done | bytes 2359328 | tf_op jit(solution)/shard_map/all_to_all | solution.py:336
  117.0 1.6 %shard_map.78 = (f32[24,32,384]{2,1,0:T(8,128)}, f32[24,32,384]{2,1,0:T(8,128)}) custom-call(f32[4608,128]{1,0:T(8,128)S(1)} %bitcast.13), custom_call_target="tpu_custom_call" | custom-call | tf_op jit(solution)/shard_map/pallas_call | solution.py:155
  (1 shorter events, 0.0 us)
Async XLA Ops:
  2.8 12.9 %copy-start = (f32[24,2,16,384]{3,2,1,0:T(8,128)S(1)}, f32[24,2,16,384]{3,2,1,0:T(8,128)}, u32[]{:S(2)}) copy-start(f32[24,2,16,384]{3,2,1,0:T(8,128)} %param.4) | copy-start | bytes 3538948
  2.8 44.5 %all-to-all-start = ((f32[64,9,4,128]{3,2,1,0:T(4,128)}), f32[64,9,4,128]{3,2,1,0:T(4,128)S(1)}, u32[]{:S(2)}, u32[]{:S(2)}) async-start(f32[64,9,4,128]{3,2,1,0:T(4,128)} %bitcast.17), calls=%async_computation | async-start | bytes 2359296 | tf_op jit(solution)/shard_map/all_to_all | solution.py:336
  15.7 20.1 %collective-permute-start.1 = (f32[768,384]{1,0:T(8,128)S(1)}, f32[768,384]{1,0:T(8,128)S(1)}, u32[]{:S(2)}, u32[]{:S(2)}) collective-permute-start(f32[768,384]{1,0:T(8,128)S(1)} %bitcast.15), channel_id=1, source_target_pairs={{0,1},{1,0},{2,3},{3,2},{4,5},{5,4},{6,7},{7,6},{8,9},{9,8},{10,11... | collective-permute-start | bytes 3538952 | tf_op jit(solution)/shard_map/ppermute | solution.py:342
  15.8 20.0 %collective-permute-start = (f32[256,384]{1,0:T(8,128)S(1)}, f32[256,384]{1,0:T(8,128)}, u32[]{:S(2)}, u32[]{:S(2)}) collective-permute-start(f32[256,384]{1,0:T(8,128)S(1)} %bitcast.21), channel_id=1, source_target_pairs={{0,2},{2,0},{1,3},{3,1},{4,6},{6,4},{5,7},{7,5},{8,10},{10,8},{9,1... | collective-permute-start | bytes 1179656 | tf_op jit(solution)/shard_map/ppermute | solution.py:341
  35.8 1.0 copy-start.1
  47.3 1.0 copy-start.4
  55.3 61.7 %all-to-all-start.1 = ((f32[64,72,128]{2,1,0:T(8,128)}), f32[64,72,128]{2,1,0:T(8,128)S(1)}, u32[]{:S(2)}, u32[]{:S(2)}) async-start(f32[64,72,128]{2,1,0:T(8,128)} %bitcast.18), calls=%async_computation.1 | async-start | bytes 4718592 | tf_op jit(solution)/shard_map/all_to_all | solution.py:336
  61.3 35.1 %collective-permute-start.2 = (f32[512,384]{1,0:T(8,128)S(1)}, f32[512,384]{1,0:T(8,128)}, u32[]{:S(2)}, u32[]{:S(2)}) collective-permute-start(f32[512,384]{1,0:T(8,128)S(1)} %bitcast.20), channel_id=1, source_target_pairs={{0,2},{2,0},{1,3},{3,1},{4,6},{6,4},{5,7},{7,5},{8,10},{10,8},{9,1... | collective-permute-start | bytes 2359304 | tf_op jit(solution)/shard_map/ppermute | solution.py:345
  96.5 2.6 %collective-permute-start.4 = (f32[512,384]{1,0:T(8,128)}, f32[512,384]{1,0:T(8,128)}, u32[]{:S(2)}, u32[]{:S(2)}) collective-permute-start(f32[512,384]{1,0:T(8,128)} %collective-permute-done.2.far_b), channel_id=1, source_target_pairs={{0,1},{1,0},{2,3},{3,2},{4,5},{5,4},{6,7},{7,6},{8,9},{9,8},{10,11... | collective-permute-start | bytes 2359304 | tf_op jit(solution)/shard_map/ppermute | solution.py:348
  96.5 3.2 %collective-permute-start.3 = (f32[256,384]{1,0:T(8,128)}, f32[256,384]{1,0:T(8,128)}, u32[]{:S(2)}, u32[]{:S(2)}) collective-permute-start(f32[256,384]{1,0:T(8,128)} %collective-permute-done.far_a), channel_id=1, source_target_pairs={{0,1},{1,0},{2,3},{3,2},{4,5},{5,4},{6,7},{7,6},{8,9},{9,8},{10,11... | collective-permute-start | bytes 1179656 | tf_op jit(solution)/shard_map/ppermute | solution.py:347
  99.7 1.3 %copy-start.2 = (f32[768,384]{1,0:T(8,128)S(1)}, f32[768,384]{1,0:T(8,128)}, u32[]{:S(2)}) copy-start(f32[768,384]{1,0:T(8,128)} %copy-done.1) | copy-start | bytes 3538948
  100.9 2.3 %copy-start.3 = (bf16[2,4,384,768]{3,2,1,0:T(8,128)(2,1)S(1)}, bf16[2,4,384,768]{3,2,1,0:T(8,128)(2,1)}, u32[]{:S(2)}) copy-start(bf16[2,4,384,768]{3,2,1,0:T(8,128)(2,1)} %constant.12.clone.table_ref) | copy-start | bytes 14155780

commit v5 on v4

--- a/solution.py
+++ b/solution.py
@@ -166,38 +166,33 @@
 
 
 def cross_kernel(
+    token,
     small_hbm,
     large_hbm,
-    msg_hbm,
+    msg,
     out_hbm,
     small_strip,
     large_strip,
     small,
-    msg,
     out,
     line,
     got_small,
     got_large,
-    in_sems,
     table_sems,
     out_sems,
 ):
-    gets = [
-        pltpu.make_async_copy(msg_hbm.at[:, c], msg.at[c], in_sems.at[c]) for c in range(4)
-    ]
     strips = [
         pltpu.make_async_copy(small_hbm, small_strip, table_sems.at[0]),
         pltpu.make_async_copy(large_hbm, large_strip, table_sems.at[1]),
     ]
     puts = [pltpu.make_async_copy(out.at[z], out_hbm.at[z], out_sems.at[z]) for z in range(8)]
-    for copy in gets + strips:
+    for copy in strips:
         copy.start()
 
     for c in range(4):
-        gets[c].wait()
         for y in range(4):
             at = 48 * (4 * c + y)
-            top, bottom = msg[c, 0, y], msg[c, 1, y]
+            top, bottom = msg[0, c, y], msg[1, c, y]
             for k, value in enumerate((top + bottom, top - bottom)):
                 line[k, at : at + 24, 0:128] = value[0:24]
                 line[k, at + 24 : at + 48, 0:128] = value[36:60]
@@ -258,34 +253,33 @@
         put.wait()
 
 
-def cross(small, large, message):
+def cross(token, small, large, message):
     return pl.pallas_call(
         cross_kernel,
         out_shape=jax.ShapeDtypeStruct((8, 4, 2, 72, 128), F32),
         in_specs=[
+            pl.BlockSpec(memory_space=pltpu.SMEM),
             pl.BlockSpec(memory_space=pltpu.HBM),
             pl.BlockSpec(memory_space=pltpu.HBM),
-            pl.BlockSpec(memory_space=pl.ANY),
+            pl.BlockSpec(memory_space=pltpu.VMEM),
         ],
         out_specs=pl.BlockSpec(memory_space=pltpu.HBM),
         scratch_shapes=[
             pltpu.VMEM(small.shape, BF16),
             pltpu.VMEM(large.shape, BF16),
             pltpu.VMEM((2, 2, HALF, QUARTER), BF16),
-            pltpu.VMEM((4, 2, 4, 72, 128), F32),
             pltpu.VMEM((8, 4, 2, 72, 128), F32),
             pltpu.VMEM((2, HALF, 256), F32),
             pltpu.VMEM((2, HALF, 256), F32),
             pltpu.VMEM((COUNT, 256), F32),
-            pltpu.SemaphoreType.DMA((4,)),
             pltpu.SemaphoreType.DMA((2,)),
             pltpu.SemaphoreType.DMA((8,)),
         ],
-        compiler_params=pltpu.CompilerParams(vmem_limit_bytes=60 * 2**20),
+        compiler_params=pltpu.CompilerParams(vmem_limit_bytes=56 * 2**20),
         cost_estimate=pl.CostEstimate(
             flops=3 * 2 * 3 * HALF * HALF * 256, bytes_accessed=12 * 2**20, transcendentals=0
         ),
-    )(small, large, message.reshape(2, 4, 4, 72, 128))
+    )(token, small, large, message.reshape(2, 4, 4, 72, 128))
 
 
 def along_kernel(
@@ -341,9 +335,11 @@
         far_a = lax.ppermute(own[:256], "xh", pair)
         near = lax.ppermute(own, "c", pair)
         home = swap(pack(moments.reshape(ROWS, PLANES, LANES)).reshape(64, 9, 4, 128))
-        home, far_a, near = lax.optimization_barrier((home, far_a, near))
+        token = jnp.zeros((1,), jnp.int32)
+        token, far_a, near = lax.optimization_barrier((token, far_a, near))
         far_b = lax.ppermute(own[256:], "xh", pair)
-        back = swap(cross(jnp.asarray(small_t), jnp.asarray(large_t), home).reshape(64, 72, 128))
+        results = cross(token, jnp.asarray(small_t), jnp.asarray(large_t), home)
+        back = swap(results.reshape(64, 72, 128))
         far_near_a = lax.ppermute(far_a, "c", pair)
         far_near_b = lax.ppermute(far_b, "c", pair)
         core = lax.axis_index("c").reshape(1)

time: 119 us -> 120 us (level)
  no operation moved by 1% of the time
where the time goes in v5:
time: 120 us
  waiting for transfers between devices  70.2 us (58%)
  Pallas kernels  21.6 us (18%)
  starting transfers between devices  21.2 us (18%)
  local copies, waits for them, and re-layouts  5.72 us (5%)
    ppermute x1, waiting for transfers between devices, shards(): far_b = lax.ppermute(own[256:], 'xh', pair)  34.3 us
    ppermute x1, waiting for transfers between devices, shards(): far_a = lax.ppermute(own[:256], 'xh', pair)  19.1 us
    all_to_all x2, starting transfers between devices, swap(): lax.all_to_all(message, ('z', 'y', 'xl'), split_axis=0, concat_axis=0, ti...  18.9 us
    all_to_all x2, waiting for transfers between devices, swap(): lax.all_to_all(message, ('z', 'y', 'xl'), split_axis=0, concat_axis=0, ti...  14.2 us
    pallas_call x1, Pallas kernels, along(): pl.pallas_call(along_kernel, grid_spec=pltpu.PrefetchScalarGridSpec(num_s...  9.99 us
    pallas_call x1, Pallas kernels, cross(): pl.pallas_call(cross_kernel, out_shape=jax.ShapeDtypeStruct((8, 4, 2, 72,...  7.86 us
    unnamed x10, local copies, waits for them, and re-layouts  5.64 us
  transfers between devices with their start and end apart: 7, of which 6 were waited for; matrix products, arithmetic and copies ran while one was open for 0% of the time, Pallas kernels for 8%

profile of v5, /device:TPU:4, one launch (start us, length us, event | category | flops | bytes accessed | tf_op | source)
XLA Modules:
  0.0 119.5 jit_solution(17827717166273927086)
XLA Ops:
  0.6 2.1 %shard_map.76 = f32[2304,128]{1,0:T(8,128)} custom-call(f32[24,32,384]{2,1,0:T(8,128)} %bitcast.14), custom_call_target="tpu_custom_call" | custom-call | tf_op jit(solution)/shard_map/pallas_call | solution.py:112
  2.8 0.0 copy-start
  2.8 12.9 %all-to-all-start = ((f32[64,9,4,128]{3,2,1,0:T(4,128)}), f32[64,9,4,128]{3,2,1,0:T(4,128)S(1)}, u32[]{:S(2)}, u32[]{:S(2)}) async-start(f32[64,9,4,128]{3,2,1,0:T(4,128)} %bitcast.17), calls=%async_computation | async-start | bytes 2359296 | tf_op jit(solution)/shard_map/all_to_all | solution.py:330
  15.7 0.0 copy-done
  15.7 0.1 collective-permute-start.1
  15.8 0.9 collective-permute-start
  16.7 19.1 %collective-permute-done.far_a = f32[256,384]{1,0:T(8,128)} collective-permute-done((f32[256,384]{1,0:T(8,128)S(1)}, f32[256,384]{1,0:T(8,128)}, u32[]{:S(2)}, u32[]{:S(2)}) %collective-permute-start) | collective-permute-done | bytes 393248 | tf_op jit(solution)/shard_map/ppermute | solution.py:335
  35.8 0.0 collective-permute-done.1.near
  35.8 0.0 copy-start.1
  35.8 1.0 copy-done.1
  36.8 10.5 %all-to-all-done = f32[64,9,4,128]{3,2,1,0:T(4,128)S(1)} async-done(((f32[64,9,4,128]{3,2,1,0:T(4,128)}), f32[64,9,4,128]{3,2,1,0:T(4,128)S(1)}, u32[]{:S(2)}, u32[]{:S(2)}) %all-to-all-start) | async-done | bytes 1179680 | tf_op jit(solution)/shard_map/all_to_all | solution.py:330
  47.3 0.0 copy-start.4
  47.3 1.0 copy-done.4
  48.3 7.9 %shard_map.77 = f32[8,4,2,72,128]{4,3,2,1,0:T(8,128)} custom-call(s32[1]{0:T(128)} %constant.4.clone.1.token, bf16[2,2,2,128,640]{4,3,2,1,0:T(8,128)(2,1)} %constant.12.clone.small_hbm, bf16[2,2,256,1280]{3,2,1,0:T(8,128)(2,1)} %constant.13.clone.large_hbm, f32[2,4,4,72,128]{4,3,2,1,0:T(8,128)} %bitcast.19), custom_call_target="tpu_custom_call" | custom-call | flops 2717908992 | bytes 12582912 | tf_op jit(solution)/shard_map/pallas_call | solution.py:257
  56.1 6.0 %all-to-all-start.1 = ((f32[64,72,128]{2,1,0:T(8,128)}), f32[64,72,128]{2,1,0:T(8,128)S(1)}, u32[]{:S(2)}, u32[]{:S(2)}) async-start(f32[64,72,128]{2,1,0:T(8,128)} %bitcast.18), calls=%async_computation.1 | async-start | bytes 4718592 | tf_op jit(solution)/shard_map/all_to_all | solution.py:330
  62.1 0.1 slice.14
  62.2 0.9 collective-permute-start.2
  63.1 34.3 %collective-permute-done.2.far_b = f32[512,384]{1,0:T(8,128)} collective-permute-done((f32[512,384]{1,0:T(8,128)S(1)}, f32[512,384]{1,0:T(8,128)}, u32[]{:S(2)}, u32[]{:S(2)}) %collective-permute-start.2) | collective-permute-done | bytes 786464 | tf_op jit(solution)/shard_map/ppermute | solution.py:340
  97.3 0.0 collective-permute-start.4
  97.3 0.5 collective-permute-start.3
  97.8 2.1 %collective-permute-done.4.far_near_b = f32[512,384]{1,0:T(8,128)} collective-permute-done((f32[512,384]{1,0:T(8,128)}, f32[512,384]{1,0:T(8,128)}, u32[]{:S(2)}, u32[]{:S(2)}) %collective-permute-start.4) | collective-permute-done | bytes 786464 | tf_op jit(solution)/shard_map/ppermute | solution.py:344
  100.0 0.6 collective-permute-done.3.far_near_a
  100.5 0.0 copy-start.2
  100.5 1.3 %copy-done.2 = f32[768,384]{1,0:T(8,128)S(1)} copy-done((f32[768,384]{1,0:T(8,128)S(1)}, f32[768,384]{1,0:T(8,128)}, u32[]{:S(2)}) %copy-start.2) | copy-done | bytes 1179672
  101.8 0.0 copy-start.3
  101.8 2.3 %copy-done.3 = bf16[2,4,384,768]{3,2,1,0:T(8,128)(2,1)S(1)} copy-done((bf16[2,4,384,768]{3,2,1,0:T(8,128)(2,1)S(1)}, bf16[2,4,384,768]{3,2,1,0:T(8,128)(2,1)}, u32[]{:S(2)}) %copy-start.3) | copy-done | bytes 4718616
  104.1 10.0 %shard_map.75 = (f32[768,384]{1,0:T(8,128)}, f32[768,384]{1,0:T(8,128)}) custom-call(s32[1]{0:T(128)} %bitcast.core_ref, bf16[2,4,384,768]{3,2,1,0:T(8,128)(2,1)S(1)} %copy-done.3, f32[768,384]{1,0:T(8,128)S(1)} %bitcast.16, f32[768,384]{1,0:T(8,128)S(1)} %copy-done.2, f32[256,384]{1,0:T(8,128)} %collective-permute-done.far_a, ...), custom_call_target="tpu_custom_call" | custom-call | flops 5435817984 | bytes 16777216 | tf_op jit(solution)/shard_map/pallas_call | solution.py:306
  114.1 3.8 %all-to-all-done.1 = f32[64,72,128]{2,1,0:T(8,128)S(1)} async-done(((f32[64,72,128]{2,1,0:T(8,128)}), f32[64,72,128]{2,1,0:T(8,128)S(1)}, u32[]{:S(2)}, u32[]{:S(2)}) %all-to-all-start.1) | async-done | bytes 2359328 | tf_op jit(solution)/shard_map/all_to_all | solution.py:330
  117.9 1.6 %shard_map.78 = (f32[24,32,384]{2,1,0:T(8,128)}, f32[24,32,384]{2,1,0:T(8,128)}) custom-call(f32[4608,128]{1,0:T(8,128)S(1)} %bitcast.13), custom_call_target="tpu_custom_call" | custom-call | tf_op jit(solution)/shard_map/pallas_call | solution.py:155
  (1 shorter events, 0.0 us)
Async XLA Ops:
  2.8 12.9 %copy-start = (f32[24,2,16,384]{3,2,1,0:T(8,128)S(1)}, f32[24,2,16,384]{3,2,1,0:T(8,128)}, u32[]{:S(2)}) copy-start(f32[24,2,16,384]{3,2,1,0:T(8,128)} %param.4) | copy-start | bytes 3538948
  2.8 44.5 %all-to-all-start = ((f32[64,9,4,128]{3,2,1,0:T(4,128)}), f32[64,9,4,128]{3,2,1,0:T(4,128)S(1)}, u32[]{:S(2)}, u32[]{:S(2)}) async-start(f32[64,9,4,128]{3,2,1,0:T(4,128)} %bitcast.17), calls=%async_computation | async-start | bytes 2359296 | tf_op jit(solution)/shard_map/all_to_all | solution.py:330
  15.7 20.1 %collective-permute-start.1 = (f32[768,384]{1,0:T(8,128)S(1)}, f32[768,384]{1,0:T(8,128)S(1)}, u32[]{:S(2)}, u32[]{:S(2)}) collective-permute-start(f32[768,384]{1,0:T(8,128)S(1)} %bitcast.15), channel_id=1, source_target_pairs={{0,1},{1,0},{2,3},{3,2},{4,5},{5,4},{6,7},{7,6},{8,9},{9,8},{10,11... | collective-permute-start | bytes 3538952 | tf_op jit(solution)/shard_map/ppermute | solution.py:336
  15.8 20.0 %collective-permute-start = (f32[256,384]{1,0:T(8,128)S(1)}, f32[256,384]{1,0:T(8,128)}, u32[]{:S(2)}, u32[]{:S(2)}) collective-permute-start(f32[256,384]{1,0:T(8,128)S(1)} %bitcast.21), channel_id=1, source_target_pairs={{0,2},{2,0},{1,3},{3,1},{4,6},{6,4},{5,7},{7,5},{8,10},{10,8},{9,1... | collective-permute-start | bytes 1179656 | tf_op jit(solution)/shard_map/ppermute | solution.py:335
  35.8 1.0 copy-start.1
  47.3 1.0 copy-start.4
  56.1 61.7 %all-to-all-start.1 = ((f32[64,72,128]{2,1,0:T(8,128)}), f32[64,72,128]{2,1,0:T(8,128)S(1)}, u32[]{:S(2)}, u32[]{:S(2)}) async-start(f32[64,72,128]{2,1,0:T(8,128)} %bitcast.18), calls=%async_computation.1 | async-start | bytes 4718592 | tf_op jit(solution)/shard_map/all_to_all | solution.py:330
  62.2 35.1 %collective-permute-start.2 = (f32[512,384]{1,0:T(8,128)S(1)}, f32[512,384]{1,0:T(8,128)}, u32[]{:S(2)}, u32[]{:S(2)}) collective-permute-start(f32[512,384]{1,0:T(8,128)S(1)} %bitcast.20), channel_id=1, source_target_pairs={{0,2},{2,0},{1,3},{3,1},{4,6},{6,4},{5,7},{7,5},{8,10},{10,8},{9,1... | collective-permute-start | bytes 2359304 | tf_op jit(solution)/shard_map/ppermute | solution.py:340
  97.3 2.6 %collective-permute-start.4 = (f32[512,384]{1,0:T(8,128)}, f32[512,384]{1,0:T(8,128)}, u32[]{:S(2)}, u32[]{:S(2)}) collective-permute-start(f32[512,384]{1,0:T(8,128)} %collective-permute-done.2.far_b), channel_id=1, source_target_pairs={{0,1},{1,0},{2,3},{3,2},{4,5},{5,4},{6,7},{7,6},{8,9},{9,8},{10,11... | collective-permute-start | bytes 2359304 | tf_op jit(solution)/shard_map/ppermute | solution.py:344
  97.3 3.2 %collective-permute-start.3 = (f32[256,384]{1,0:T(8,128)}, f32[256,384]{1,0:T(8,128)}, u32[]{:S(2)}, u32[]{:S(2)}) collective-permute-start(f32[256,384]{1,0:T(8,128)} %collective-permute-done.far_a), channel_id=1, source_target_pairs={{0,1},{1,0},{2,3},{3,2},{4,5},{5,4},{6,7},{7,6},{8,9},{9,8},{10,11... | collective-permute-start | bytes 1179656 | tf_op jit(solution)/shard_map/ppermute | solution.py:343
  100.5 1.3 %copy-start.2 = (f32[768,384]{1,0:T(8,128)S(1)}, f32[768,384]{1,0:T(8,128)}, u32[]{:S(2)}) copy-start(f32[768,384]{1,0:T(8,128)} %copy-done.1) | copy-start | bytes 3538948
  101.8 2.3 %copy-start.3 = (bf16[2,4,384,768]{3,2,1,0:T(8,128)(2,1)S(1)}, bf16[2,4,384,768]{3,2,1,0:T(8,128)(2,1)}, u32[]{:S(2)}) copy-start(bf16[2,4,384,768]{3,2,1,0:T(8,128)(2,1)} %constant.14.clone.table_ref) | copy-start | bytes 14155780

commit v6 on v4

--- a/solution.py
+++ b/solution.py
@@ -81,18 +81,33 @@
 
 def pack_kernel(x_hbm, msg_hbm, x_ref, msg_ref, in_sems, out_sems):
     gets = [
-        pltpu.make_async_copy(x_hbm.at[:, 8 * g : 8 * g + 8], x_ref.at[g], in_sems.at[g])
+        [
+            pltpu.make_async_copy(
+                x_hbm.at[12 * part : 12 * part + 12, 8 * g : 8 * g + 8],
+                x_ref.at[g, 12 * part : 12 * part + 12],
+                in_sems.at[2 * g + part],
+            )
+            for part in range(2)
+        ]
         for g in range(4)
     ]
     puts = [
-        pltpu.make_async_copy(msg_ref.at[g], msg_hbm.at[576 * g : 576 * g + 576], out_sems.at[g])
+        [
+            pltpu.make_async_copy(
+                msg_ref.at[g, 288 * part : 288 * part + 288],
+                msg_hbm.at[576 * g + 288 * part : 576 * g + 288 * part + 288],
+                out_sems.at[2 * g + part],
+            )
+            for part in range(2)
+        ]
         for g in range(4)
     ]
     near = low_lanes((8, 128))
-    for get in gets:
+    for get in sum(gets, []):
         get.start()
     for g in range(4):
-        gets[g].wait()
+        for get in gets[g]:
+            get.wait()
         for i in range(ROWS):
             for low in range(2):
                 at = pl.ds(36 * low + i, 8, stride=72)
@@ -103,8 +118,9 @@
             upper = jnp.where(near, pltpu.roll(top, 64, 1), bottom)
             msg_ref[g, pl.ds(24 + i, 8, stride=72), :] = lower
             msg_ref[g, pl.ds(60 + i, 8, stride=72), :] = upper
-        puts[g].start()
-    for put in puts:
+        for put in puts[g]:
+            put.start()
+    for put in sum(puts, []):
         put.wait()
 
 
@@ -117,8 +133,8 @@
         scratch_shapes=[
             pltpu.VMEM((4, ROWS, 8, LANES), F32),
             pltpu.VMEM((4, 576, 128), F32),
-            pltpu.SemaphoreType.DMA((4,)),
-            pltpu.SemaphoreType.DMA((4,)),
+            pltpu.SemaphoreType.DMA((8,)),
+            pltpu.SemaphoreType.DMA((8,)),
         ],
         compiler_params=pltpu.CompilerParams(vmem_limit_bytes=56 * 2**20),
     )(block)
@@ -183,18 +199,33 @@
     out_sems,
 ):
     gets = [
-        pltpu.make_async_copy(msg_hbm.at[:, c], msg.at[c], in_sems.at[c]) for c in range(4)
-    ]
-    strips = [
-        pltpu.make_async_copy(small_hbm, small_strip, table_sems.at[0]),
-        pltpu.make_async_copy(large_hbm, large_strip, table_sems.at[1]),
+        [
+            pltpu.make_async_copy(msg_hbm.at[side, c], msg.at[c, side], in_sems.at[2 * c + side])
+            for side in range(2)
+        ]
+        for c in range(4)
+    ]
+    small_loads = [
+        pltpu.make_async_copy(
+            small_hbm.at[k, h], small_strip.at[k, h], table_sems.at[2 * k + h]
+        )
+        for k in range(2)
+        for h in range(2)
+    ]
+    large_loads = [
+        pltpu.make_async_copy(
+            large_hbm.at[h, d], large_strip.at[h, d], table_sems.at[4 + 2 * h + d]
+        )
+        for h in range(2)
+        for d in range(2)
     ]
     puts = [pltpu.make_async_copy(out.at[z], out_hbm.at[z], out_sems.at[z]) for z in range(8)]
-    for copy in gets + strips:
+    for copy in sum(gets, []) + small_loads + large_loads:
         copy.start()
 
     for c in range(4):
-        gets[c].wait()
+        for get in gets[c]:
+            get.wait()
         for y in range(4):
             at = 48 * (4 * c + y)
             top, bottom = msg[c, 0, y], msg[c, 1, y]
@@ -205,7 +236,7 @@
                 parts = [even, pltpu.roll(even, 64, 1), odd, pltpu.roll(odd, 64, 1)]
                 line[k, at : at + 48, 128:256] = jnp.concatenate(parts, axis=0)
 
-    for copy in strips:
+    for copy in small_loads:
         copy.wait()
     for h in range(2):
         for d in range(2):
@@ -220,6 +251,8 @@
         got_small[k] = three(small[k, 0], small[k, 1], high, low)
 
     high, low = split(line[1])
+    for copy in large_loads:
+        copy.wait()
     near = low_lanes((12, 128))
 
     def products(i):
@@ -277,8 +310,8 @@
             pltpu.VMEM((2, HALF, 256), F32),
             pltpu.VMEM((2, HALF, 256), F32),
             pltpu.VMEM((COUNT, 256), F32),
-            pltpu.SemaphoreType.DMA((4,)),
-            pltpu.SemaphoreType.DMA((2,)),
+            pltpu.SemaphoreType.DMA((8,)),
+            pltpu.SemaphoreType.DMA((8,)),
             pltpu.SemaphoreType.DMA((8,)),
         ],
         compiler_params=pltpu.CompilerParams(vmem_limit_bytes=60 * 2**20),

time: 119 us -> 119 us (level)
  no operation moved by 1% of the time
where the time goes in v6:
time: 119 us
  waiting for transfers between devices  70.2 us (59%)
  starting transfers between devices  21.2 us (18%)
  Pallas kernels  21.1 us (18%)
  local copies, waits for them, and re-layouts  5.72 us (5%)
    ppermute x1, waiting for transfers between devices, shards(): far_b = lax.ppermute(own[256:], 'xh', pair)  34.3 us
    ppermute x1, waiting for transfers between devices, shards(): far_a = lax.ppermute(own[:256], 'xh', pair)  19.1 us
    all_to_all x2, starting transfers between devices, swap(): lax.all_to_all(message, ('z', 'y', 'xl'), split_axis=0, concat_axis=0, ti...  18.9 us
    all_to_all x2, waiting for transfers between devices, swap(): lax.all_to_all(message, ('z', 'y', 'xl'), split_axis=0, concat_axis=0, ti...  14.2 us
    pallas_call x1, Pallas kernels, along(): pl.pallas_call(along_kernel, grid_spec=pltpu.PrefetchScalarGridSpec(num_s...  9.99 us
    pallas_call x1, Pallas kernels, cross(): pl.pallas_call(cross_kernel, out_shape=jax.ShapeDtypeStruct((8, 4, 2, 72,...  7.19 us
    unnamed x10, local copies, waits for them, and re-layouts  5.64 us
  transfers between devices with their start and end apart: 7, of which 6 were waited for; matrix products, arithmetic and copies ran while one was open for 0% of the time, Pallas kernels for 8%

profile of v6, /device:TPU:4, one launch (start us, length us, event | category | flops | bytes accessed | tf_op | source)
XLA Modules:
  0.0 119.0 jit_solution(10681269982124744633)
XLA Ops:
  0.6 2.3 %shard_map.75 = f32[2304,128]{1,0:T(8,128)} custom-call(f32[24,32,384]{2,1,0:T(8,128)} %bitcast.14), custom_call_target="tpu_custom_call" | custom-call | tf_op jit(solution)/shard_map/pallas_call | solution.py:128
  2.9 0.0 copy-start
  2.9 12.9 %all-to-all-start = ((f32[64,9,4,128]{3,2,1,0:T(4,128)}), f32[64,9,4,128]{3,2,1,0:T(4,128)S(1)}, u32[]{:S(2)}, u32[]{:S(2)}) async-start(f32[64,9,4,128]{3,2,1,0:T(4,128)} %bitcast.17), calls=%async_computation | async-start | bytes 2359296 | tf_op jit(solution)/shard_map/all_to_all | solution.py:369
  15.8 0.0 copy-done
  15.8 0.1 collective-permute-start.1
  16.0 0.9 collective-permute-start
  16.9 19.1 %collective-permute-done.far_a = f32[256,384]{1,0:T(8,128)} collective-permute-done((f32[256,384]{1,0:T(8,128)S(1)}, f32[256,384]{1,0:T(8,128)}, u32[]{:S(2)}, u32[]{:S(2)}) %collective-permute-start) | collective-permute-done | bytes 393248 | tf_op jit(solution)/shard_map/ppermute | solution.py:374
  35.9 0.0 collective-permute-done.1.near
  35.9 0.0 copy-start.1
  36.0 1.0 copy-done.1
  37.0 10.5 %all-to-all-done = f32[64,9,4,128]{3,2,1,0:T(4,128)S(1)} async-done(((f32[64,9,4,128]{3,2,1,0:T(4,128)}), f32[64,9,4,128]{3,2,1,0:T(4,128)S(1)}, u32[]{:S(2)}, u32[]{:S(2)}) %all-to-all-start) | async-done | bytes 1179680 | tf_op jit(solution)/shard_map/all_to_all | solution.py:369
  47.4 0.0 copy-start.4
  47.4 1.0 copy-done.4
  48.4 7.2 %shard_map.77 = f32[8,4,2,72,128]{4,3,2,1,0:T(8,128)} custom-call(bf16[2,2,2,128,640]{4,3,2,1,0:T(8,128)(2,1)} %constant.10.clone.small_hbm, bf16[2,2,256,1280]{3,2,1,0:T(8,128)(2,1)} %constant.11.clone.large_hbm, f32[2,4,4,72,128]{4,3,2,1,0:T(8,128)} %bitcast.19), custom_call_target="tpu_custom_call" | custom-call | flops 2717908992 | bytes 12582912 | tf_op jit(solution)/shard_map/pallas_call | solution.py:295
  55.6 6.0 %all-to-all-start.1 = ((f32[64,72,128]{2,1,0:T(8,128)}), f32[64,72,128]{2,1,0:T(8,128)S(1)}, u32[]{:S(2)}, u32[]{:S(2)}) async-start(f32[64,72,128]{2,1,0:T(8,128)} %bitcast.18), calls=%async_computation.1 | async-start | bytes 4718592 | tf_op jit(solution)/shard_map/all_to_all | solution.py:369
  61.6 0.1 slice.14
  61.7 0.9 collective-permute-start.2
  62.6 34.3 %collective-permute-done.2.far_b = f32[512,384]{1,0:T(8,128)} collective-permute-done((f32[512,384]{1,0:T(8,128)S(1)}, f32[512,384]{1,0:T(8,128)}, u32[]{:S(2)}, u32[]{:S(2)}) %collective-permute-start.2) | collective-permute-done | bytes 786464 | tf_op jit(solution)/shard_map/ppermute | solution.py:378
  96.8 0.0 collective-permute-start.4
  96.8 0.5 collective-permute-start.3
  97.3 2.1 %collective-permute-done.4.far_near_b = f32[512,384]{1,0:T(8,128)} collective-permute-done((f32[512,384]{1,0:T(8,128)}, f32[512,384]{1,0:T(8,128)}, u32[]{:S(2)}, u32[]{:S(2)}) %collective-permute-start.4) | collective-permute-done | bytes 786464 | tf_op jit(solution)/shard_map/ppermute | solution.py:381
  99.4 0.6 collective-permute-done.3.far_near_a
  100.0 0.0 copy-start.2
  100.0 1.3 %copy-done.2 = f32[768,384]{1,0:T(8,128)S(1)} copy-done((f32[768,384]{1,0:T(8,128)S(1)}, f32[768,384]{1,0:T(8,128)}, u32[]{:S(2)}) %copy-start.2) | copy-done | bytes 1179672
  101.3 0.0 copy-start.3
  101.3 2.3 %copy-done.3 = bf16[2,4,384,768]{3,2,1,0:T(8,128)(2,1)S(1)} copy-done((bf16[2,4,384,768]{3,2,1,0:T(8,128)(2,1)S(1)}, bf16[2,4,384,768]{3,2,1,0:T(8,128)(2,1)}, u32[]{:S(2)}) %copy-start.3) | copy-done | bytes 4718616
  103.6 10.0 %shard_map.76 = (f32[768,384]{1,0:T(8,128)}, f32[768,384]{1,0:T(8,128)}) custom-call(s32[1]{0:T(128)} %bitcast.core_ref, bf16[2,4,384,768]{3,2,1,0:T(8,128)(2,1)S(1)} %copy-done.3, f32[768,384]{1,0:T(8,128)S(1)} %bitcast.16, f32[768,384]{1,0:T(8,128)S(1)} %copy-done.2, f32[256,384]{1,0:T(8,128)} %collective-permute-done.far_a, ...), custom_call_target="tpu_custom_call" | custom-call | flops 5435817984 | bytes 16777216 | tf_op jit(solution)/shard_map/pallas_call | solution.py:345
  113.6 3.8 %all-to-all-done.1 = f32[64,72,128]{2,1,0:T(8,128)S(1)} async-done(((f32[64,72,128]{2,1,0:T(8,128)}), f32[64,72,128]{2,1,0:T(8,128)S(1)}, u32[]{:S(2)}, u32[]{:S(2)}) %all-to-all-start.1) | async-done | bytes 2359328 | tf_op jit(solution)/shard_map/all_to_all | solution.py:369
  117.4 1.6 %shard_map.78 = (f32[24,32,384]{2,1,0:T(8,128)}, f32[24,32,384]{2,1,0:T(8,128)}) custom-call(f32[4608,128]{1,0:T(8,128)S(1)} %bitcast.13), custom_call_target="tpu_custom_call" | custom-call | tf_op jit(solution)/shard_map/pallas_call | solution.py:171
  (1 shorter events, 0.0 us)
Async XLA Ops:
  2.9 12.9 %copy-start = (f32[24,2,16,384]{3,2,1,0:T(8,128)S(1)}, f32[24,2,16,384]{3,2,1,0:T(8,128)}, u32[]{:S(2)}) copy-start(f32[24,2,16,384]{3,2,1,0:T(8,128)} %param.4) | copy-start | bytes 3538948
  2.9 44.5 %all-to-all-start = ((f32[64,9,4,128]{3,2,1,0:T(4,128)}), f32[64,9,4,128]{3,2,1,0:T(4,128)S(1)}, u32[]{:S(2)}, u32[]{:S(2)}) async-start(f32[64,9,4,128]{3,2,1,0:T(4,128)} %bitcast.17), calls=%async_computation | async-start | bytes 2359296 | tf_op jit(solution)/shard_map/all_to_all | solution.py:369
  15.8 20.1 %collective-permute-start.1 = (f32[768,384]{1,0:T(8,128)S(1)}, f32[768,384]{1,0:T(8,128)S(1)}, u32[]{:S(2)}, u32[]{:S(2)}) collective-permute-start(f32[768,384]{1,0:T(8,128)S(1)} %bitcast.15), channel_id=1, source_target_pairs={{0,1},{1,0},{2,3},{3,2},{4,5},{5,4},{6,7},{7,6},{8,9},{9,8},{10,11... | collective-permute-start | bytes 3538952 | tf_op jit(solution)/shard_map/ppermute | solution.py:375
  16.0 20.0 %collective-permute-start = (f32[256,384]{1,0:T(8,128)S(1)}, f32[256,384]{1,0:T(8,128)}, u32[]{:S(2)}, u32[]{:S(2)}) collective-permute-start(f32[256,384]{1,0:T(8,128)S(1)} %bitcast.21), channel_id=1, source_target_pairs={{0,2},{2,0},{1,3},{3,1},{4,6},{6,4},{5,7},{7,5},{8,10},{10,8},{9,1... | collective-permute-start | bytes 1179656 | tf_op jit(solution)/shard_map/ppermute | solution.py:374
  35.9 1.0 copy-start.1
  47.4 1.0 copy-start.4
  55.6 61.7 %all-to-all-start.1 = ((f32[64,72,128]{2,1,0:T(8,128)}), f32[64,72,128]{2,1,0:T(8,128)S(1)}, u32[]{:S(2)}, u32[]{:S(2)}) async-start(f32[64,72,128]{2,1,0:T(8,128)} %bitcast.18), calls=%async_computation.1 | async-start | bytes 4718592 | tf_op jit(solution)/shard_map/all_to_all | solution.py:369
  61.7 35.1 %collective-permute-start.2 = (f32[512,384]{1,0:T(8,128)S(1)}, f32[512,384]{1,0:T(8,128)}, u32[]{:S(2)}, u32[]{:S(2)}) collective-permute-start(f32[512,384]{1,0:T(8,128)S(1)} %bitcast.20), channel_id=1, source_target_pairs={{0,2},{2,0},{1,3},{3,1},{4,6},{6,4},{5,7},{7,5},{8,10},{10,8},{9,1... | collective-permute-start | bytes 2359304 | tf_op jit(solution)/shard_map/ppermute | solution.py:378
  96.8 2.6 %collective-permute-start.4 = (f32[512,384]{1,0:T(8,128)}, f32[512,384]{1,0:T(8,128)}, u32[]{:S(2)}, u32[]{:S(2)}) collective-permute-start(f32[512,384]{1,0:T(8,128)} %collective-permute-done.2.far_b), channel_id=1, source_target_pairs={{0,1},{1,0},{2,3},{3,2},{4,5},{5,4},{6,7},{7,6},{8,9},{9,8},{10,11... | collective-permute-start | bytes 2359304 | tf_op jit(solution)/shard_map/ppermute | solution.py:381
  96.8 3.2 %collective-permute-start.3 = (f32[256,384]{1,0:T(8,128)}, f32[256,384]{1,0:T(8,128)}, u32[]{:S(2)}, u32[]{:S(2)}) collective-permute-start(f32[256,384]{1,0:T(8,128)} %collective-permute-done.far_a), channel_id=1, source_target_pairs={{0,1},{1,0},{2,3},{3,2},{4,5},{5,4},{6,7},{7,6},{8,9},{9,8},{10,11... | collective-permute-start | bytes 1179656 | tf_op jit(solution)/shard_map/ppermute | solution.py:380
  100.0 1.3 %copy-start.2 = (f32[768,384]{1,0:T(8,128)S(1)}, f32[768,384]{1,0:T(8,128)}, u32[]{:S(2)}) copy-start(f32[768,384]{1,0:T(8,128)} %copy-done.1) | copy-start | bytes 3538948
  101.3 2.3 %copy-start.3 = (bf16[2,4,384,768]{3,2,1,0:T(8,128)(2,1)S(1)}, bf16[2,4,384,768]{3,2,1,0:T(8,128)(2,1)}, u32[]{:S(2)}) copy-start(bf16[2,4,384,768]{3,2,1,0:T(8,128)(2,1)} %constant.12.clone.table_ref) | copy-start | bytes 14155780

commit v7 on v4

--- a/solution.py
+++ b/solution.py
@@ -183,13 +183,13 @@
     out_sems,
 ):
     gets = [
-        pltpu.make_async_copy(msg_hbm.at[:, c], msg.at[c], in_sems.at[c]) for c in range(4)
+        pltpu.make_async_copy(msg_hbm.at[:, :, c], msg.at[c], in_sems.at[c]) for c in range(4)
     ]
     strips = [
         pltpu.make_async_copy(small_hbm, small_strip, table_sems.at[0]),
         pltpu.make_async_copy(large_hbm, large_strip, table_sems.at[1]),
     ]
-    puts = [pltpu.make_async_copy(out.at[z], out_hbm.at[z], out_sems.at[z]) for z in range(8)]
+    puts = [pltpu.make_async_copy(out.at[z], out_hbm.at[:, z], out_sems.at[z]) for z in range(8)]
     for copy in gets + strips:
         copy.start()
 
@@ -197,7 +197,7 @@
         gets[c].wait()
         for y in range(4):
             at = 48 * (4 * c + y)
-            top, bottom = msg[c, 0, y], msg[c, 1, y]
+            top, bottom = msg[c, y, 0], msg[c, y, 1]
             for k, value in enumerate((top + bottom, top - bottom)):
                 line[k, at : at + 24, 0:128] = value[0:24]
                 line[k, at + 24 : at + 48, 0:128] = value[36:60]
@@ -261,7 +261,7 @@
 def cross(small, large, message):
     return pl.pallas_call(
         cross_kernel,
-        out_shape=jax.ShapeDtypeStruct((8, 4, 2, 72, 128), F32),
+        out_shape=jax.ShapeDtypeStruct((4, 8, 2, 72, 128), F32),
         in_specs=[
             pl.BlockSpec(memory_space=pltpu.HBM),
             pl.BlockSpec(memory_space=pltpu.HBM),
@@ -272,7 +272,7 @@
             pltpu.VMEM(small.shape, BF16),
             pltpu.VMEM(large.shape, BF16),
             pltpu.VMEM((2, 2, HALF, QUARTER), BF16),
-            pltpu.VMEM((4, 2, 4, 72, 128), F32),
+            pltpu.VMEM((4, 4, 2, 72, 128), F32),
             pltpu.VMEM((8, 4, 2, 72, 128), F32),
             pltpu.VMEM((2, HALF, 256), F32),
             pltpu.VMEM((2, HALF, 256), F32),
@@ -285,7 +285,7 @@
         cost_estimate=pl.CostEstimate(
             flops=3 * 2 * 3 * HALF * HALF * 256, bytes_accessed=12 * 2**20, transcendentals=0
         ),
-    )(small, large, message.reshape(2, 4, 4, 72, 128))
+    )(small, large, message.reshape(4, 2, 4, 72, 128))
 
 
 def along_kernel(
@@ -333,7 +333,7 @@
     pair = [(0, 1), (1, 0)]
 
     def swap(message):
-        return lax.all_to_all(message, ("z", "y", "xl"), split_axis=0, concat_axis=0, tiled=True)
+        return lax.all_to_all(message, ("y", "z", "xl"), split_axis=0, concat_axis=0, tiled=True)
 
     def shards(moments):
         grid = moments.shape

time: 119 us -> 120 us (level)
    all_to_all x2, waiting for transfers between devices: 14.2 us -> 15.6 us  [swap(): lax.all_to_all(message, ('y', 'z', 'xl'), split_axis=0, concat_axis=0, ti...]
where the time goes in v7:
time: 120 us
  waiting for transfers between devices  71.1 us (59%)
  starting transfers between devices  21.2 us (18%)
  Pallas kernels  20.8 us (17%)
  local copies, waits for them, and re-layouts  5.72 us (5%)
    ppermute x1, waiting for transfers between devices, shards(): far_b = lax.ppermute(own[256:], 'xh', pair)  33.9 us
    ppermute x1, waiting for transfers between devices, shards(): far_a = lax.ppermute(own[:256], 'xh', pair)  18.9 us
    all_to_all x2, starting transfers between devices, swap(): lax.all_to_all(message, ('y', 'z', 'xl'), split_axis=0, concat_axis=0, ti...  18.9 us
    all_to_all x2, waiting for transfers between devices, swap(): lax.all_to_all(message, ('y', 'z', 'xl'), split_axis=0, concat_axis=0, ti...  15.6 us
    pallas_call x1, Pallas kernels, along(): pl.pallas_call(along_kernel, grid_spec=pltpu.PrefetchScalarGridSpec(num_s...  9.99 us
    pallas_call x1, Pallas kernels, cross(): pl.pallas_call(cross_kernel, out_shape=jax.ShapeDtypeStruct((4, 8, 2, 72,...  7.04 us
    unnamed x10, local copies, waits for them, and re-layouts  5.64 us
  transfers between devices with their start and end apart: 7, of which 6 were waited for; matrix products, arithmetic and copies ran while one was open for 0% of the time, Pallas kernels for 8%

profile of v7, /device:TPU:4, one launch (start us, length us, event | category | flops | bytes accessed | tf_op | source)
XLA Modules:
  0.0 119.5 jit_solution(9021469531050652456)
XLA Ops:
  0.6 2.1 %shard_map.75 = f32[2304,128]{1,0:T(8,128)} custom-call(f32[24,32,384]{2,1,0:T(8,128)} %bitcast.14), custom_call_target="tpu_custom_call" | custom-call | tf_op jit(solution)/shard_map/pallas_call | solution.py:112
  2.8 0.0 copy-start
  2.8 12.9 %all-to-all-start = ((f32[64,9,4,128]{3,2,1,0:T(4,128)}), f32[64,9,4,128]{3,2,1,0:T(4,128)S(1)}, u32[]{:S(2)}, u32[]{:S(2)}) async-start(f32[64,9,4,128]{3,2,1,0:T(4,128)} %bitcast.17), calls=%async_computation | async-start | bytes 2359296 | tf_op jit(solution)/shard_map/all_to_all | solution.py:336
  15.7 0.0 copy-done
  15.7 0.1 collective-permute-start.1
  15.8 0.9 collective-permute-start
  16.7 18.9 %collective-permute-done.far_a = f32[256,384]{1,0:T(8,128)} collective-permute-done((f32[256,384]{1,0:T(8,128)S(1)}, f32[256,384]{1,0:T(8,128)}, u32[]{:S(2)}, u32[]{:S(2)}) %collective-permute-start) | collective-permute-done | bytes 393248 | tf_op jit(solution)/shard_map/ppermute | solution.py:341
  35.6 0.0 collective-permute-done.1.near
  35.6 0.0 copy-start.1
  35.6 1.0 copy-done.1
  36.6 10.8 %all-to-all-done = f32[64,9,4,128]{3,2,1,0:T(4,128)S(1)} async-done(((f32[64,9,4,128]{3,2,1,0:T(4,128)}), f32[64,9,4,128]{3,2,1,0:T(4,128)S(1)}, u32[]{:S(2)}, u32[]{:S(2)}) %all-to-all-start) | async-done | bytes 1179680 | tf_op jit(solution)/shard_map/all_to_all | solution.py:336
  47.4 0.0 copy-start.4
  47.4 1.0 copy-done.4
  48.4 7.0 %shard_map.77 = f32[4,8,2,72,128]{4,3,2,1,0:T(8,128)} custom-call(bf16[2,2,2,128,640]{4,3,2,1,0:T(8,128)(2,1)} %constant.10.clone.small_hbm, bf16[2,2,256,1280]{3,2,1,0:T(8,128)(2,1)} %constant.11.clone.large_hbm, f32[4,2,4,72,128]{4,3,2,1,0:T(8,128)} %bitcast.19), custom_call_target="tpu_custom_call" | custom-call | flops 2717908992 | bytes 12582912 | tf_op jit(solution)/shard_map/pallas_call | solution.py:262
  55.5 6.0 %all-to-all-start.1 = ((f32[64,72,128]{2,1,0:T(8,128)}), f32[64,72,128]{2,1,0:T(8,128)S(1)}, u32[]{:S(2)}, u32[]{:S(2)}) async-start(f32[64,72,128]{2,1,0:T(8,128)} %bitcast.18), calls=%async_computation.1 | async-start | bytes 4718592 | tf_op jit(solution)/shard_map/all_to_all | solution.py:336
  61.5 0.1 slice.14
  61.5 0.9 collective-permute-start.2
  62.4 33.9 %collective-permute-done.2.far_b = f32[512,384]{1,0:T(8,128)} collective-permute-done((f32[512,384]{1,0:T(8,128)S(1)}, f32[512,384]{1,0:T(8,128)}, u32[]{:S(2)}, u32[]{:S(2)}) %collective-permute-start.2) | collective-permute-done | bytes 786464 | tf_op jit(solution)/shard_map/ppermute | solution.py:345
  96.3 0.0 collective-permute-start.4
  96.3 0.5 collective-permute-start.3
  96.8 2.1 %collective-permute-done.4.far_near_b = f32[512,384]{1,0:T(8,128)} collective-permute-done((f32[512,384]{1,0:T(8,128)}, f32[512,384]{1,0:T(8,128)}, u32[]{:S(2)}, u32[]{:S(2)}) %collective-permute-start.4) | collective-permute-done | bytes 786464 | tf_op jit(solution)/shard_map/ppermute | solution.py:348
  99.0 0.6 collective-permute-done.3.far_near_a
  99.5 0.0 copy-start.2
  99.5 1.3 %copy-done.2 = f32[768,384]{1,0:T(8,128)S(1)} copy-done((f32[768,384]{1,0:T(8,128)S(1)}, f32[768,384]{1,0:T(8,128)}, u32[]{:S(2)}) %copy-start.2) | copy-done | bytes 1179672
  100.8 0.0 copy-start.3
  100.8 2.3 %copy-done.3 = bf16[2,4,384,768]{3,2,1,0:T(8,128)(2,1)S(1)} copy-done((bf16[2,4,384,768]{3,2,1,0:T(8,128)(2,1)S(1)}, bf16[2,4,384,768]{3,2,1,0:T(8,128)(2,1)}, u32[]{:S(2)}) %copy-start.3) | copy-done | bytes 4718616
  103.1 10.0 %shard_map.76 = (f32[768,384]{1,0:T(8,128)}, f32[768,384]{1,0:T(8,128)}) custom-call(s32[1]{0:T(128)} %bitcast.core_ref, bf16[2,4,384,768]{3,2,1,0:T(8,128)(2,1)S(1)} %copy-done.3, f32[768,384]{1,0:T(8,128)S(1)} %bitcast.16, f32[768,384]{1,0:T(8,128)S(1)} %copy-done.2, f32[256,384]{1,0:T(8,128)} %collective-permute-done.far_a, ...), custom_call_target="tpu_custom_call" | custom-call | flops 5435817984 | bytes 16777216 | tf_op jit(solution)/shard_map/pallas_call | solution.py:312
  113.1 4.8 %all-to-all-done.1 = f32[64,72,128]{2,1,0:T(8,128)S(1)} async-done(((f32[64,72,128]{2,1,0:T(8,128)}), f32[64,72,128]{2,1,0:T(8,128)S(1)}, u32[]{:S(2)}, u32[]{:S(2)}) %all-to-all-start.1) | async-done | bytes 2359328 | tf_op jit(solution)/shard_map/all_to_all | solution.py:336
  117.9 1.6 %shard_map.78 = (f32[24,32,384]{2,1,0:T(8,128)}, f32[24,32,384]{2,1,0:T(8,128)}) custom-call(f32[4608,128]{1,0:T(8,128)S(1)} %bitcast.13), custom_call_target="tpu_custom_call" | custom-call | tf_op jit(solution)/shard_map/pallas_call | solution.py:155
  (1 shorter events, 0.0 us)
Async XLA Ops:
  2.8 12.9 %copy-start = (f32[24,2,16,384]{3,2,1,0:T(8,128)S(1)}, f32[24,2,16,384]{3,2,1,0:T(8,128)}, u32[]{:S(2)}) copy-start(f32[24,2,16,384]{3,2,1,0:T(8,128)} %param.4) | copy-start | bytes 3538948
  2.8 44.6 %all-to-all-start = ((f32[64,9,4,128]{3,2,1,0:T(4,128)}), f32[64,9,4,128]{3,2,1,0:T(4,128)S(1)}, u32[]{:S(2)}, u32[]{:S(2)}) async-start(f32[64,9,4,128]{3,2,1,0:T(4,128)} %bitcast.17), calls=%async_computation | async-start | bytes 2359296 | tf_op jit(solution)/shard_map/all_to_all | solution.py:336
  15.7 19.9 %collective-permute-start.1 = (f32[768,384]{1,0:T(8,128)S(1)}, f32[768,384]{1,0:T(8,128)S(1)}, u32[]{:S(2)}, u32[]{:S(2)}) collective-permute-start(f32[768,384]{1,0:T(8,128)S(1)} %bitcast.15), channel_id=1, source_target_pairs={{0,1},{1,0},{2,3},{3,2},{4,5},{5,4},{6,7},{7,6},{8,9},{9,8},{10,11... | collective-permute-start | bytes 3538952 | tf_op jit(solution)/shard_map/ppermute | solution.py:342
  15.8 19.8 %collective-permute-start = (f32[256,384]{1,0:T(8,128)S(1)}, f32[256,384]{1,0:T(8,128)}, u32[]{:S(2)}, u32[]{:S(2)}) collective-permute-start(f32[256,384]{1,0:T(8,128)S(1)} %bitcast.21), channel_id=1, source_target_pairs={{0,2},{2,0},{1,3},{3,1},{4,6},{6,4},{5,7},{7,5},{8,10},{10,8},{9,1... | collective-permute-start | bytes 1179656 | tf_op jit(solution)/shard_map/ppermute | solution.py:341
  35.6 1.0 copy-start.1
  47.4 1.0 copy-start.4
  55.5 62.4 %all-to-all-start.1 = ((f32[64,72,128]{2,1,0:T(8,128)}), f32[64,72,128]{2,1,0:T(8,128)S(1)}, u32[]{:S(2)}, u32[]{:S(2)}) async-start(f32[64,72,128]{2,1,0:T(8,128)} %bitcast.18), calls=%async_computation.1 | async-start | bytes 4718592 | tf_op jit(solution)/shard_map/all_to_all | solution.py:336
  61.5 34.8 %collective-permute-start.2 = (f32[512,384]{1,0:T(8,128)S(1)}, f32[512,384]{1,0:T(8,128)}, u32[]{:S(2)}, u32[]{:S(2)}) collective-permute-start(f32[512,384]{1,0:T(8,128)S(1)} %bitcast.20), channel_id=1, source_target_pairs={{0,2},{2,0},{1,3},{3,1},{4,6},{6,4},{5,7},{7,5},{8,10},{10,8},{9,1... | collective-permute-start | bytes 2359304 | tf_op jit(solution)/shard_map/ppermute | solution.py:345
  96.3 2.6 %collective-permute-start.4 = (f32[512,384]{1,0:T(8,128)}, f32[512,384]{1,0:T(8,128)}, u32[]{:S(2)}, u32[]{:S(2)}) collective-permute-start(f32[512,384]{1,0:T(8,128)} %collective-permute-done.2.far_b), channel_id=1, source_target_pairs={{0,1},{1,0},{2,3},{3,2},{4,5},{5,4},{6,7},{7,6},{8,9},{9,8},{10,11... | collective-permute-start | bytes 2359304 | tf_op jit(solution)/shard_map/ppermute | solution.py:348
  96.3 3.2 %collective-permute-start.3 = (f32[256,384]{1,0:T(8,128)}, f32[256,384]{1,0:T(8,128)}, u32[]{:S(2)}, u32[]{:S(2)}) collective-permute-start(f32[256,384]{1,0:T(8,128)} %collective-permute-done.far_a), channel_id=1, source_target_pairs={{0,1},{1,0},{2,3},{3,2},{4,5},{5,4},{6,7},{7,6},{8,9},{9,8},{10,11... | collective-permute-start | bytes 1179656 | tf_op jit(solution)/shard_map/ppermute | solution.py:347
  99.5 1.3 %copy-start.2 = (f32[768,384]{1,0:T(8,128)S(1)}, f32[768,384]{1,0:T(8,128)}, u32[]{:S(2)}) copy-start(f32[768,384]{1,0:T(8,128)} %copy-done.1) | copy-start | bytes 3538948
  100.8 2.3 %copy-start.3 = (bf16[2,4,384,768]{3,2,1,0:T(8,128)(2,1)S(1)}, bf16[2,4,384,768]{3,2,1,0:T(8,128)(2,1)}, u32[]{:S(2)}) copy-start(bf16[2,4,384,768]{3,2,1,0:T(8,128)(2,1)} %constant.12.clone.table_ref) | copy-start | bytes 14155780

commit v8 on v4

--- a/solution.py
+++ b/solution.py
@@ -215,7 +215,9 @@
                 for k in range(2):
                     small[k, h, rows, :] = small_strip[k, h, d, :, lanes]
     head, tail = line[0, :QUARTER, :], line[0, QUARTER:, :]
-    for k, value in enumerate((head + tail, head - tail)):
+    whole = head + tail
+    whole = whole - jnp.sum(whole, axis=0, keepdims=True) * (1.0 / QUARTER)
+    for k, value in enumerate((whole, head - tail)):
         high, low = split(value)
         got_small[k] = three(small[k, 0], small[k, 1], high, low)
 
@@ -297,8 +299,9 @@
     far_near = jnp.where(early, far_near_a[...], far_near_b[...])
     total = jnp.zeros((256, 2 * LANES), F32)
     pairs = ((own[...], 0), (near[...], 1 + 2 * core), (far, 2), (far_near, 3 - 2 * core))
+    level = jnp.sum(own[...], axis=1, keepdims=True) * (1.0 / LANES)
     for block, r in pairs:
-        high, low = split(block)
+        high, low = split(block - level)
         total = total + three(high, low, table_ref[0, r], table_ref[1, r])
     first_ref[...] = total[:, :LANES]
     second_ref[...] = total[:, LANES:]

time: 119 us -> 119 us (level)
  transfers between devices with their start and end apart: 7 -> 7, of which waited for: 6 -> 6; matrix products, arithmetic and copies ran while one was open for 0% -> 0% of each run, Pallas kernels for 8% -> 9%
where the time goes in v8:
time: 119 us
  waiting for transfers between devices  69.7 us (59%)
  Pallas kernels  21.3 us (18%)
  starting transfers between devices  21.2 us (18%)
  local copies, waits for them, and re-layouts  5.72 us (5%)
    ppermute x1, waiting for transfers between devices, shards(): far_b = lax.ppermute(own[256:], 'xh', pair)  34.3 us
    ppermute x1, waiting for transfers between devices, shards(): far_a = lax.ppermute(own[:256], 'xh', pair)  19.1 us
    all_to_all x2, starting transfers between devices, swap(): lax.all_to_all(message, ('z', 'y', 'xl'), split_axis=0, concat_axis=0, ti...  18.9 us
    all_to_all x2, waiting for transfers between devices, swap(): lax.all_to_all(message, ('z', 'y', 'xl'), split_axis=0, concat_axis=0, ti...  13.7 us
    pallas_call x1, Pallas kernels, along(): pl.pallas_call(along_kernel, grid_spec=pltpu.PrefetchScalarGridSpec(num_s...  10.5 us
    pallas_call x1, Pallas kernels, cross(): pl.pallas_call(cross_kernel, out_shape=jax.ShapeDtypeStruct((8, 4, 2, 72,...  7.1 us
    unnamed x10, local copies, waits for them, and re-layouts  5.64 us
  transfers between devices with their start and end apart: 7, of which 6 were waited for; matrix products, arithmetic and copies ran while one was open for 0% of the time, Pallas kernels for 9%

profile of v8, /device:TPU:4, one launch (start us, length us, event | category | flops | bytes accessed | tf_op | source)
XLA Modules:
  0.0 118.7 jit_solution(6074143079393740829)
XLA Ops:
  0.6 2.1 %shard_map.75 = f32[2304,128]{1,0:T(8,128)} custom-call(f32[24,32,384]{2,1,0:T(8,128)} %bitcast.14), custom_call_target="tpu_custom_call" | custom-call | tf_op jit(solution)/shard_map/pallas_call | solution.py:112
  2.8 0.0 copy-start
  2.8 12.9 %all-to-all-start = ((f32[64,9,4,128]{3,2,1,0:T(4,128)}), f32[64,9,4,128]{3,2,1,0:T(4,128)S(1)}, u32[]{:S(2)}, u32[]{:S(2)}) async-start(f32[64,9,4,128]{3,2,1,0:T(4,128)} %bitcast.17), calls=%async_computation | async-start | bytes 2359296 | tf_op jit(solution)/shard_map/all_to_all | solution.py:339
  15.7 0.0 copy-done
  15.7 0.1 collective-permute-start.1
  15.8 0.9 collective-permute-start
  16.7 19.1 %collective-permute-done.far_a = f32[256,384]{1,0:T(8,128)} collective-permute-done((f32[256,384]{1,0:T(8,128)S(1)}, f32[256,384]{1,0:T(8,128)}, u32[]{:S(2)}, u32[]{:S(2)}) %collective-permute-start) | collective-permute-done | bytes 393248 | tf_op jit(solution)/shard_map/ppermute | solution.py:344
  35.8 0.0 collective-permute-done.1.near
  35.8 0.0 copy-start.1
  35.8 1.0 copy-done.1
  36.8 10.5 %all-to-all-done = f32[64,9,4,128]{3,2,1,0:T(4,128)S(1)} async-done(((f32[64,9,4,128]{3,2,1,0:T(4,128)}), f32[64,9,4,128]{3,2,1,0:T(4,128)S(1)}, u32[]{:S(2)}, u32[]{:S(2)}) %all-to-all-start) | async-done | bytes 1179680 | tf_op jit(solution)/shard_map/all_to_all | solution.py:339
  47.3 0.0 copy-start.4
  47.3 1.0 copy-done.4
  48.3 7.1 %shard_map.77 = f32[8,4,2,72,128]{4,3,2,1,0:T(8,128)} custom-call(bf16[2,2,2,128,640]{4,3,2,1,0:T(8,128)(2,1)} %constant.10.clone.small_hbm, bf16[2,2,256,1280]{3,2,1,0:T(8,128)(2,1)} %constant.11.clone.large_hbm, f32[2,4,4,72,128]{4,3,2,1,0:T(8,128)} %bitcast.19), custom_call_target="tpu_custom_call" | custom-call | flops 2717908992 | bytes 12582912 | tf_op jit(solution)/shard_map/pallas_call | solution.py:264
  55.4 6.0 %all-to-all-start.1 = ((f32[64,72,128]{2,1,0:T(8,128)}), f32[64,72,128]{2,1,0:T(8,128)S(1)}, u32[]{:S(2)}, u32[]{:S(2)}) async-start(f32[64,72,128]{2,1,0:T(8,128)} %bitcast.18), calls=%async_computation.1 | async-start | bytes 4718592 | tf_op jit(solution)/shard_map/all_to_all | solution.py:339
  61.4 0.1 slice.14
  61.4 0.9 collective-permute-start.2
  62.3 34.3 %collective-permute-done.2.far_b = f32[512,384]{1,0:T(8,128)} collective-permute-done((f32[512,384]{1,0:T(8,128)S(1)}, f32[512,384]{1,0:T(8,128)}, u32[]{:S(2)}, u32[]{:S(2)}) %collective-permute-start.2) | collective-permute-done | bytes 786464 | tf_op jit(solution)/shard_map/ppermute | solution.py:348
  96.6 0.0 collective-permute-start.4
  96.6 0.5 collective-permute-start.3
  97.1 2.1 %collective-permute-done.4.far_near_b = f32[512,384]{1,0:T(8,128)} collective-permute-done((f32[512,384]{1,0:T(8,128)}, f32[512,384]{1,0:T(8,128)}, u32[]{:S(2)}, u32[]{:S(2)}) %collective-permute-start.4) | collective-permute-done | bytes 786464 | tf_op jit(solution)/shard_map/ppermute | solution.py:351
  99.2 0.6 collective-permute-done.3.far_near_a
  99.8 0.0 copy-start.2
  99.8 1.3 %copy-done.2 = f32[768,384]{1,0:T(8,128)S(1)} copy-done((f32[768,384]{1,0:T(8,128)S(1)}, f32[768,384]{1,0:T(8,128)}, u32[]{:S(2)}) %copy-start.2) | copy-done | bytes 1179672
  101.0 0.0 copy-start.3
  101.0 2.3 %copy-done.3 = bf16[2,4,384,768]{3,2,1,0:T(8,128)(2,1)S(1)} copy-done((bf16[2,4,384,768]{3,2,1,0:T(8,128)(2,1)S(1)}, bf16[2,4,384,768]{3,2,1,0:T(8,128)(2,1)}, u32[]{:S(2)}) %copy-start.3) | copy-done | bytes 4718616
  103.4 10.5 %shard_map.76 = (f32[768,384]{1,0:T(8,128)}, f32[768,384]{1,0:T(8,128)}) custom-call(s32[1]{0:T(128)} %bitcast.core_ref, bf16[2,4,384,768]{3,2,1,0:T(8,128)(2,1)S(1)} %copy-done.3, f32[768,384]{1,0:T(8,128)S(1)} %bitcast.16, f32[768,384]{1,0:T(8,128)S(1)} %copy-done.2, f32[256,384]{1,0:T(8,128)} %collective-permute-done.far_a, ...), custom_call_target="tpu_custom_call" | custom-call | flops 5435817984 | bytes 16777216 | tf_op jit(solution)/shard_map/pallas_call | solution.py:315
  113.8 3.3 %all-to-all-done.1 = f32[64,72,128]{2,1,0:T(8,128)S(1)} async-done(((f32[64,72,128]{2,1,0:T(8,128)}), f32[64,72,128]{2,1,0:T(8,128)S(1)}, u32[]{:S(2)}, u32[]{:S(2)}) %all-to-all-start.1) | async-done | bytes 2359328 | tf_op jit(solution)/shard_map/all_to_all | solution.py:339
  117.1 1.6 %shard_map.78 = (f32[24,32,384]{2,1,0:T(8,128)}, f32[24,32,384]{2,1,0:T(8,128)}) custom-call(f32[4608,128]{1,0:T(8,128)S(1)} %bitcast.13), custom_call_target="tpu_custom_call" | custom-call | tf_op jit(solution)/shard_map/pallas_call | solution.py:155
  (1 shorter events, 0.0 us)
Async XLA Ops:
  2.8 12.9 %copy-start = (f32[24,2,16,384]{3,2,1,0:T(8,128)S(1)}, f32[24,2,16,384]{3,2,1,0:T(8,128)}, u32[]{:S(2)}) copy-start(f32[24,2,16,384]{3,2,1,0:T(8,128)} %param.4) | copy-start | bytes 3538948
  2.8 44.5 %all-to-all-start = ((f32[64,9,4,128]{3,2,1,0:T(4,128)}), f32[64,9,4,128]{3,2,1,0:T(4,128)S(1)}, u32[]{:S(2)}, u32[]{:S(2)}) async-start(f32[64,9,4,128]{3,2,1,0:T(4,128)} %bitcast.17), calls=%async_computation | async-start | bytes 2359296 | tf_op jit(solution)/shard_map/all_to_all | solution.py:339
  15.7 20.1 %collective-permute-start.1 = (f32[768,384]{1,0:T(8,128)S(1)}, f32[768,384]{1,0:T(8,128)S(1)}, u32[]{:S(2)}, u32[]{:S(2)}) collective-permute-start(f32[768,384]{1,0:T(8,128)S(1)} %bitcast.15), channel_id=1, source_target_pairs={{0,1},{1,0},{2,3},{3,2},{4,5},{5,4},{6,7},{7,6},{8,9},{9,8},{10,11... | collective-permute-start | bytes 3538952 | tf_op jit(solution)/shard_map/ppermute | solution.py:345
  15.8 20.0 %collective-permute-start = (f32[256,384]{1,0:T(8,128)S(1)}, f32[256,384]{1,0:T(8,128)}, u32[]{:S(2)}, u32[]{:S(2)}) collective-permute-start(f32[256,384]{1,0:T(8,128)S(1)} %bitcast.21), channel_id=1, source_target_pairs={{0,2},{2,0},{1,3},{3,1},{4,6},{6,4},{5,7},{7,5},{8,10},{10,8},{9,1... | collective-permute-start | bytes 1179656 | tf_op jit(solution)/shard_map/ppermute | solution.py:344
  35.8 1.0 copy-start.1
  47.3 1.0 copy-start.4
  55.4 61.7 %all-to-all-start.1 = ((f32[64,72,128]{2,1,0:T(8,128)}), f32[64,72,128]{2,1,0:T(8,128)S(1)}, u32[]{:S(2)}, u32[]{:S(2)}) async-start(f32[64,72,128]{2,1,0:T(8,128)} %bitcast.18), calls=%async_computation.1 | async-start | bytes 4718592 | tf_op jit(solution)/shard_map/all_to_all | solution.py:339
  61.4 35.1 %collective-permute-start.2 = (f32[512,384]{1,0:T(8,128)S(1)}, f32[512,384]{1,0:T(8,128)}, u32[]{:S(2)}, u32[]{:S(2)}) collective-permute-start(f32[512,384]{1,0:T(8,128)S(1)} %bitcast.20), channel_id=1, source_target_pairs={{0,2},{2,0},{1,3},{3,1},{4,6},{6,4},{5,7},{7,5},{8,10},{10,8},{9,1... | collective-permute-start | bytes 2359304 | tf_op jit(solution)/shard_map/ppermute | solution.py:348
  96.6 2.6 %collective-permute-start.4 = (f32[512,384]{1,0:T(8,128)}, f32[512,384]{1,0:T(8,128)}, u32[]{:S(2)}, u32[]{:S(2)}) collective-permute-start(f32[512,384]{1,0:T(8,128)} %collective-permute-done.2.far_b), channel_id=1, source_target_pairs={{0,1},{1,0},{2,3},{3,2},{4,5},{5,4},{6,7},{7,6},{8,9},{9,8},{10,11... | collective-permute-start | bytes 2359304 | tf_op jit(solution)/shard_map/ppermute | solution.py:351
  96.6 3.2 %collective-permute-start.3 = (f32[256,384]{1,0:T(8,128)}, f32[256,384]{1,0:T(8,128)}, u32[]{:S(2)}, u32[]{:S(2)}) collective-permute-start(f32[256,384]{1,0:T(8,128)} %collective-permute-done.far_a), channel_id=1, source_target_pairs={{0,1},{1,0},{2,3},{3,2},{4,5},{5,4},{6,7},{7,6},{8,9},{9,8},{10,11... | collective-permute-start | bytes 1179656 | tf_op jit(solution)/shard_map/ppermute | solution.py:350
  99.8 1.3 %copy-start.2 = (f32[768,384]{1,0:T(8,128)S(1)}, f32[768,384]{1,0:T(8,128)}, u32[]{:S(2)}) copy-start(f32[768,384]{1,0:T(8,128)} %copy-done.1) | copy-start | bytes 3538948
  101.0 2.3 %copy-start.3 = (bf16[2,4,384,768]{3,2,1,0:T(8,128)(2,1)S(1)}, bf16[2,4,384,768]{3,2,1,0:T(8,128)(2,1)}, u32[]{:S(2)}) copy-start(bf16[2,4,384,768]{3,2,1,0:T(8,128)(2,1)} %constant.12.clone.table_ref) | copy-start | bytes 14155780

commit v9 on v8

--- a/solution.py
+++ b/solution.py
@@ -290,43 +290,67 @@
     )(small, large, message.reshape(2, 4, 4, 72, 128))
 
 
-def along_kernel(
-    core_ref, table_ref, own, near, far_a, far_b, far_near_a, far_near_b, first_ref, second_ref
+def add_lines(total, table_ref, pairs, level):
+    for block, r in pairs:
+        high, low = split(block - level)
+        total = total + three(high, low, table_ref[0, r], table_ref[1, r])
+    return total
+
+
+def line_level(own):
+    return jnp.sum(own[...], axis=1, keepdims=True) * (1.0 / LANES)
+
+
+def close_kernel(core_ref, table_ref, own, near, out_ref):
+    pairs = ((own[...], 0), (near[...], 1 + 2 * core_ref[0]))
+    total = jnp.zeros((256, 2 * LANES), F32)
+    out_ref[...] = add_lines(total, table_ref, pairs, line_level(own))
+
+
+def far_kernel(
+    core_ref, table_ref, own, part, far_a, far_b, far_near_a, far_near_b, first_ref, second_ref
 ):
-    core = core_ref[0]
     early = pl.program_id(0) == 0
     far = jnp.where(early, far_a[...], far_b[...])
     far_near = jnp.where(early, far_near_a[...], far_near_b[...])
-    total = jnp.zeros((256, 2 * LANES), F32)
-    pairs = ((own[...], 0), (near[...], 1 + 2 * core), (far, 2), (far_near, 3 - 2 * core))
-    level = jnp.sum(own[...], axis=1, keepdims=True) * (1.0 / LANES)
-    for block, r in pairs:
-        high, low = split(block - level)
-        total = total + three(high, low, table_ref[0, r], table_ref[1, r])
+    pairs = ((far, 2), (far_near, 3 - 2 * core_ref[0]))
+    total = add_lines(part[...], table_ref, pairs, line_level(own))
     first_ref[...] = total[:, :LANES]
     second_ref[...] = total[:, LANES:]
 
 
-def along(core, table, *blocks):
-    out = jax.ShapeDtypeStruct((ROWS * PLANES, LANES), F32)
-    lines = pl.BlockSpec((256, LANES), lambda i, core: (i, 0))
-    early = pl.BlockSpec((256, LANES), lambda i, core: (0, 0))
-    late = pl.BlockSpec((256, LANES), lambda i, core: (jnp.maximum(i, 1) - 1, 0))
+LINES = pl.BlockSpec((256, LANES), lambda i, core: (i, 0))
+BOTH = pl.BlockSpec((256, 2 * LANES), lambda i, core: (i, 0))
+
+
+def along(kernel, ins, outs, shapes):
     return pl.pallas_call(
-        along_kernel,
+        kernel,
         grid_spec=pltpu.PrefetchScalarGridSpec(
             num_scalar_prefetch=1,
             grid=(3,),
-            in_specs=[pl.BlockSpec((2, 4, LANES, 2 * LANES), lambda i, core: (0, 0, 0, 0))]
-            + [lines, lines, early, late, early, late],
-            out_specs=[lines] * 2,
+            in_specs=[pl.BlockSpec((2, 4, LANES, 2 * LANES), lambda i, core: (0, 0, 0, 0))] + ins,
+            out_specs=outs,
         ),
-        out_shape=(out, out),
+        out_shape=shapes,
         compiler_params=pltpu.CompilerParams(vmem_limit_bytes=24 * 2**20),
         cost_estimate=pl.CostEstimate(
-            flops=2 * 3 * 768 * COUNT * 768, bytes_accessed=16 * 2**20, transcendentals=0
+            flops=3 * 768 * COUNT * 768, bytes_accessed=12 * 2**20, transcendentals=0
         ),
-    )(core, table, *blocks)
+    )
+
+
+def along_close(*args):
+    shape = jax.ShapeDtypeStruct((ROWS * PLANES, 2 * LANES), F32)
+    return along(close_kernel, [LINES, LINES], BOTH, shape)(*args)
+
+
+def along_far(*args):
+    out = jax.ShapeDtypeStruct((ROWS * PLANES, LANES), F32)
+    early = pl.BlockSpec((256, LANES), lambda i, core: (0, 0))
+    late = pl.BlockSpec((256, LANES), lambda i, core: (jnp.maximum(i, 1) - 1, 0))
+    ins = [LINES, BOTH, early, late, early, late]
+    return along(far_kernel, ins, [LINES] * 2, (out, out))(*args)
 
 
 def solution(mesh):
@@ -350,8 +374,10 @@
         far_near_a = lax.ppermute(far_a, "c", pair)
         far_near_b = lax.ppermute(far_b, "c", pair)
         core = lax.axis_index("c").reshape(1)
-        first_z, second_z = along(
-            core, jnp.asarray(along_t), own, near, far_a, far_b, far_near_a, far_near_b
+        table = jnp.asarray(along_t)
+        part = along_close(core, table, own, near)
+        first_z, second_z = along_far(
+            core, table, own, part, far_a, far_b, far_near_a, far_near_b
         )
         first_z, second_z, back = lax.optimization_barrier((first_z, second_z, back))
         first, second = unpack(back.reshape(4608, 128))

time: 119 us -> 119 us (level)
    all_to_all x2, waiting for transfers between devices: 13.7 us -> 15.9 us  [swap(): lax.all_to_all(message, ('z', 'y', 'xl'), split_axis=0, concat_axis=0, ti...]
    ppermute x1, waiting for transfers between devices: 2.12 us -> 0.01 us  [shards(): far_near_b = lax.ppermute(far_b, 'c', pair)]
    pallas_call x1 -> x2, Pallas kernels: 10.5 us -> 11 us  [the longest x1 6.62 us: along_far(): return along(far_kernel, ins, [LINES] * 2, (out, out))(*args)]
  transfers between devices with their start and end apart: 7 -> 7, of which waited for: 6 -> 4; matrix products, arithmetic and copies ran while one was open for 0% -> 0% of each run, Pallas kernels for 9% -> 9%
where the time goes in v9:
time: 119 us
  waiting for transfers between devices  69.2 us (58%)
  Pallas kernels  21.9 us (18%)
  starting transfers between devices  21.2 us (18%)
  local copies, waits for them, and re-layouts  5.72 us (5%)
    ppermute x1, waiting for transfers between devices, shards(): far_b = lax.ppermute(own[256:], 'xh', pair)  34.3 us
    ppermute x1, waiting for transfers between devices, shards(): far_a = lax.ppermute(own[:256], 'xh', pair)  19.1 us
    all_to_all x2, starting transfers between devices, swap(): lax.all_to_all(message, ('z', 'y', 'xl'), split_axis=0, concat_axis=0, ti...  18.9 us
    all_to_all x2, waiting for transfers between devices, swap(): lax.all_to_all(message, ('z', 'y', 'xl'), split_axis=0, concat_axis=0, ti...  15.9 us
    pallas_call x1, Pallas kernels, cross(): pl.pallas_call(cross_kernel, out_shape=jax.ShapeDtypeStruct((8, 4, 2, 72,...  7.1 us
    pallas_call x1, Pallas kernels, along_far(): return along(far_kernel, ins, [LINES] * 2, (out, out))(*args)  6.62 us
    unnamed x10, local copies, waits for them, and re-layouts  5.64 us
    pallas_call x1, Pallas kernels, along_close(): return along(close_kernel, [LINES, LINES], BOTH, shape)(*args)  4.38 us
  transfers between devices with their start and end apart: 7, of which 4 were waited for; matrix products, arithmetic and copies ran while one was open for 0% of the time, Pallas kernels for 9%

profile of v9, /device:TPU:4, one launch (start us, length us, event | category | flops | bytes accessed | tf_op | source)
XLA Modules:
  0.0 118.7 jit_solution(2777947976772413456)
XLA Ops:
  0.6 2.1 %shard_map.75 = f32[2304,128]{1,0:T(8,128)} custom-call(f32[24,32,384]{2,1,0:T(8,128)} %bitcast.13), custom_call_target="tpu_custom_call" | custom-call | tf_op jit(solution)/shard_map/pallas_call | solution.py:112
  2.8 0.0 copy-start
  2.8 12.9 %all-to-all-start = ((f32[64,9,4,128]{3,2,1,0:T(4,128)}), f32[64,9,4,128]{3,2,1,0:T(4,128)S(1)}, u32[]{:S(2)}, u32[]{:S(2)}) async-start(f32[64,9,4,128]{3,2,1,0:T(4,128)} %bitcast.18), calls=%async_computation | async-start | bytes 2359296 | tf_op jit(solution)/shard_map/all_to_all | solution.py:363
  15.7 0.0 copy-done
  15.7 0.1 collective-permute-start.1
  15.8 0.9 collective-permute-start
  16.7 19.1 %collective-permute-done.far_a = f32[256,384]{1,0:T(8,128)} collective-permute-done((f32[256,384]{1,0:T(8,128)S(1)}, f32[256,384]{1,0:T(8,128)}, u32[]{:S(2)}, u32[]{:S(2)}) %collective-permute-start) | collective-permute-done | bytes 393248 | tf_op jit(solution)/shard_map/ppermute | solution.py:368
  35.8 0.0 collective-permute-done.1.near
  35.8 0.0 copy-start.2
  35.8 1.0 copy-done.2
  36.8 10.5 %all-to-all-done = f32[64,9,4,128]{3,2,1,0:T(4,128)S(1)} async-done(((f32[64,9,4,128]{3,2,1,0:T(4,128)}), f32[64,9,4,128]{3,2,1,0:T(4,128)S(1)}, u32[]{:S(2)}, u32[]{:S(2)}) %all-to-all-start) | async-done | bytes 1179680 | tf_op jit(solution)/shard_map/all_to_all | solution.py:363
  47.3 0.0 copy-start.4
  47.3 1.0 copy-done.4
  48.3 7.1 %shard_map.78 = f32[8,4,2,72,128]{4,3,2,1,0:T(8,128)} custom-call(bf16[2,2,2,128,640]{4,3,2,1,0:T(8,128)(2,1)} %constant.10.clone.small_hbm, bf16[2,2,256,1280]{3,2,1,0:T(8,128)(2,1)} %constant.11.clone.large_hbm, f32[2,4,4,72,128]{4,3,2,1,0:T(8,128)} %bitcast.20), custom_call_target="tpu_custom_call" | custom-call | flops 2717908992 | bytes 12582912 | tf_op jit(solution)/shard_map/pallas_call | solution.py:264
  55.4 6.0 %all-to-all-start.1 = ((f32[64,72,128]{2,1,0:T(8,128)}), f32[64,72,128]{2,1,0:T(8,128)S(1)}, u32[]{:S(2)}, u32[]{:S(2)}) async-start(f32[64,72,128]{2,1,0:T(8,128)} %bitcast.19), calls=%async_computation.1 | async-start | bytes 4718592 | tf_op jit(solution)/shard_map/all_to_all | solution.py:363
  61.4 0.1 slice.14
  61.4 0.9 collective-permute-start.2
  62.3 34.3 %collective-permute-done.2.far_b = f32[512,384]{1,0:T(8,128)} collective-permute-done((f32[512,384]{1,0:T(8,128)S(1)}, f32[512,384]{1,0:T(8,128)}, u32[]{:S(2)}, u32[]{:S(2)}) %collective-permute-start.2) | collective-permute-done | bytes 786464 | tf_op jit(solution)/shard_map/ppermute | solution.py:372
  96.6 0.0 collective-permute-start.4
  96.6 0.5 collective-permute-start.3
  97.1 0.0 copy-start.1
  97.1 2.3 %copy-done.1 = bf16[2,4,384,768]{3,2,1,0:T(8,128)(2,1)S(1)} copy-done((bf16[2,4,384,768]{3,2,1,0:T(8,128)(2,1)S(1)}, bf16[2,4,384,768]{3,2,1,0:T(8,128)(2,1)}, u32[]{:S(2)}) %copy-start.1) | copy-done | bytes 4718616
  99.4 0.0 copy-start.3
  99.4 1.3 %copy-done.3 = f32[768,384]{1,0:T(8,128)S(1)} copy-done((f32[768,384]{1,0:T(8,128)S(1)}, f32[768,384]{1,0:T(8,128)}, u32[]{:S(2)}) %copy-start.3) | copy-done | bytes 1179672
  100.7 4.4 %shard_map.76.part = f32[768,768]{1,0:T(8,128)S(1)} custom-call(s32[1]{0:T(128)} %bitcast.core_ref, bf16[2,4,384,768]{3,2,1,0:T(8,128)(2,1)S(1)} %copy-done.1, f32[768,384]{1,0:T(8,128)S(1)} %bitcast.15, f32[768,384]{1,0:T(8,128)S(1)} %copy-done.3), custom_call_target="tpu_custom_call" | custom-call | flops 2717908992 | bytes 12582912 | tf_op jit(solution)/shard_map/pallas_call | solution.py:345
  105.1 0.0 collective-permute-done.4.far_near_b
  105.1 0.0 collective-permute-done.3.far_near_a
  105.1 6.6 %shard_map.77 = (f32[768,384]{1,0:T(8,128)}, f32[768,384]{1,0:T(8,128)}) custom-call(s32[1]{0:T(128)} %bitcast.core_ref, bf16[2,4,384,768]{3,2,1,0:T(8,128)(2,1)S(1)} %copy-done.1, f32[768,384]{1,0:T(8,128)S(1)} %bitcast.16, f32[768,768]{1,0:T(8,128)S(1)} %shard_map.76.part, f32[256,384]{1,0:T(8,128)} %collective-permute-done.far_a, ...), custom_call_target="tpu_custom_call" | custom-call | flops 2717908992 | bytes 12582912 | tf_op jit(solution)/shard_map/pallas_call | solution.py:353
  111.7 5.4 %all-to-all-done.1 = f32[64,72,128]{2,1,0:T(8,128)S(1)} async-done(((f32[64,72,128]{2,1,0:T(8,128)}), f32[64,72,128]{2,1,0:T(8,128)S(1)}, u32[]{:S(2)}, u32[]{:S(2)}) %all-to-all-start.1) | async-done | bytes 2359328 | tf_op jit(solution)/shard_map/all_to_all | solution.py:363
  117.1 1.6 %shard_map.79 = (f32[24,32,384]{2,1,0:T(8,128)}, f32[24,32,384]{2,1,0:T(8,128)}) custom-call(f32[4608,128]{1,0:T(8,128)S(1)} %bitcast.17), custom_call_target="tpu_custom_call" | custom-call | tf_op jit(solution)/shard_map/pallas_call | solution.py:155
  (1 shorter events, 0.0 us)
Async XLA Ops:
  2.8 12.9 %copy-start = (f32[24,2,16,384]{3,2,1,0:T(8,128)S(1)}, f32[24,2,16,384]{3,2,1,0:T(8,128)}, u32[]{:S(2)}) copy-start(f32[24,2,16,384]{3,2,1,0:T(8,128)} %param.4) | copy-start | bytes 3538948
  2.8 44.5 %all-to-all-start = ((f32[64,9,4,128]{3,2,1,0:T(4,128)}), f32[64,9,4,128]{3,2,1,0:T(4,128)S(1)}, u32[]{:S(2)}, u32[]{:S(2)}) async-start(f32[64,9,4,128]{3,2,1,0:T(4,128)} %bitcast.18), calls=%async_computation | async-start | bytes 2359296 | tf_op jit(solution)/shard_map/all_to_all | solution.py:363
  15.7 20.1 %collective-permute-start.1 = (f32[768,384]{1,0:T(8,128)S(1)}, f32[768,384]{1,0:T(8,128)S(1)}, u32[]{:S(2)}, u32[]{:S(2)}) collective-permute-start(f32[768,384]{1,0:T(8,128)S(1)} %bitcast.14), channel_id=1, source_target_pairs={{0,1},{1,0},{2,3},{3,2},{4,5},{5,4},{6,7},{7,6},{8,9},{9,8},{10,11... | collective-permute-start | bytes 3538952 | tf_op jit(solution)/shard_map/ppermute | solution.py:369
  15.8 20.0 %collective-permute-start = (f32[256,384]{1,0:T(8,128)S(1)}, f32[256,384]{1,0:T(8,128)}, u32[]{:S(2)}, u32[]{:S(2)}) collective-permute-start(f32[256,384]{1,0:T(8,128)S(1)} %bitcast.22), channel_id=1, source_target_pairs={{0,2},{2,0},{1,3},{3,1},{4,6},{6,4},{5,7},{7,5},{8,10},{10,8},{9,1... | collective-permute-start | bytes 1179656 | tf_op jit(solution)/shard_map/ppermute | solution.py:368
  35.8 1.0 copy-start.2
  47.3 1.0 copy-start.4
  55.4 61.7 %all-to-all-start.1 = ((f32[64,72,128]{2,1,0:T(8,128)}), f32[64,72,128]{2,1,0:T(8,128)S(1)}, u32[]{:S(2)}, u32[]{:S(2)}) async-start(f32[64,72,128]{2,1,0:T(8,128)} %bitcast.19), calls=%async_computation.1 | async-start | bytes 4718592 | tf_op jit(solution)/shard_map/all_to_all | solution.py:363
  61.4 35.1 %collective-permute-start.2 = (f32[512,384]{1,0:T(8,128)S(1)}, f32[512,384]{1,0:T(8,128)}, u32[]{:S(2)}, u32[]{:S(2)}) collective-permute-start(f32[512,384]{1,0:T(8,128)S(1)} %bitcast.21), channel_id=1, source_target_pairs={{0,2},{2,0},{1,3},{3,1},{4,6},{6,4},{5,7},{7,5},{8,10},{10,8},{9,1... | collective-permute-start | bytes 2359304 | tf_op jit(solution)/shard_map/ppermute | solution.py:372
  96.6 8.5 %collective-permute-start.4 = (f32[512,384]{1,0:T(8,128)}, f32[512,384]{1,0:T(8,128)}, u32[]{:S(2)}, u32[]{:S(2)}) collective-permute-start(f32[512,384]{1,0:T(8,128)} %collective-permute-done.2.far_b), channel_id=1, source_target_pairs={{0,1},{1,0},{2,3},{3,2},{4,5},{5,4},{6,7},{7,6},{8,9},{9,8},{10,11... | collective-permute-start | bytes 2359304 | tf_op jit(solution)/shard_map/ppermute | solution.py:375
  96.6 8.5 %collective-permute-start.3 = (f32[256,384]{1,0:T(8,128)}, f32[256,384]{1,0:T(8,128)}, u32[]{:S(2)}, u32[]{:S(2)}) collective-permute-start(f32[256,384]{1,0:T(8,128)} %collective-permute-done.far_a), channel_id=1, source_target_pairs={{0,1},{1,0},{2,3},{3,2},{4,5},{5,4},{6,7},{7,6},{8,9},{9,8},{10,11... | collective-permute-start | bytes 1179656 | tf_op jit(solution)/shard_map/ppermute | solution.py:374
  97.1 2.3 %copy-start.1 = (bf16[2,4,384,768]{3,2,1,0:T(8,128)(2,1)S(1)}, bf16[2,4,384,768]{3,2,1,0:T(8,128)(2,1)}, u32[]{:S(2)}) copy-start(bf16[2,4,384,768]{3,2,1,0:T(8,128)(2,1)} %constant.12.clone.table_ref) | copy-start | bytes 14155780
  99.4 1.3 %copy-start.3 = (f32[768,384]{1,0:T(8,128)S(1)}, f32[768,384]{1,0:T(8,128)}, u32[]{:S(2)}) copy-start(f32[768,384]{1,0:T(8,128)} %copy-done.2) | copy-start | bytes 3538948

commit v10 on v9

--- a/solution.py
+++ b/solution.py
@@ -283,7 +283,7 @@
             pltpu.SemaphoreType.DMA((2,)),
             pltpu.SemaphoreType.DMA((8,)),
         ],
-        compiler_params=pltpu.CompilerParams(vmem_limit_bytes=60 * 2**20),
+        compiler_params=pltpu.CompilerParams(vmem_limit_bytes=56 * 2**20),
         cost_estimate=pl.CostEstimate(
             flops=3 * 2 * 3 * HALF * HALF * 256, bytes_accessed=12 * 2**20, transcendentals=0
         ),
@@ -366,9 +366,9 @@
         grid = moments.shape
         own = moments.reshape(ROWS * PLANES, LANES)
         far_a = lax.ppermute(own[:256], "xh", pair)
+        home = swap(pack(moments.reshape(ROWS, PLANES, LANES)).reshape(64, 9, 4, 128))
+        home, far_a, own = lax.optimization_barrier((home, far_a, own))
         near = lax.ppermute(own, "c", pair)
-        home = swap(pack(moments.reshape(ROWS, PLANES, LANES)).reshape(64, 9, 4, 128))
-        home, far_a, near = lax.optimization_barrier((home, far_a, near))
         far_b = lax.ppermute(own[256:], "xh", pair)
         back = swap(cross(jnp.asarray(small_t), jnp.asarray(large_t), home).reshape(64, 72, 128))
         far_near_a = lax.ppermute(far_a, "c", pair)

time: 119 us -> 119 us (level)
  local copies, waits for them, and re-layouts: 5.72 us -> 3.44 us
  waiting for transfers between devices: 69.2 us -> 70.6 us
    unnamed x10 -> x6, local copies, waits for them, and re-layouts: 5.64 us -> 3.36 us
    all_to_all x2, waiting for transfers between devices: 15.9 us -> 18 us  [swap(): lax.all_to_all(message, ('z', 'y', 'xl'), split_axis=0, concat_axis=0, ti...]
  transfers between devices with their start and end apart: 7 -> 7, of which waited for: 4 -> 4; matrix products, arithmetic and copies ran while one was open for 0% -> 0% of each run, Pallas kernels for 9% -> 10%
where the time goes in v10:
time: 119 us
  waiting for transfers between devices  70.6 us (59%)
  Pallas kernels  22.9 us (19%)
  starting transfers between devices  21.1 us (18%)
  local copies, waits for them, and re-layouts  3.44 us (3%)
    ppermute x1, waiting for transfers between devices, shards(): far_b = lax.ppermute(own[256:], 'xh', pair)  34.3 us
    all_to_all x2, starting transfers between devices, swap(): lax.all_to_all(message, ('z', 'y', 'xl'), split_axis=0, concat_axis=0, ti...  18.9 us
    ppermute x1, waiting for transfers between devices, shards(): far_a = lax.ppermute(own[:256], 'xh', pair)  18.3 us
    all_to_all x2, waiting for transfers between devices, swap(): lax.all_to_all(message, ('z', 'y', 'xl'), split_axis=0, concat_axis=0, ti...  18 us
    pallas_call x1, Pallas kernels, cross(): pl.pallas_call(cross_kernel, out_shape=jax.ShapeDtypeStruct((8, 4, 2, 72,...  7.09 us
    pallas_call x1, Pallas kernels, along_far(): return along(far_kernel, ins, [LINES] * 2, (out, out))(*args)  6.62 us
    pallas_call x1, Pallas kernels, along_close(): return along(close_kernel, [LINES, LINES], BOTH, shape)(*args)  5.39 us
    unnamed x6, local copies, waits for them, and re-layouts  3.36 us
  transfers between devices with their start and end apart: 7, of which 4 were waited for; matrix products, arithmetic and copies ran while one was open for 0% of the time, Pallas kernels for 10%

profile of v10, /device:TPU:4, one launch (start us, length us, event | category | flops | bytes accessed | tf_op | source)
XLA Modules:
  0.0 118.7 jit_solution(5195650701729585827)
XLA Ops:
  0.6 2.1 %shard_map.75 = f32[2304,128]{1,0:T(8,128)} custom-call(f32[24,32,384]{2,1,0:T(8,128)} %bitcast.12), custom_call_target="tpu_custom_call" | custom-call | tf_op jit(solution)/shard_map/pallas_call | solution.py:112
  2.8 0.0 copy-start
  2.8 12.9 %all-to-all-start = ((f32[64,9,4,128]{3,2,1,0:T(4,128)}), f32[64,9,4,128]{3,2,1,0:T(4,128)S(1)}, u32[]{:S(2)}, u32[]{:S(2)}) async-start(f32[64,9,4,128]{3,2,1,0:T(4,128)} %bitcast.18), calls=%async_computation | async-start | bytes 2359296 | tf_op jit(solution)/shard_map/all_to_all | solution.py:363
  15.7 0.0 copy-done
  15.7 0.9 collective-permute-start
  16.6 18.3 %collective-permute-done.far_a = f32[256,384]{1,0:T(8,128)} collective-permute-done((f32[256,384]{1,0:T(8,128)S(1)}, f32[256,384]{1,0:T(8,128)}, u32[]{:S(2)}, u32[]{:S(2)}) %collective-permute-start) | collective-permute-done | bytes 393248 | tf_op jit(solution)/shard_map/ppermute | solution.py:368
  34.9 12.4 %all-to-all-done = f32[64,9,4,128]{3,2,1,0:T(4,128)S(1)} async-done(((f32[64,9,4,128]{3,2,1,0:T(4,128)}), f32[64,9,4,128]{3,2,1,0:T(4,128)S(1)}, u32[]{:S(2)}, u32[]{:S(2)}) %all-to-all-start) | async-done | bytes 1179680 | tf_op jit(solution)/shard_map/all_to_all | solution.py:363
  47.3 0.0 copy-start.2
  47.3 1.0 copy-done.2
  48.3 7.1 %shard_map.78 = f32[8,4,2,72,128]{4,3,2,1,0:T(8,128)} custom-call(bf16[2,2,2,128,640]{4,3,2,1,0:T(8,128)(2,1)} %constant.10.clone.small_hbm, bf16[2,2,256,1280]{3,2,1,0:T(8,128)(2,1)} %constant.11.clone.large_hbm, f32[2,4,4,72,128]{4,3,2,1,0:T(8,128)} %bitcast.20), custom_call_target="tpu_custom_call" | custom-call | flops 2717908992 | bytes 12582912 | tf_op jit(solution)/shard_map/pallas_call | solution.py:264
  55.4 6.0 %all-to-all-start.1 = ((f32[64,72,128]{2,1,0:T(8,128)}), f32[64,72,128]{2,1,0:T(8,128)S(1)}, u32[]{:S(2)}, u32[]{:S(2)}) async-start(f32[64,72,128]{2,1,0:T(8,128)} %bitcast.19), calls=%async_computation.1 | async-start | bytes 4718592 | tf_op jit(solution)/shard_map/all_to_all | solution.py:363
  61.4 0.1 slice.11
  61.4 0.9 collective-permute-start.2
  62.3 0.0 collective-permute-start.1
  62.3 34.3 %collective-permute-done.2.far_b = f32[512,384]{1,0:T(8,128)} collective-permute-done((f32[512,384]{1,0:T(8,128)S(1)}, f32[512,384]{1,0:T(8,128)}, u32[]{:S(2)}, u32[]{:S(2)}) %collective-permute-start.2) | collective-permute-done | bytes 786464 | tf_op jit(solution)/shard_map/ppermute | solution.py:372
  96.6 0.0 collective-permute-start.4
  96.6 0.5 collective-permute-start.3
  97.1 0.0 collective-permute-done.1.near
  97.1 0.0 copy-start.1
  97.1 2.3 %copy-done.1 = bf16[2,4,384,768]{3,2,1,0:T(8,128)(2,1)S(1)} copy-done((bf16[2,4,384,768]{3,2,1,0:T(8,128)(2,1)S(1)}, bf16[2,4,384,768]{3,2,1,0:T(8,128)(2,1)}, u32[]{:S(2)}) %copy-start.1) | copy-done | bytes 4718616
  99.4 5.4 %shard_map.76.part = f32[768,768]{1,0:T(8,128)S(1)} custom-call(s32[1]{0:T(128)} %bitcast.core_ref, bf16[2,4,384,768]{3,2,1,0:T(8,128)(2,1)S(1)} %copy-done.1, f32[768,384]{1,0:T(8,128)S(1)} %bitcast.15, f32[768,384]{1,0:T(8,128)} %collective-permute-done.1.near), custom_call_target="tpu_custom_call" | custom-call | flops 2717908992 | bytes 12582912 | tf_op jit(solution)/shard_map/pallas_call | solution.py:345
  104.8 0.0 collective-permute-done.3.far_near_a
  104.8 0.0 collective-permute-done.4.far_near_b
  104.8 6.6 %shard_map.77 = (f32[768,384]{1,0:T(8,128)}, f32[768,384]{1,0:T(8,128)}) custom-call(s32[1]{0:T(128)} %bitcast.core_ref, bf16[2,4,384,768]{3,2,1,0:T(8,128)(2,1)S(1)} %copy-done.1, f32[768,384]{1,0:T(8,128)S(1)} %bitcast.16, f32[768,768]{1,0:T(8,128)S(1)} %shard_map.76.part, f32[256,384]{1,0:T(8,128)} %collective-permute-done.far_a, ...), custom_call_target="tpu_custom_call" | custom-call | flops 2717908992 | bytes 12582912 | tf_op jit(solution)/shard_map/pallas_call | solution.py:353
  111.5 5.7 %all-to-all-done.1 = f32[64,72,128]{2,1,0:T(8,128)S(1)} async-done(((f32[64,72,128]{2,1,0:T(8,128)}), f32[64,72,128]{2,1,0:T(8,128)S(1)}, u32[]{:S(2)}, u32[]{:S(2)}) %all-to-all-start.1) | async-done | bytes 2359328 | tf_op jit(solution)/shard_map/all_to_all | solution.py:363
  117.1 1.6 %shard_map.79 = (f32[24,32,384]{2,1,0:T(8,128)}, f32[24,32,384]{2,1,0:T(8,128)}) custom-call(f32[4608,128]{1,0:T(8,128)S(1)} %bitcast.17), custom_call_target="tpu_custom_call" | custom-call | tf_op jit(solution)/shard_map/pallas_call | solution.py:155
  (1 shorter events, 0.0 us)
Async XLA Ops:
  2.8 12.9 %copy-start = (f32[24,2,16,384]{3,2,1,0:T(8,128)S(1)}, f32[24,2,16,384]{3,2,1,0:T(8,128)}, u32[]{:S(2)}) copy-start(f32[24,2,16,384]{3,2,1,0:T(8,128)} %param.4) | copy-start | bytes 3538948
  2.8 44.5 %all-to-all-start = ((f32[64,9,4,128]{3,2,1,0:T(4,128)}), f32[64,9,4,128]{3,2,1,0:T(4,128)S(1)}, u32[]{:S(2)}, u32[]{:S(2)}) async-start(f32[64,9,4,128]{3,2,1,0:T(4,128)} %bitcast.18), calls=%async_computation | async-start | bytes 2359296 | tf_op jit(solution)/shard_map/all_to_all | solution.py:363
  15.7 19.2 %collective-permute-start = (f32[256,384]{1,0:T(8,128)S(1)}, f32[256,384]{1,0:T(8,128)}, u32[]{:S(2)}, u32[]{:S(2)}) collective-permute-start(f32[256,384]{1,0:T(8,128)S(1)} %bitcast.21), channel_id=1, source_target_pairs={{0,2},{2,0},{1,3},{3,1},{4,6},{6,4},{5,7},{7,5},{8,10},{10,8},{9,1... | collective-permute-start | bytes 1179656 | tf_op jit(solution)/shard_map/ppermute | solution.py:368
  47.3 1.0 copy-start.2
  55.4 61.7 %all-to-all-start.1 = ((f32[64,72,128]{2,1,0:T(8,128)}), f32[64,72,128]{2,1,0:T(8,128)S(1)}, u32[]{:S(2)}, u32[]{:S(2)}) async-start(f32[64,72,128]{2,1,0:T(8,128)} %bitcast.19), calls=%async_computation.1 | async-start | bytes 4718592 | tf_op jit(solution)/shard_map/all_to_all | solution.py:363
  61.4 35.1 %collective-permute-start.2 = (f32[512,384]{1,0:T(8,128)S(1)}, f32[512,384]{1,0:T(8,128)}, u32[]{:S(2)}, u32[]{:S(2)}) collective-permute-start(f32[512,384]{1,0:T(8,128)S(1)} %slice.11), channel_id=1, source_target_pairs={{0,2},{2,0},{1,3},{3,1},{4,6},{6,4},{5,7},{7,5},{8,10},{10,8},{9,1... | collective-permute-start | bytes 2359304 | tf_op jit(solution)/shard_map/ppermute | solution.py:372
  62.3 34.8 %collective-permute-start.1 = (f32[768,384]{1,0:T(8,128)S(1)}, f32[768,384]{1,0:T(8,128)}, u32[]{:S(2)}, u32[]{:S(2)}) collective-permute-start(f32[768,384]{1,0:T(8,128)S(1)} %bitcast.14), channel_id=1, source_target_pairs={{0,1},{1,0},{2,3},{3,2},{4,5},{5,4},{6,7},{7,6},{8,9},{9,8},{10,11... | collective-permute-start | bytes 3538952 | tf_op jit(solution)/shard_map/ppermute | solution.py:371
  96.6 8.3 %collective-permute-start.4 = (f32[512,384]{1,0:T(8,128)}, f32[512,384]{1,0:T(8,128)}, u32[]{:S(2)}, u32[]{:S(2)}) collective-permute-start(f32[512,384]{1,0:T(8,128)} %collective-permute-done.2.far_b), channel_id=1, source_target_pairs={{0,1},{1,0},{2,3},{3,2},{4,5},{5,4},{6,7},{7,6},{8,9},{9,8},{10,11... | collective-permute-start | bytes 2359304 | tf_op jit(solution)/shard_map/ppermute | solution.py:375
  96.6 8.3 %collective-permute-start.3 = (f32[256,384]{1,0:T(8,128)}, f32[256,384]{1,0:T(8,128)}, u32[]{:S(2)}, u32[]{:S(2)}) collective-permute-start(f32[256,384]{1,0:T(8,128)} %collective-permute-done.far_a), channel_id=1, source_target_pairs={{0,1},{1,0},{2,3},{3,2},{4,5},{5,4},{6,7},{7,6},{8,9},{9,8},{10,11... | collective-permute-start | bytes 1179656 | tf_op jit(solution)/shard_map/ppermute | solution.py:374
  97.1 2.3 %copy-start.1 = (bf16[2,4,384,768]{3,2,1,0:T(8,128)(2,1)S(1)}, bf16[2,4,384,768]{3,2,1,0:T(8,128)(2,1)}, u32[]{:S(2)}) copy-start(bf16[2,4,384,768]{3,2,1,0:T(8,128)(2,1)} %constant.12.clone.table_ref) | copy-start | bytes 14155780

commit v11 on v8

--- a/solution.py
+++ b/solution.py
@@ -72,6 +72,14 @@
 def three(left_high, left_low, right_high, right_low):
     total = jnp.dot(left_high, right_high, preferred_element_type=F32)
     total = total + jnp.dot(left_high, right_low, preferred_element_type=F32)
+    return total + jnp.dot(left_low, right_high, preferred_element_type=F32)
+
+
+def wide_three(left_high, left_low, right_high, right_low):
+    both = jnp.concatenate([right_high, right_low], axis=1)
+    width = right_high.shape[1]
+    total = jnp.dot(left_high, both, preferred_element_type=F32)
+    total = total[:, :width] + total[:, width:]
     return total + jnp.dot(left_low, right_high, preferred_element_type=F32)
 
 
@@ -219,7 +227,7 @@
     whole = whole - jnp.sum(whole, axis=0, keepdims=True) * (1.0 / QUARTER)
     for k, value in enumerate((whole, head - tail)):
         high, low = split(value)
-        got_small[k] = three(small[k, 0], small[k, 1], high, low)
+        got_small[k] = wide_three(small[k, 0], small[k, 1], high, low)
 
     high, low = split(line[1])
     near = low_lanes((12, 128))
@@ -228,7 +236,9 @@
         for d in range(2):
             lanes = slice(256 * (2 - i), 256 * (2 - i) + HALF)
             left = large_strip[0, d, :, lanes], large_strip[1, d, :, lanes]
-            got_large[HALF * d + 256 * i : HALF * d + 256 * i + 256, :] = three(*left, high, low)
+            got_large[HALF * d + 256 * i : HALF * d + 256 * i + 256, :] = wide_three(
+                *left, high, low
+            )
 
     def close(c):
         for y in range(4):

time: 119 us -> 119 us (level)
  no operation moved by 1% of the time
where the time goes in v11:
time: 119 us
  waiting for transfers between devices  69.7 us (59%)
  Pallas kernels  21.3 us (18%)
  starting transfers between devices  21.2 us (18%)
  local copies, waits for them, and re-layouts  5.72 us (5%)
    ppermute x1, waiting for transfers between devices, shards(): far_b = lax.ppermute(own[256:], 'xh', pair)  34.3 us
    ppermute x1, waiting for transfers between devices, shards(): far_a = lax.ppermute(own[:256], 'xh', pair)  19.1 us
    all_to_all x2, starting transfers between devices, swap(): lax.all_to_all(message, ('z', 'y', 'xl'), split_axis=0, concat_axis=0, ti...  18.8 us
    all_to_all x2, waiting for transfers between devices, swap(): lax.all_to_all(message, ('z', 'y', 'xl'), split_axis=0, concat_axis=0, ti...  13.7 us
    pallas_call x1, Pallas kernels, along(): pl.pallas_call(along_kernel, grid_spec=pltpu.PrefetchScalarGridSpec(num_s...  10.5 us
    pallas_call x1, Pallas kernels, cross(): pl.pallas_call(cross_kernel, out_shape=jax.ShapeDtypeStruct((8, 4, 2, 72,...  7.03 us
    unnamed x10, local copies, waits for them, and re-layouts  5.64 us
  transfers between devices with their start and end apart: 7, of which 6 were waited for; matrix products, arithmetic and copies ran while one was open for 0% of the time, Pallas kernels for 9%

profile of v11, /device:TPU:4, one launch (start us, length us, event | category | flops | bytes accessed | tf_op | source)
XLA Modules:
  0.0 118.7 jit_solution(3098810276990816695)
XLA Ops:
  0.6 2.1 %shard_map.75 = f32[2304,128]{1,0:T(8,128)} custom-call(f32[24,32,384]{2,1,0:T(8,128)} %bitcast.14), custom_call_target="tpu_custom_call" | custom-call | tf_op jit(solution)/shard_map/pallas_call | solution.py:120
  2.8 0.0 copy-start
  2.8 12.9 %all-to-all-start = ((f32[64,9,4,128]{3,2,1,0:T(4,128)}), f32[64,9,4,128]{3,2,1,0:T(4,128)S(1)}, u32[]{:S(2)}, u32[]{:S(2)}) async-start(f32[64,9,4,128]{3,2,1,0:T(4,128)} %bitcast.17), calls=%async_computation | async-start | bytes 2359296 | tf_op jit(solution)/shard_map/all_to_all | solution.py:349
  15.7 0.0 copy-done
  15.7 0.1 collective-permute-start.1
  15.8 0.9 collective-permute-start
  16.7 19.1 %collective-permute-done.far_a = f32[256,384]{1,0:T(8,128)} collective-permute-done((f32[256,384]{1,0:T(8,128)S(1)}, f32[256,384]{1,0:T(8,128)}, u32[]{:S(2)}, u32[]{:S(2)}) %collective-permute-start) | collective-permute-done | bytes 393248 | tf_op jit(solution)/shard_map/ppermute | solution.py:354
  35.8 0.0 collective-permute-done.1.near
  35.8 0.0 copy-start.1
  35.8 1.0 copy-done.1
  36.8 10.5 %all-to-all-done = f32[64,9,4,128]{3,2,1,0:T(4,128)S(1)} async-done(((f32[64,9,4,128]{3,2,1,0:T(4,128)}), f32[64,9,4,128]{3,2,1,0:T(4,128)S(1)}, u32[]{:S(2)}, u32[]{:S(2)}) %all-to-all-start) | async-done | bytes 1179680 | tf_op jit(solution)/shard_map/all_to_all | solution.py:349
  47.3 0.0 copy-start.4
  47.3 1.0 copy-done.4
  48.3 7.0 %shard_map.77 = f32[8,4,2,72,128]{4,3,2,1,0:T(8,128)} custom-call(bf16[2,2,2,128,640]{4,3,2,1,0:T(8,128)(2,1)} %constant.10.clone.small_hbm, bf16[2,2,256,1280]{3,2,1,0:T(8,128)(2,1)} %constant.11.clone.large_hbm, f32[2,4,4,72,128]{4,3,2,1,0:T(8,128)} %bitcast.19), custom_call_target="tpu_custom_call" | custom-call | flops 2717908992 | bytes 12582912 | tf_op jit(solution)/shard_map/pallas_call | solution.py:274
  55.3 6.0 %all-to-all-start.1 = ((f32[64,72,128]{2,1,0:T(8,128)}), f32[64,72,128]{2,1,0:T(8,128)S(1)}, u32[]{:S(2)}, u32[]{:S(2)}) async-start(f32[64,72,128]{2,1,0:T(8,128)} %bitcast.18), calls=%async_computation.1 | async-start | bytes 4718592 | tf_op jit(solution)/shard_map/all_to_all | solution.py:349
  61.3 0.1 slice.14
  61.3 0.9 collective-permute-start.2
  62.2 34.3 %collective-permute-done.2.far_b = f32[512,384]{1,0:T(8,128)} collective-permute-done((f32[512,384]{1,0:T(8,128)S(1)}, f32[512,384]{1,0:T(8,128)}, u32[]{:S(2)}, u32[]{:S(2)}) %collective-permute-start.2) | collective-permute-done | bytes 786464 | tf_op jit(solution)/shard_map/ppermute | solution.py:358
  96.5 0.0 collective-permute-start.4
  96.5 0.5 collective-permute-start.3
  97.0 2.1 %collective-permute-done.4.far_near_b = f32[512,384]{1,0:T(8,128)} collective-permute-done((f32[512,384]{1,0:T(8,128)}, f32[512,384]{1,0:T(8,128)}, u32[]{:S(2)}, u32[]{:S(2)}) %collective-permute-start.4) | collective-permute-done | bytes 786464 | tf_op jit(solution)/shard_map/ppermute | solution.py:361
  99.1 0.6 collective-permute-done.3.far_near_a
  99.7 0.0 copy-start.2
  99.7 1.3 %copy-done.2 = f32[768,384]{1,0:T(8,128)S(1)} copy-done((f32[768,384]{1,0:T(8,128)S(1)}, f32[768,384]{1,0:T(8,128)}, u32[]{:S(2)}) %copy-start.2) | copy-done | bytes 1179672
  101.0 0.0 copy-start.3
  101.0 2.3 %copy-done.3 = bf16[2,4,384,768]{3,2,1,0:T(8,128)(2,1)S(1)} copy-done((bf16[2,4,384,768]{3,2,1,0:T(8,128)(2,1)S(1)}, bf16[2,4,384,768]{3,2,1,0:T(8,128)(2,1)}, u32[]{:S(2)}) %copy-start.3) | copy-done | bytes 4718616
  103.3 10.5 %shard_map.76 = (f32[768,384]{1,0:T(8,128)}, f32[768,384]{1,0:T(8,128)}) custom-call(s32[1]{0:T(128)} %bitcast.core_ref, bf16[2,4,384,768]{3,2,1,0:T(8,128)(2,1)S(1)} %copy-done.3, f32[768,384]{1,0:T(8,128)S(1)} %bitcast.16, f32[768,384]{1,0:T(8,128)S(1)} %copy-done.2, f32[256,384]{1,0:T(8,128)} %collective-permute-done.far_a, ...), custom_call_target="tpu_custom_call" | custom-call | flops 5435817984 | bytes 16777216 | tf_op jit(solution)/shard_map/pallas_call | solution.py:325
  113.8 3.3 %all-to-all-done.1 = f32[64,72,128]{2,1,0:T(8,128)S(1)} async-done(((f32[64,72,128]{2,1,0:T(8,128)}), f32[64,72,128]{2,1,0:T(8,128)S(1)}, u32[]{:S(2)}, u32[]{:S(2)}) %all-to-all-start.1) | async-done | bytes 2359328 | tf_op jit(solution)/shard_map/all_to_all | solution.py:349
  117.1 1.6 %shard_map.78 = (f32[24,32,384]{2,1,0:T(8,128)}, f32[24,32,384]{2,1,0:T(8,128)}) custom-call(f32[4608,128]{1,0:T(8,128)S(1)} %bitcast.13), custom_call_target="tpu_custom_call" | custom-call | tf_op jit(solution)/shard_map/pallas_call | solution.py:163
  (1 shorter events, 0.0 us)
Async XLA Ops:
  2.8 12.9 %copy-start = (f32[24,2,16,384]{3,2,1,0:T(8,128)S(1)}, f32[24,2,16,384]{3,2,1,0:T(8,128)}, u32[]{:S(2)}) copy-start(f32[24,2,16,384]{3,2,1,0:T(8,128)} %param.4) | copy-start | bytes 3538948
  2.8 44.5 %all-to-all-start = ((f32[64,9,4,128]{3,2,1,0:T(4,128)}), f32[64,9,4,128]{3,2,1,0:T(4,128)S(1)}, u32[]{:S(2)}, u32[]{:S(2)}) async-start(f32[64,9,4,128]{3,2,1,0:T(4,128)} %bitcast.17), calls=%async_computation | async-start | bytes 2359296 | tf_op jit(solution)/shard_map/all_to_all | solution.py:349
  15.7 20.1 %collective-permute-start.1 = (f32[768,384]{1,0:T(8,128)S(1)}, f32[768,384]{1,0:T(8,128)S(1)}, u32[]{:S(2)}, u32[]{:S(2)}) collective-permute-start(f32[768,384]{1,0:T(8,128)S(1)} %bitcast.15), channel_id=1, source_target_pairs={{0,1},{1,0},{2,3},{3,2},{4,5},{5,4},{6,7},{7,6},{8,9},{9,8},{10,11... | collective-permute-start | bytes 3538952 | tf_op jit(solution)/shard_map/ppermute | solution.py:355
  15.8 20.0 %collective-permute-start = (f32[256,384]{1,0:T(8,128)S(1)}, f32[256,384]{1,0:T(8,128)}, u32[]{:S(2)}, u32[]{:S(2)}) collective-permute-start(f32[256,384]{1,0:T(8,128)S(1)} %bitcast.21), channel_id=1, source_target_pairs={{0,2},{2,0},{1,3},{3,1},{4,6},{6,4},{5,7},{7,5},{8,10},{10,8},{9,1... | collective-permute-start | bytes 1179656 | tf_op jit(solution)/shard_map/ppermute | solution.py:354
  35.8 1.0 copy-start.1
  47.3 1.0 copy-start.4
  55.3 61.7 %all-to-all-start.1 = ((f32[64,72,128]{2,1,0:T(8,128)}), f32[64,72,128]{2,1,0:T(8,128)S(1)}, u32[]{:S(2)}, u32[]{:S(2)}) async-start(f32[64,72,128]{2,1,0:T(8,128)} %bitcast.18), calls=%async_computation.1 | async-start | bytes 4718592 | tf_op jit(solution)/shard_map/all_to_all | solution.py:349
  61.3 35.2 %collective-permute-start.2 = (f32[512,384]{1,0:T(8,128)S(1)}, f32[512,384]{1,0:T(8,128)}, u32[]{:S(2)}, u32[]{:S(2)}) collective-permute-start(f32[512,384]{1,0:T(8,128)S(1)} %bitcast.20), channel_id=1, source_target_pairs={{0,2},{2,0},{1,3},{3,1},{4,6},{6,4},{5,7},{7,5},{8,10},{10,8},{9,1... | collective-permute-start | bytes 2359304 | tf_op jit(solution)/shard_map/ppermute | solution.py:358
  96.5 2.6 %collective-permute-start.4 = (f32[512,384]{1,0:T(8,128)}, f32[512,384]{1,0:T(8,128)}, u32[]{:S(2)}, u32[]{:S(2)}) collective-permute-start(f32[512,384]{1,0:T(8,128)} %collective-permute-done.2.far_b), channel_id=1, source_target_pairs={{0,1},{1,0},{2,3},{3,2},{4,5},{5,4},{6,7},{7,6},{8,9},{9,8},{10,11... | collective-permute-start | bytes 2359304 | tf_op jit(solution)/shard_map/ppermute | solution.py:361
  96.5 3.2 %collective-permute-start.3 = (f32[256,384]{1,0:T(8,128)}, f32[256,384]{1,0:T(8,128)}, u32[]{:S(2)}, u32[]{:S(2)}) collective-permute-start(f32[256,384]{1,0:T(8,128)} %collective-permute-done.far_a), channel_id=1, source_target_pairs={{0,1},{1,0},{2,3},{3,2},{4,5},{5,4},{6,7},{7,6},{8,9},{9,8},{10,11... | collective-permute-start | bytes 1179656 | tf_op jit(solution)/shard_map/ppermute | solution.py:360
  99.7 1.3 %copy-start.2 = (f32[768,384]{1,0:T(8,128)S(1)}, f32[768,384]{1,0:T(8,128)}, u32[]{:S(2)}) copy-start(f32[768,384]{1,0:T(8,128)} %copy-done.1) | copy-start | bytes 3538948
  101.0 2.3 %copy-start.3 = (bf16[2,4,384,768]{3,2,1,0:T(8,128)(2,1)S(1)}, bf16[2,4,384,768]{3,2,1,0:T(8,128)(2,1)}, u32[]{:S(2)}) copy-start(bf16[2,4,384,768]{3,2,1,0:T(8,128)(2,1)} %constant.12.clone.table_ref) | copy-start | bytes 14155780

commit v12 on v9

--- a/solution.py
+++ b/solution.py
@@ -72,6 +72,14 @@
 def three(left_high, left_low, right_high, right_low):
     total = jnp.dot(left_high, right_high, preferred_element_type=F32)
     total = total + jnp.dot(left_high, right_low, preferred_element_type=F32)
+    return total + jnp.dot(left_low, right_high, preferred_element_type=F32)
+
+
+def wide_three(left_high, left_low, right_high, right_low):
+    both = jnp.concatenate([right_high, right_low], axis=1)
+    width = right_high.shape[1]
+    total = jnp.dot(left_high, both, preferred_element_type=F32)
+    total = total[:, :width] + total[:, width:]
     return total + jnp.dot(left_low, right_high, preferred_element_type=F32)
 
 
@@ -219,7 +227,7 @@
     whole = whole - jnp.sum(whole, axis=0, keepdims=True) * (1.0 / QUARTER)
     for k, value in enumerate((whole, head - tail)):
         high, low = split(value)
-        got_small[k] = three(small[k, 0], small[k, 1], high, low)
+        got_small[k] = wide_three(small[k, 0], small[k, 1], high, low)
 
     high, low = split(line[1])
     near = low_lanes((12, 128))
@@ -228,7 +236,9 @@
         for d in range(2):
             lanes = slice(256 * (2 - i), 256 * (2 - i) + HALF)
             left = large_strip[0, d, :, lanes], large_strip[1, d, :, lanes]
-            got_large[HALF * d + 256 * i : HALF * d + 256 * i + 256, :] = three(*left, high, low)
+            got_large[HALF * d + 256 * i : HALF * d + 256 * i + 256, :] = wide_three(
+                *left, high, low
+            )
 
     def close(c):
         for y in range(4):

time: 119 us -> 119 us (level)
  no operation moved by 1% of the time
where the time goes in v12:
time: 119 us
  waiting for transfers between devices  69.2 us (58%)
  Pallas kernels  21.8 us (18%)
  starting transfers between devices  21.2 us (18%)
  local copies, waits for them, and re-layouts  5.72 us (5%)
    ppermute x1, waiting for transfers between devices, shards(): far_b = lax.ppermute(own[256:], 'xh', pair)  34.3 us
    ppermute x1, waiting for transfers between devices, shards(): far_a = lax.ppermute(own[:256], 'xh', pair)  19.1 us
    all_to_all x2, starting transfers between devices, swap(): lax.all_to_all(message, ('z', 'y', 'xl'), split_axis=0, concat_axis=0, ti...  18.8 us
    all_to_all x2, waiting for transfers between devices, swap(): lax.all_to_all(message, ('z', 'y', 'xl'), split_axis=0, concat_axis=0, ti...  15.9 us
    pallas_call x1, Pallas kernels, cross(): pl.pallas_call(cross_kernel, out_shape=jax.ShapeDtypeStruct((8, 4, 2, 72,...  7.03 us
    pallas_call x1, Pallas kernels, along_far(): return along(far_kernel, ins, [LINES] * 2, (out, out))(*args)  6.62 us
    unnamed x10, local copies, waits for them, and re-layouts  5.64 us
    pallas_call x1, Pallas kernels, along_close(): return along(close_kernel, [LINES, LINES], BOTH, shape)(*args)  4.38 us
  transfers between devices with their start and end apart: 7, of which 4 were waited for; matrix products, arithmetic and copies ran while one was open for 0% of the time, Pallas kernels for 9%

profile of v12, /device:TPU:4, one launch (start us, length us, event | category | flops | bytes accessed | tf_op | source)
XLA Modules:
  0.0 118.7 jit_solution(12587485801337324114)
XLA Ops:
  0.6 2.1 %shard_map.75 = f32[2304,128]{1,0:T(8,128)} custom-call(f32[24,32,384]{2,1,0:T(8,128)} %bitcast.13), custom_call_target="tpu_custom_call" | custom-call | tf_op jit(solution)/shard_map/pallas_call | solution.py:120
  2.8 0.0 copy-start
  2.8 12.9 %all-to-all-start = ((f32[64,9,4,128]{3,2,1,0:T(4,128)}), f32[64,9,4,128]{3,2,1,0:T(4,128)S(1)}, u32[]{:S(2)}, u32[]{:S(2)}) async-start(f32[64,9,4,128]{3,2,1,0:T(4,128)} %bitcast.18), calls=%async_computation | async-start | bytes 2359296 | tf_op jit(solution)/shard_map/all_to_all | solution.py:373
  15.7 0.0 copy-done
  15.7 0.1 collective-permute-start.1
  15.8 0.9 collective-permute-start
  16.7 19.1 %collective-permute-done.far_a = f32[256,384]{1,0:T(8,128)} collective-permute-done((f32[256,384]{1,0:T(8,128)S(1)}, f32[256,384]{1,0:T(8,128)}, u32[]{:S(2)}, u32[]{:S(2)}) %collective-permute-start) | collective-permute-done | bytes 393248 | tf_op jit(solution)/shard_map/ppermute | solution.py:378
  35.8 0.0 collective-permute-done.1.near
  35.8 0.0 copy-start.2
  35.8 1.0 copy-done.2
  36.8 10.5 %all-to-all-done = f32[64,9,4,128]{3,2,1,0:T(4,128)S(1)} async-done(((f32[64,9,4,128]{3,2,1,0:T(4,128)}), f32[64,9,4,128]{3,2,1,0:T(4,128)S(1)}, u32[]{:S(2)}, u32[]{:S(2)}) %all-to-all-start) | async-done | bytes 1179680 | tf_op jit(solution)/shard_map/all_to_all | solution.py:373
  47.3 0.0 copy-start.4
  47.3 1.0 copy-done.4
  48.3 7.0 %shard_map.78 = f32[8,4,2,72,128]{4,3,2,1,0:T(8,128)} custom-call(bf16[2,2,2,128,640]{4,3,2,1,0:T(8,128)(2,1)} %constant.10.clone.small_hbm, bf16[2,2,256,1280]{3,2,1,0:T(8,128)(2,1)} %constant.11.clone.large_hbm, f32[2,4,4,72,128]{4,3,2,1,0:T(8,128)} %bitcast.20), custom_call_target="tpu_custom_call" | custom-call | flops 2717908992 | bytes 12582912 | tf_op jit(solution)/shard_map/pallas_call | solution.py:274
  55.3 6.0 %all-to-all-start.1 = ((f32[64,72,128]{2,1,0:T(8,128)}), f32[64,72,128]{2,1,0:T(8,128)S(1)}, u32[]{:S(2)}, u32[]{:S(2)}) async-start(f32[64,72,128]{2,1,0:T(8,128)} %bitcast.19), calls=%async_computation.1 | async-start | bytes 4718592 | tf_op jit(solution)/shard_map/all_to_all | solution.py:373
  61.3 0.1 slice.14
  61.3 0.9 collective-permute-start.2
  62.2 34.3 %collective-permute-done.2.far_b = f32[512,384]{1,0:T(8,128)} collective-permute-done((f32[512,384]{1,0:T(8,128)S(1)}, f32[512,384]{1,0:T(8,128)}, u32[]{:S(2)}, u32[]{:S(2)}) %collective-permute-start.2) | collective-permute-done | bytes 786464 | tf_op jit(solution)/shard_map/ppermute | solution.py:382
  96.5 0.0 collective-permute-start.4
  96.5 0.5 collective-permute-start.3
  97.0 0.0 copy-start.1
  97.0 2.3 %copy-done.1 = bf16[2,4,384,768]{3,2,1,0:T(8,128)(2,1)S(1)} copy-done((bf16[2,4,384,768]{3,2,1,0:T(8,128)(2,1)S(1)}, bf16[2,4,384,768]{3,2,1,0:T(8,128)(2,1)}, u32[]{:S(2)}) %copy-start.1) | copy-done | bytes 4718616
  99.3 0.0 copy-start.3
  99.3 1.3 %copy-done.3 = f32[768,384]{1,0:T(8,128)S(1)} copy-done((f32[768,384]{1,0:T(8,128)S(1)}, f32[768,384]{1,0:T(8,128)}, u32[]{:S(2)}) %copy-start.3) | copy-done | bytes 1179672
  100.6 4.4 %shard_map.76.part = f32[768,768]{1,0:T(8,128)S(1)} custom-call(s32[1]{0:T(128)} %bitcast.core_ref, bf16[2,4,384,768]{3,2,1,0:T(8,128)(2,1)S(1)} %copy-done.1, f32[768,384]{1,0:T(8,128)S(1)} %bitcast.15, f32[768,384]{1,0:T(8,128)S(1)} %copy-done.3), custom_call_target="tpu_custom_call" | custom-call | flops 2717908992 | bytes 12582912 | tf_op jit(solution)/shard_map/pallas_call | solution.py:355
  105.0 0.0 collective-permute-done.4.far_near_b
  105.0 0.0 collective-permute-done.3.far_near_a
  105.0 6.6 %shard_map.77 = (f32[768,384]{1,0:T(8,128)}, f32[768,384]{1,0:T(8,128)}) custom-call(s32[1]{0:T(128)} %bitcast.core_ref, bf16[2,4,384,768]{3,2,1,0:T(8,128)(2,1)S(1)} %copy-done.1, f32[768,384]{1,0:T(8,128)S(1)} %bitcast.16, f32[768,768]{1,0:T(8,128)S(1)} %shard_map.76.part, f32[256,384]{1,0:T(8,128)} %collective-permute-done.far_a, ...), custom_call_target="tpu_custom_call" | custom-call | flops 2717908992 | bytes 12582912 | tf_op jit(solution)/shard_map/pallas_call | solution.py:363
  111.6 5.4 %all-to-all-done.1 = f32[64,72,128]{2,1,0:T(8,128)S(1)} async-done(((f32[64,72,128]{2,1,0:T(8,128)}), f32[64,72,128]{2,1,0:T(8,128)S(1)}, u32[]{:S(2)}, u32[]{:S(2)}) %all-to-all-start.1) | async-done | bytes 2359328 | tf_op jit(solution)/shard_map/all_to_all | solution.py:373
  117.1 1.6 %shard_map.79 = (f32[24,32,384]{2,1,0:T(8,128)}, f32[24,32,384]{2,1,0:T(8,128)}) custom-call(f32[4608,128]{1,0:T(8,128)S(1)} %bitcast.17), custom_call_target="tpu_custom_call" | custom-call | tf_op jit(solution)/shard_map/pallas_call | solution.py:163
  (1 shorter events, 0.0 us)
Async XLA Ops:
  2.8 12.9 %copy-start = (f32[24,2,16,384]{3,2,1,0:T(8,128)S(1)}, f32[24,2,16,384]{3,2,1,0:T(8,128)}, u32[]{:S(2)}) copy-start(f32[24,2,16,384]{3,2,1,0:T(8,128)} %param.4) | copy-start | bytes 3538948
  2.8 44.5 %all-to-all-start = ((f32[64,9,4,128]{3,2,1,0:T(4,128)}), f32[64,9,4,128]{3,2,1,0:T(4,128)S(1)}, u32[]{:S(2)}, u32[]{:S(2)}) async-start(f32[64,9,4,128]{3,2,1,0:T(4,128)} %bitcast.18), calls=%async_computation | async-start | bytes 2359296 | tf_op jit(solution)/shard_map/all_to_all | solution.py:373
  15.7 20.1 %collective-permute-start.1 = (f32[768,384]{1,0:T(8,128)S(1)}, f32[768,384]{1,0:T(8,128)S(1)}, u32[]{:S(2)}, u32[]{:S(2)}) collective-permute-start(f32[768,384]{1,0:T(8,128)S(1)} %bitcast.14), channel_id=1, source_target_pairs={{0,1},{1,0},{2,3},{3,2},{4,5},{5,4},{6,7},{7,6},{8,9},{9,8},{10,11... | collective-permute-start | bytes 3538952 | tf_op jit(solution)/shard_map/ppermute | solution.py:379
  15.8 20.0 %collective-permute-start = (f32[256,384]{1,0:T(8,128)S(1)}, f32[256,384]{1,0:T(8,128)}, u32[]{:S(2)}, u32[]{:S(2)}) collective-permute-start(f32[256,384]{1,0:T(8,128)S(1)} %bitcast.22), channel_id=1, source_target_pairs={{0,2},{2,0},{1,3},{3,1},{4,6},{6,4},{5,7},{7,5},{8,10},{10,8},{9,1... | collective-permute-start | bytes 1179656 | tf_op jit(solution)/shard_map/ppermute | solution.py:378
  35.8 1.0 copy-start.2
  47.3 1.0 copy-start.4
  55.3 61.7 %all-to-all-start.1 = ((f32[64,72,128]{2,1,0:T(8,128)}), f32[64,72,128]{2,1,0:T(8,128)S(1)}, u32[]{:S(2)}, u32[]{:S(2)}) async-start(f32[64,72,128]{2,1,0:T(8,128)} %bitcast.19), calls=%async_computation.1 | async-start | bytes 4718592 | tf_op jit(solution)/shard_map/all_to_all | solution.py:373
  61.3 35.2 %collective-permute-start.2 = (f32[512,384]{1,0:T(8,128)S(1)}, f32[512,384]{1,0:T(8,128)}, u32[]{:S(2)}, u32[]{:S(2)}) collective-permute-start(f32[512,384]{1,0:T(8,128)S(1)} %bitcast.21), channel_id=1, source_target_pairs={{0,2},{2,0},{1,3},{3,1},{4,6},{6,4},{5,7},{7,5},{8,10},{10,8},{9,1... | collective-permute-start | bytes 2359304 | tf_op jit(solution)/shard_map/ppermute | solution.py:382
  96.5 8.5 %collective-permute-start.4 = (f32[512,384]{1,0:T(8,128)}, f32[512,384]{1,0:T(8,128)}, u32[]{:S(2)}, u32[]{:S(2)}) collective-permute-start(f32[512,384]{1,0:T(8,128)} %collective-permute-done.2.far_b), channel_id=1, source_target_pairs={{0,1},{1,0},{2,3},{3,2},{4,5},{5,4},{6,7},{7,6},{8,9},{9,8},{10,11... | collective-permute-start | bytes 2359304 | tf_op jit(solution)/shard_map/ppermute | solution.py:385
  96.5 8.5 %collective-permute-start.3 = (f32[256,384]{1,0:T(8,128)}, f32[256,384]{1,0:T(8,128)}, u32[]{:S(2)}, u32[]{:S(2)}) collective-permute-start(f32[256,384]{1,0:T(8,128)} %collective-permute-done.far_a), channel_id=1, source_target_pairs={{0,1},{1,0},{2,3},{3,2},{4,5},{5,4},{6,7},{7,6},{8,9},{9,8},{10,11... | collective-permute-start | bytes 1179656 | tf_op jit(solution)/shard_map/ppermute | solution.py:384
  97.0 2.3 %copy-start.1 = (bf16[2,4,384,768]{3,2,1,0:T(8,128)(2,1)S(1)}, bf16[2,4,384,768]{3,2,1,0:T(8,128)(2,1)}, u32[]{:S(2)}) copy-start(bf16[2,4,384,768]{3,2,1,0:T(8,128)(2,1)} %constant.12.clone.table_ref) | copy-start | bytes 14155780
  99.3 1.3 %copy-start.3 = (f32[768,384]{1,0:T(8,128)S(1)}, f32[768,384]{1,0:T(8,128)}, u32[]{:S(2)}) copy-start(f32[768,384]{1,0:T(8,128)} %copy-done.2) | copy-start | bytes 3538948
